TPU v7x, 32 devices: a whole 2x2x4 slice. The times are simulated.
32 devices in a mesh: seq: 8 (over z, y), doc: 4 (over x, core).
Axes of the slice: x: 2, y: 2, z: 4, core: 2. Of those that a mesh axis runs over, the one named last changes fastest.
Arguments:
- tokens: bfloat16 [4, 1024, 4096], P('doc', 'seq'), may hold values from -6 to 6
- norm_gain: float32 [4096], replicated, may hold values from 0.5 to 9
- w_query: bfloat16 [4096, 2048], P(None, 'doc'), may hold values from -0.09375 to 0.09375
- key_weight: bfloat16 [4096, 512], P(None, 'doc'), may hold values from -0.09375 to 0.09375
- value_weight: bfloat16 [4096, 512], P(None, 'doc'), may hold values from -0.09375 to 0.09375
- vertical_blocks: int32 [4, 4, 4], replicated, may hold values from 0 to 7, as said below
- slash_offsets: int32 [4, 4, 4], replicated, may hold values from 2 to 7, as said below
Outputs:
- attended: bfloat16 [4, 1024, 2048], P('doc', 'seq')
Inputs may be any that keep to these rules, and one draw needn't show every extreme that they name: `vertical_blocks`: within one document and key-value head the 4 block indices are distinct. `slash_offsets`: within one document and key-value head the 4 offsets are distinct.
All inputs are finite; a program needn't handle non-finite values.
Results may differ from a plain program's by a relative error of at most 0.013.
The roundings to bfloat16 on the way count: a program that leaves them out, or rounds other values in their place, can miss the bound.
Values may be sent and summed in bfloat16 or wider, within the bound.
No kernel may reach another device: no remote copies, remote signals or barrier semaphores. Data moves between devices by JAX's collectives and lax.ppermute only.
A program may use at most 64 MiB of HBM per device.

v0:
```python
import functools
import math

import jax
import jax.numpy as jnp
from jax import lax
from jax.experimental import pallas as pl
from jax.experimental.pallas import tpu as pltpu
from jax.sharding import PartitionSpec as P

HEAD_WIDTH = 128
QUERY_HEADS = 16
KEY_VALUE_HEADS = 4
QUERY_GROUP = QUERY_HEADS // KEY_VALUE_HEADS
EPSILON = 1e-05
BAND = 16
MIB = 1024 * 1024
OUT_OF_REACH = 1 << 30

SMEM = pl.BlockSpec(memory_space=pltpu.SMEM)
VMEM = pl.BlockSpec(memory_space=pltpu.VMEM)
ANYWHERE = pl.BlockSpec(memory_space=pl.ANY)
HBM = pl.BlockSpec(memory_space=pltpu.HBM)


def swap(value, axis, mask):
    count = lax.axis_size(axis)
    return lax.ppermute(value, axis, [(source, source ^ mask) for source in range(count)])


def after(value, *others):
    return lax.optimization_barrier((value,) + others)[0]


def in_hbm(array):
    return pltpu.with_memory_space_constraint(array, pltpu.HBM)


def rope_table(positions, width):
    inverse = jnp.power(jnp.float32(500000.0), -jnp.arange(0, width, 2, dtype=jnp.float32) / width)
    angles = positions.astype(jnp.float32)[:, None] * inverse[None, :]
    return (jnp.cos(angles), jnp.sin(angles))


def project_kernel(pieces, early, before, *refs):
    token_refs, refs = list(refs[:pieces]), list(refs[pieces:])
    ahead = 0
    if before:
        before_ref, refs = refs[0], refs[1:]
        ahead = before_ref.shape[0]
    gain_ref, wq_ref, wk_ref, wv_ref, table_ref, q_ref, kv_ref = refs[:7]
    refs = refs[7:]
    if before:
        kv_ref[:ahead, :] = before_ref[...]
    copies = []
    if early:
        sources = (gain_ref, token_refs[0], wk_ref, wv_ref, wq_ref)
        held, refs = refs[:1] + refs[5:6] + refs[1:4], refs[4:5] + refs[6:]
        sems = refs[1]
        gain_ref, token_refs[0], wk_ref, wv_ref, wq_ref = held
        for at, (source, target) in enumerate(zip(sources, held)):
            copies.append(pltpu.make_async_copy(source, target, sems.at[at]))
            copies[-1].start()
        copies[0].wait()
    normed = refs[0]
    width = gain_ref.shape[1]
    heads = wk_ref.shape[1] // HEAD_WIDTH
    deep = min(1024, width)

    rows = token_refs[0].shape[0]
    for piece in reversed(range(pieces)):
        if piece == 0 and early:
            copies[1].wait()
        ref, first = token_refs[piece], piece * rows

        def norm_band(index, carry, ref=ref, first=first):
            at = pl.ds(pl.multiple_of(index * BAND, BAND), BAND)
            wide = ref[at, :].astype(jnp.float32)
            scale = lax.rsqrt(jnp.mean(wide * wide, axis=-1, keepdims=True) + EPSILON)
            normed[pl.ds(pl.multiple_of(first + index * BAND, BAND), BAND), :] = (
                wide * scale * gain_ref[...]
            ).astype(jnp.bfloat16)
            return carry

        lax.fori_loop(0, rows // BAND, norm_band, 0, unroll=2)

    half = HEAD_WIDTH // 2

    def rotate(value):
        turned = jnp.concatenate([value[:, half:], value[:, :half]], axis=1)
        return (
            value * table_ref[:, :HEAD_WIDTH] + turned * table_ref[:, HEAD_WIDTH:]
        ).astype(jnp.bfloat16)

    def multiply(weight_of):
        total = None
        for start in range(0, width, deep):
            part = jnp.dot(
                normed[:, start:start + deep],
                weight_of(slice(start, start + deep)),
                preferred_element_type=jnp.float32,
            )
            total = part if total is None else total + part
        return total

    if early:
        copies[2].wait()
        copies[3].wait()
    for head in range(heads):
        at = slice(head * HEAD_WIDTH, (head + 1) * HEAD_WIDTH)
        both = multiply(lambda k: jnp.concatenate([wk_ref[k, at], wv_ref[k, at]], axis=1))
        out = 2 * head * HEAD_WIDTH
        for piece in range(pieces):
            mine = both[piece * rows:(piece + 1) * rows]
            band = slice(ahead + piece * rows, ahead + (piece + 1) * rows)
            kv_ref[band, out:out + HEAD_WIDTH] = rotate(mine[:, :HEAD_WIDTH])
            kv_ref[band, out + HEAD_WIDTH:out + 2 * HEAD_WIDTH] = mine[:, HEAD_WIDTH:].astype(
                jnp.bfloat16
            )
    if early:
        copies[4].wait()
    pair = 2 * HEAD_WIDTH
    for start in range(0, wq_ref.shape[1], pair):
        both = multiply(lambda k: wq_ref[k, start:start + pair])
        for piece in range(pieces):
            band = slice(piece * rows, (piece + 1) * rows)
            for at in (0, HEAD_WIDTH):
                q_ref[band, start + at:start + at + HEAD_WIDTH] = rotate(
                    both[band, at:at + HEAD_WIDTH]
                )


def project(pieces, gain, w_query, key_weight, value_weight, table, early=False, before=None):
    width = gain.shape[1]
    q_cols, k_cols = w_query.shape[1], key_weight.shape[1]
    total = len(pieces) * pieces[0].shape[0]
    params = (gain, w_query, key_weight, value_weight)
    held = () if before is None else (before,)
    scratch = [pltpu.VMEM((total, width), jnp.bfloat16)]
    kind = [VMEM] * (len(pieces) + len(held) + len(params))
    shapes = [
        jax.ShapeDtypeStruct((total, q_cols), jnp.bfloat16),
        jax.ShapeDtypeStruct((total + sum(a.shape[0] for a in held), 2 * k_cols), jnp.bfloat16),
    ]
    if early:
        scratch.append(pltpu.VMEM(pieces[0].shape, pieces[0].dtype))
        scratch.append(pltpu.SemaphoreType.DMA((5,)))
        params = tuple(in_hbm(array) for array in params)
        shapes += [
            jax.ShapeDtypeStruct(array.shape, array.dtype)
            for array in (gain, key_weight, value_weight, w_query)
        ]
        pieces = [in_hbm(pieces[0])] + list(pieces[1:])
        kind = [HBM] + [VMEM] * (len(pieces) - 1) + [HBM] * len(params)
    return pl.pallas_call(
        functools.partial(project_kernel, len(pieces), early, before is not None),
        in_specs=kind + [VMEM],
        out_specs=[VMEM] * len(shapes),
        out_shape=shapes,
        scratch_shapes=scratch,
        compiler_params=pltpu.CompilerParams(vmem_limit_bytes=28 * MIB),
        cost_estimate=pl.CostEstimate(
            flops=2 * total * width * (q_cols + 2 * k_cols),
            bytes_accessed=2 * width * (q_cols + 2 * k_cols) + 2 * total * width,
            transcendentals=0,
        ),
        name="project",
    )(*pieces, *held, *params, table)


def ring_order(count):
    return list(range(0, count, 2)) + list(range(count - 1, 0, -2))


class Gathered:
    def __init__(self, kv):
        count = lax.axis_size("seq")
        total = kv.shape[0]
        chunk = 8 if count % 8 == 0 else 1
        self.chunks, self.latest = count // chunk, ()
        self.arrays = [lax.all_gather(kv, "seq", axis=0, tiled=True)]
        self.slots = [
            lambda index, j=j: (0, pl.multiple_of((index * chunk + j) * total, BAND))
            for j in range(chunk)
        ]

    def advance(self, *others):
        pass


class Ring:
    def __init__(self, kv):
        self.count, self.chunks, self.stage = lax.axis_size("seq"), 1, 0
        self.order = ring_order(self.count)
        self.arrays, self.slots, self.latest = [], [], ()
        self.front = {1: kv, -1: kv}
        self.hold(kv)

    @staticmethod
    def sources(at, count):
        steps = [0]
        for stage in range(1, count // 2 + 1):
            steps += [stage, -stage] if 2 * stage < count else [stage]
        return [(at - step) % count for step in steps]

    def hold(self, array):
        self.slots.append(lambda index, r=len(self.arrays): (r, 0))
        self.arrays.append(array)

    def advance(self, *others):
        if self.stage >= self.count // 2:
            return
        self.stage += 1
        fresh = []
        for way in (1, -1) if 2 * self.stage < self.count else (1,):
            value = after(self.front[way], *others) if others else self.front[way]
            pairs = [
                (source, self.order[(at + way) % self.count]) for at, source in enumerate(self.order)
            ]
            self.front[way] = lax.ppermute(value, "seq", pairs)
            fresh.append(self.front[way])
            self.hold(self.front[way])
        self.latest = tuple(fresh)


def plan_kernel(ring, lanes, heads, count, rows, info_ref, vertical_ref, slash_ref, plan_ref):
    place, me = info_ref[0], info_ref[1]
    plan_ref[0] = place

    def enter(number, block):
        for lane in range(lanes):
            doc = me ^ lane
            for head in range(heads):
                group = me * heads + head
                found = (block == place) | (block == place - 1)
                for s in range(slash_ref.shape[2]):
                    found = found | (block == place - slash_ref[doc, group, s])
                for s in range(vertical_ref.shape[2]):
                    found = found | ((block == vertical_ref[doc, group, s]) & (block < place - 1))
                at = 1 + (lane * heads + head) * count + number
                plan_ref[at] = jnp.where(found & (block >= 0), block * rows, OUT_OF_REACH)

    if ring:
        order = ring_order(count)
        lists = {order[at]: [order[r] for r in Ring.sources(at, count)] for at in range(count)}
        for number in range(count):
            block = jnp.int32(0)
            for here, blocks in lists.items():
                block = jnp.where(place == here, blocks[number], block)
            enter(number, block)
    else:

        def one(number, carry):
            enter(number, number)
            return carry

        lax.fori_loop(0, count, one, 0)


def plan(info, vertical, slash, ring, rows):
    count, lanes = lax.axis_size("seq"), lax.axis_size("doc")
    heads = vertical.shape[1] // lanes
    length = 1 + lanes * heads * count
    return pl.pallas_call(
        functools.partial(plan_kernel, ring, lanes, heads, count, rows),
        in_specs=[SMEM] * 3,
        out_specs=SMEM,
        out_shape=jax.ShapeDtypeStruct((length,), jnp.int32),
        compiler_params=pltpu.CompilerParams(vmem_limit_bytes=16 * MIB),
        name="plan",
    )(info, vertical, slash)


def attend_kernel(lanes, stride, slot_at, slots, chunks, q_count, kv_count, begin, end, plan_ref, *refs):
    q_refs, kv_refs, refs = refs[:q_count], refs[q_count:q_count + kv_count], refs[q_count + kv_count:]
    state_refs = refs[:0 if begin else 3 * len(lanes)]
    out_refs = refs[len(state_refs):]
    heads = kv_refs[0].shape[1] // (2 * HEAD_WIDTH)
    place = plan_ref[0]
    factor = HEAD_WIDTH ** (-0.5) * math.log2(math.e)

    for lane, (mask, q_at, kv_first, rows) in enumerate(lanes):
        rank = QUERY_GROUP * rows
        row_at = place * rows + lax.broadcasted_iota(jnp.int32, (1, rows), 1)
        query_at = jnp.concatenate([row_at] * QUERY_GROUP, axis=1)
        key_at = lax.broadcasted_iota(jnp.int32, (rows, rank), 0)
        for head in range(heads):
            table = 1 + (mask * heads + head) * stride + slot_at
            queries = jnp.concatenate(
                [
                    q_refs[q_at[0]][
                        q_at[1]:q_at[1] + rows,
                        (head * QUERY_GROUP + h) * HEAD_WIDTH:(head * QUERY_GROUP + h + 1) * HEAD_WIDTH,
                    ]
                    for h in range(QUERY_GROUP)
                ],
                axis=0,
            )

            def step(index, carry):
                found = [slot(index) for slot in slots]

                def column(at):
                    cols = slice(at * HEAD_WIDTH, (at + 1) * HEAD_WIDTH)
                    parts = []
                    for r, first in found:
                        if isinstance(first, int):
                            where = slice(first + kv_first, first + kv_first + rows)
                        else:
                            where = pl.ds(pl.multiple_of(first + kv_first, BAND), rows)
                        parts.append(kv_refs[r][where, cols])
                    return jnp.concatenate(parts, axis=0)

                keys, values = column(2 * head), column(2 * head + 1)
                scores = lax.dot_general(
                    keys, queries, (((1,), (1,)), ((), ())), preferred_element_type=jnp.float32
                )
                parts = []
                for j in range(len(slots)):
                    shift = plan_ref[table + index * len(slots) + j]
                    parts.append(
                        jnp.where(
                            key_at <= query_at - shift,
                            scores[j * rows:(j + 1) * rows],
                            -jnp.inf,
                        )
                    )
                scores = jnp.concatenate(parts, axis=0)
                top = jnp.max(scores, axis=0, keepdims=True)
                if carry is None:
                    fresh = safe = top
                else:
                    fresh = jnp.maximum(carry[0], top)
                    safe = jnp.where(fresh == -jnp.inf, jnp.float32(0), fresh)
                raised = jnp.exp2((scores - safe) * factor)
                total = jnp.sum(raised, axis=0, keepdims=True)
                mixed = lax.dot_general(
                    values,
                    raised.astype(jnp.bfloat16),
                    (((0,), (0,)), ((), ())),
                    preferred_element_type=jnp.float32,
                )
                if carry is not None:
                    fade = jnp.exp2((carry[0] - safe) * factor)
                    total, mixed = carry[1] * fade + total, carry[2] * fade + mixed
                return fresh, total, mixed

            carry = None
            if not begin:
                carry = tuple(ref[head] for ref in state_refs[3 * lane:3 * lane + 3])
            elif chunks > 1:
                carry = (
                    jnp.full((1, rank), -jnp.inf, jnp.float32),
                    jnp.zeros((1, rank), jnp.float32),
                    jnp.zeros((HEAD_WIDTH, rank), jnp.float32),
                )
            if chunks > 1:
                carry = lax.fori_loop(0, chunks, step, carry)
            else:
                carry = step(0, carry)
            if not end:
                for ref, value in zip(out_refs[3 * lane:3 * lane + 3], carry):
                    ref[head] = value
                continue
            result = carry[2] / carry[1]
            for h in range(QUERY_GROUP):
                cols = slice(
                    (head * QUERY_GROUP + h) * HEAD_WIDTH, (head * QUERY_GROUP + h + 1) * HEAD_WIDTH
                )
                out_refs[lane][:, cols] = result[:, h * rows:(h + 1) * rows].T.astype(jnp.bfloat16)


def attend(table, lanes, queries, spread, span=None, states=None, end=True):
    first, last = span or (0, len(spread.slots))
    q_cols = queries[0].shape[1]
    rows = lanes[0][3]
    arrays, slots = spread.arrays, spread.slots[first:last]
    if span:
        arrays, slots = arrays[first:last], spread.slots[:last - first]
    held = [array for state in states for array in state] if states else []
    if end:
        shapes = [jax.ShapeDtypeStruct((rows, q_cols), jnp.bfloat16)] * len(lanes)
    else:
        heads = q_cols // (QUERY_GROUP * HEAD_WIDTH)
        shapes = [
            jax.ShapeDtypeStruct((heads, deep, QUERY_GROUP * rows), jnp.float32)
            for deep in (1, 1, HEAD_WIDTH)
        ] * len(lanes)
    kernel = functools.partial(
        attend_kernel,
        lanes,
        lax.axis_size("seq"),
        first,
        slots,
        spread.chunks,
        len(queries),
        len(arrays),
        not states,
        end,
    )
    return pl.pallas_call(
        kernel,
        in_specs=[SMEM] + [VMEM] * (len(queries) + len(arrays) + len(held)),
        out_specs=[VMEM] * len(shapes),
        out_shape=shapes,
        compiler_params=pltpu.CompilerParams(vmem_limit_bytes=28 * MIB),
        cost_estimate=pl.CostEstimate(
            flops=4 * len(lanes) * rows * q_cols * len(slots) * spread.chunks * rows,
            bytes_accessed=2 * sum(a.size for a in arrays) + 4 * len(lanes) * rows * q_cols,
            transcendentals=len(lanes) * rows * len(slots) * spread.chunks * rows * QUERY_GROUP,
        ),
        name="attend",
    )(table, *queries, *arrays, *held)


def deliver_kernel(masks, info_ref, *refs):
    pieces, (out_ref, sems) = refs[:len(masks)], refs[-2:]
    cols = pieces[0].shape[1]
    copies = []
    for at, (mask, piece) in enumerate(zip(masks, pieces)):
        where = pl.ds(pl.multiple_of((info_ref[1] ^ mask) * cols, cols), cols)
        copies.append(pltpu.make_async_copy(piece, out_ref.at[0, :, where], sems.at[at]))
        copies[-1].start()
    for copy in copies:
        copy.wait()


def deliver(info, masks, pieces, count, before=None):
    rows, cols = pieces[0].shape
    begun = () if before is None else (before,)
    return pl.pallas_call(
        functools.partial(deliver_kernel, masks),
        in_specs=[SMEM] + [VMEM] * len(pieces) + [HBM] * len(begun),
        out_specs=HBM,
        out_shape=jax.ShapeDtypeStruct((1, rows, count * cols), jnp.bfloat16),
        input_output_aliases={1 + len(pieces): 0} if begun else {},
        scratch_shapes=[pltpu.SemaphoreType.DMA((len(pieces),))],
        compiler_params=pltpu.CompilerParams(vmem_limit_bytes=16 * MIB),
        name="deliver",
    )(info, *pieces, *begun)


def local(tokens, norm_gain, w_query, key_weight, value_weight, vertical_blocks, slash_offsets):
    _, rows, width = tokens.shape
    assert lax.axis_size("doc") == 4
    place = lax.axis_index("seq")
    doc_place = lax.axis_index("doc")
    info = jnp.stack([place, doc_place]).astype(jnp.int32)
    cosine, sine = rope_table(place * rows + jnp.arange(rows, dtype=jnp.int32), HEAD_WIDTH)
    table = jnp.concatenate([cosine, cosine, -sine, sine], axis=1)
    own = tokens[0]
    gain = norm_gain.reshape(1, width)
    long = lax.axis_size("seq") > 8 or lax.axis_size("seq") % 2 == 1
    ring = Gathered if long else Ring
    table_of = plan(info, vertical_blocks, slash_offsets, not long, rows)

    twin = swap(own, "doc", 1)
    across = swap(own, "doc", 2)
    q_near, kv_near, gain_in, wk_in, wv_in, wq_in = project(
        [own, twin], gain, w_query, key_weight, value_weight, table, early=True
    )
    params = (gain_in, wq_in, wk_in, wv_in, table)
    near = ring(kv_near)
    near.advance()
    near.advance(table_of)
    near.advance()

    across = after(across, *near.latest)
    near.advance()
    crossed = swap(across, "doc", 1)
    q_across, kv_across = project([across], *params)
    q_crossed, kv_far = project([crossed], *params, before=kv_across)
    far = ring(kv_far)
    far.advance()
    mixed_own, mixed_twin = attend(
        table_of,
        [(0, (0, 0), 0, rows), (1, (0, rows), rows, rows)],
        [after(q_near, kv_far)],
        near,
    )
    out_twin = swap(mixed_twin, "doc", 1)
    far.advance(mixed_twin)
    far.advance()
    remote = [(2, (0, 0), 0, rows), (3, (1, 0), rows, rows)]
    queries = [after(q_across, out_twin), q_crossed]
    home = []
    if long:
        for at, mixed in enumerate(attend(table_of, remote, queries, far)):
            home.append(swap(mixed, "doc", 2 + at))
    else:
        far.advance()
        last = len(far.slots) - 1
        states = attend(table_of, remote, queries, far, span=(0, last), end=False)
        for at, lane in enumerate(remote):
            state = states[3 * at:3 * at + 3]
            (mixed,) = attend(
                table_of, [lane], queries, far, span=(last, last + 1), states=[state]
            )
            home.append(swap(mixed, "doc", 2 + at))
    count = lax.axis_size("doc")
    result = deliver(info, (0, 1), [mixed_own, out_twin], count)
    return deliver(info, (2, 3), home, count, before=result)


def solution(mesh):
    return jax.shard_map(
        local,
        mesh=mesh,
        in_specs=(
            P("doc", "seq", None),
            P(),
            P(None, "doc"),
            P(None, "doc"),
            P(None, "doc"),
            P(),
            P(),
        ),
        out_specs=P("doc", "seq", None),
        check_vma=False,
    )
```

profile of v0, /device:TPU:0, one launch (start us, length us, event | category | flops | bytes accessed | tf_op | source)
XLA Modules:
  0.0 69.4 jit_solution(12967765715784680255)
XLA Ops:
  0.5 2.5 %collective-permute-start = (bf16[128,4096]{1,0:T(8,128)(2,1)}, bf16[128,4096]{1,0:T(8,128)(2,1)S(1)}, u32[]{:S(2)}, u32[]{:S(2)}) collective-permute-start(bf16[128,4096]{1,0:T(8,128)(2,1)} %bitcast.5), channel_id=1, source_target_pairs={{0,2},{1,3},{2,0},{3,1},{4,6},{5,7},{6,4},{7,5},{8,10},{9,11},{10,... | collective-permute-start | bytes 3145736 | tf_op jit(solution)/shard_map/ppermute | solution.py:28
  3.4 1.0 %copy-done.2 = bf16[128,4096]{1,0:T(8,128)(2,1)} copy-done((bf16[128,4096]{1,0:T(8,128)(2,1)}, bf16[128,4096]{1,0:T(8,128)(2,1)S(1)}, u32[]{:S(2)}) %copy-start.2) | copy-done | bytes 1048600
  4.4 1.2 %copy-done.3 = bf16[128,4096]{1,0:T(8,128)(2,1)S(1)} copy-done((bf16[128,4096]{1,0:T(8,128)(2,1)S(1)}, bf16[128,4096]{1,0:T(8,128)(2,1)}, u32[]{:S(2)}) %copy-start.3) | copy-done | bytes 1048600
  5.6 4.6 %project.3 = (bf16[256,512]{1,0:T(8,128)(2,1)S(1)}, bf16[256,256]{1,0:T(8,128)(2,1)S(1)}, f32[1,4096]{1,0:T(1,128)S(1)}, bf16[4096,128]{1,0:T(8,128)(2,1)S(1)}, ...) custom-call(bf16[128,4096]{1,0:T(8,128)(2,1)} %bitcast.6, bf16[128,4096]{1,0:T(8,128)(2,1)S(1)} %copy-done.3, ...), custom_call_target="tpu_custom_call" | custom-call | flops 1610612736 | bytes 8388608 | tf_op jit(solution)/shard_map/project/pallas_call | solution.py:155
  10.3 1.9 %copy-done = bf16[4096,512]{1,0:T(8,128)(2,1)} copy-done((bf16[4096,512]{1,0:T(8,128)(2,1)}, bf16[4096,512]{1,0:T(8,128)(2,1)S(1)}, u32[]{:S(2)}) %copy-start) | copy-done | bytes 4194328
  12.9 2.5 %collective-permute-start.2 = (bf16[256,256]{1,0:T(8,128)(2,1)S(1)}, bf16[256,256]{1,0:T(8,128)(2,1)}, u32[]{:S(2)}, u32[]{:S(2)}) collective-permute-start(bf16[256,256]{1,0:T(8,128)(2,1)S(1)} %get-tuple-element.30.refs_1_), channel_id=1, source_target_pairs={{0,8},{8,16},{16,24},{24,28},{28,20},{20,12},{12,4},{4,0},{1,9},{9... | collective-permute-start | bytes 393224 | tf_op jit(solution)/shard_map/ppermute | solution.py:220
  15.5 1.8 %plan.1.plan_ref = s32[33]{0:T(128)S(1)} custom-call(s32[2]{0:T(128)S(1)} %pad_add_fusion.info_ref, s32[4,4,4]{2,1,0:T(4,128)S(1)} %copy-done.4, s32[4,4,4]{2,1,0:T(4,128)S(1)} %copy-done.5), custom_call_target="tpu_custom_call" | custom-call | tf_op jit(solution)/shard_map/plan/pallas_call | solution.py:264
  17.3 1.9 %collective-permute-done.2.refs_2_ = bf16[256,256]{1,0:T(8,128)(2,1)} collective-permute-done((bf16[256,256]{1,0:T(8,128)(2,1)S(1)}, bf16[256,256]{1,0:T(8,128)(2,1)}, u32[]{:S(2)}, u32[]{:S(2)}) %collective-permute-start.2) | collective-permute-done | bytes 131104 | tf_op jit(solution)/shard_map/ppermute | solution.py:220
  19.2 1.8 %collective-permute-start.3 = (bf16[256,256]{1,0:T(8,128)(2,1)}, bf16[256,256]{1,0:T(8,128)(2,1)S(1)}, u32[]{:S(2)}, u32[]{:S(2)}) collective-permute-start(bf16[256,256]{1,0:T(8,128)(2,1)} %collective-permute-done.2.refs_2_), channel_id=1, source_target_pairs={{0,8},{8,16},{16,24},{24,28},{28,20},{20,12},{12,4},{4,0},{1,9},{9... | collective-permute-start | bytes 393224 | tf_op jit(solution)/shard_map/ppermute | solution.py:220
  21.3 3.2 %collective-permute-done.3.refs_4_ = bf16[256,256]{1,0:T(8,128)(2,1)S(1)} collective-permute-done((bf16[256,256]{1,0:T(8,128)(2,1)}, bf16[256,256]{1,0:T(8,128)(2,1)S(1)}, u32[]{:S(2)}, u32[]{:S(2)}) %collective-permute-start.3) | collective-permute-done | bytes 131104 | tf_op jit(solution)/shard_map/ppermute | solution.py:220
  24.5 1.7 %collective-permute-start.4 = (bf16[256,256]{1,0:T(8,128)(2,1)S(1)}, bf16[256,256]{1,0:T(8,128)(2,1)S(1)}, u32[]{:S(2)}, u32[]{:S(2)}) collective-permute-start(bf16[256,256]{1,0:T(8,128)(2,1)S(1)} %collective-permute-done.3.refs_4_), channel_id=1, source_target_pairs={{0,8},{8,16},{16,24},{24,28},{28,20},{20,12},{12,4},{4,0},{1,9},{9... | collective-permute-start | bytes 393224 | tf_op jit(solution)/shard_map/ppermute | solution.py:220
  27.0 2.4 %collective-permute-done.4.refs_6_ = bf16[256,256]{1,0:T(8,128)(2,1)S(1)} collective-permute-done((bf16[256,256]{1,0:T(8,128)(2,1)S(1)}, bf16[256,256]{1,0:T(8,128)(2,1)S(1)}, u32[]{:S(2)}, u32[]{:S(2)}) %collective-permute-start.4) | collective-permute-done | bytes 131104 | tf_op jit(solution)/shard_map/ppermute | solution.py:220
  29.4 1.7 %collective-permute-done.7.refs_7_ = bf16[256,256]{1,0:T(8,128)(2,1)S(1)} collective-permute-done((bf16[256,256]{1,0:T(8,128)(2,1)S(1)}, bf16[256,256]{1,0:T(8,128)(2,1)S(1)}, u32[]{:S(2)}, u32[]{:S(2)}) %collective-permute-start.7) | collective-permute-done | bytes 131104 | tf_op jit(solution)/shard_map/ppermute | solution.py:220
  31.2 1.6 %collective-permute-start.9 = (bf16[256,256]{1,0:T(8,128)(2,1)S(1)}, bf16[256,256]{1,0:T(8,128)(2,1)S(1)}, u32[]{:S(2)}, u32[]{:S(2)}) collective-permute-start(bf16[256,256]{1,0:T(8,128)(2,1)S(1)} %collective-permute-done.4.refs_6_), channel_id=1, source_target_pairs={{0,8},{8,16},{16,24},{24,28},{28,20},{20,12},{12,4},{4,0},{1,9},{9... | collective-permute-start | bytes 393224 | tf_op jit(solution)/shard_map/ppermute | solution.py:220
  32.8 2.2 %copy-done.1 = bf16[4096,512]{1,0:T(8,128)(2,1)S(1)} copy-done((bf16[4096,512]{1,0:T(8,128)(2,1)S(1)}, bf16[4096,512]{1,0:T(8,128)(2,1)}, u32[]{:S(2)}) %copy-start.1) | copy-done | bytes 4194328
  34.9 1.8 %project.4 = (bf16[128,512]{1,0:T(8,128)(2,1)S(1)}, bf16[128,256]{1,0:T(8,128)(2,1)S(1)}) custom-call(bf16[128,4096]{1,0:T(8,128)(2,1)S(1)} %collective-permute-done.refs_0_, f32[1,4096]{1,0:T(1,128)S(1)} %get-tuple-element.34.refs_1_.refs_2_, bf16[4096,512]{1,0:T(8,128)(2,1)S(1)} %copy-done.1, bf16[4096,128]{1,0:T(8,128)(2,1)S(1)} %get-tuple-element.36.refs_3_.refs_4_, ...), custom_call_target="tpu_custom_call" | custom-call | flops 805306368 | bytes 7340032 | tf_op jit(solution)/shard_map/project/pallas_call | solution.py:155
  36.8 1.8 %project.5 = (bf16[128,512]{1,0:T(8,128)(2,1)S(1)}, bf16[256,256]{1,0:T(8,128)(2,1)S(1)}) custom-call(bf16[128,4096]{1,0:T(8,128)(2,1)S(1)} %collective-permute-done.8.refs_0_, bf16[128,256]{1,0:T(8,128)(2,1)S(1)} %get-tuple-element.40.refs_1_, f32[1,4096]{1,0:T(1,128)S(1)} %get-tuple-element.34.refs_1_.refs_2_, bf16[4096,512]{1,0:T(8,128)(2,1)S(1)} %copy-done.1, ...), custom_call_target="tpu_custom_call" | custom-call | flops 805306368 | bytes 7340032 | tf_op jit(solution)/shard_map/project/pallas_call | solution.py:155
  38.6 1.6 %collective-permute-start.11 = (bf16[256,256]{1,0:T(8,128)(2,1)S(1)}, bf16[256,256]{1,0:T(8,128)(2,1)S(1)}, u32[]{:S(2)}, u32[]{:S(2)}) collective-permute-start(bf16[256,256]{1,0:T(8,128)(2,1)S(1)} %get-tuple-element.41.refs_2_), channel_id=1, source_target_pairs={{0,8},{8,16},{16,24},{24,28},{28,20},{20,12},{12,4},{4,0},{1,9},{9... | collective-permute-start | bytes 393224 | tf_op jit(solution)/shard_map/ppermute | solution.py:220
  40.7 2.9 %attend.4 = (bf16[128,512]{1,0:T(8,128)(2,1)S(1)}, bf16[128,512]{1,0:T(8,128)(2,1)S(1)}) custom-call(s32[33]{0:T(128)S(1)} %plan.1.plan_ref, bf16[256,512]{1,0:T(8,128)(2,1)S(1)} %copy-done.7, bf16[256,256]{1,0:T(8,128)(2,1)S(1)} %get-tuple-element.30.refs_1_, bf16[256,256]{1,0:T(8,128)(2,1)} %collective-permute-done.2.refs_2_, ...), custom_call_target="tpu_custom_call" | custom-call | flops 536870912 | bytes 1572864 | tf_op jit(solution)/shard_map/attend/pallas_call | solution.py:401
  44.3 1.6 %collective-permute-start.12 = (bf16[256,256]{1,0:T(8,128)(2,1)S(1)}, bf16[256,256]{1,0:T(8,128)(2,1)S(1)}, u32[]{:S(2)}, u32[]{:S(2)}) collective-permute-start(bf16[256,256]{1,0:T(8,128)(2,1)S(1)} %collective-permute-done.11.refs_3_), channel_id=1, source_target_pairs={{0,8},{8,16},{16,24},{24,28},{28,20},{20,12},{12,4},{4,0},{1,9},{9... | collective-permute-start | bytes 393224 | tf_op jit(solution)/shard_map/ppermute | solution.py:220
  46.3 2.9 %collective-permute-done.12.refs_5_ = bf16[256,256]{1,0:T(8,128)(2,1)S(1)} collective-permute-done((bf16[256,256]{1,0:T(8,128)(2,1)S(1)}, bf16[256,256]{1,0:T(8,128)(2,1)S(1)}, u32[]{:S(2)}, u32[]{:S(2)}) %collective-permute-start.12) | collective-permute-done | bytes 131104 | tf_op jit(solution)/shard_map/ppermute | solution.py:220
  49.2 1.6 %collective-permute-start.13 = (bf16[256,256]{1,0:T(8,128)(2,1)S(1)}, bf16[256,256]{1,0:T(8,128)(2,1)S(1)}, u32[]{:S(2)}, u32[]{:S(2)}) collective-permute-start(bf16[256,256]{1,0:T(8,128)(2,1)S(1)} %collective-permute-done.12.refs_5_), channel_id=1, source_target_pairs={{0,8},{8,16},{16,24},{24,28},{28,20},{20,12},{12,4},{4,0},{1,9},{9... | collective-permute-start | bytes 393224 | tf_op jit(solution)/shard_map/ppermute | solution.py:220
  51.3 3.0 %collective-permute-done.13.refs_7_ = bf16[256,256]{1,0:T(8,128)(2,1)S(1)} collective-permute-done((bf16[256,256]{1,0:T(8,128)(2,1)S(1)}, bf16[256,256]{1,0:T(8,128)(2,1)S(1)}, u32[]{:S(2)}, u32[]{:S(2)}) %collective-permute-start.13) | collective-permute-done | bytes 131104 | tf_op jit(solution)/shard_map/ppermute | solution.py:220
  54.3 1.6 %collective-permute-start.14 = (bf16[256,256]{1,0:T(8,128)(2,1)S(1)}, bf16[256,256]{1,0:T(8,128)(2,1)S(1)}, u32[]{:S(2)}, u32[]{:S(2)}) collective-permute-start(bf16[256,256]{1,0:T(8,128)(2,1)S(1)} %collective-permute-done.13.refs_7_), channel_id=1, source_target_pairs={{0,8},{8,16},{16,24},{24,28},{28,20},{20,12},{12,4},{4,0},{1,9},{9... | collective-permute-start | bytes 393224 | tf_op jit(solution)/shard_map/ppermute | solution.py:220
  56.7 2.3 %attend.5 = (f32[1,1,512]{2,1,0:T(1,128)S(1)}, f32[1,1,512]{2,1,0:T(1,128)S(1)}, f32[1,128,512]{2,1,0:T(8,128)S(1)}, f32[1,1,512]{2,1,0:T(1,128)S(1)}, f32[1,1,5...) custom-call(s32[33]{0:T(128)S(1)} %plan.1.plan_ref, bf16[128,512]{1,0:T(8,128)(2,1)S(1)} %get-tuple-element.44.refs_0_, ...), custom_call_target="tpu_custom_call" | custom-call | flops 469762048 | bytes 1441792 | tf_op jit(solution)/shard_map/attend/pallas_call | solution.py:401
  59.2 1.0 %attend.6 = bf16[128,512]{1,0:T(8,128)(2,1)S(1)} custom-call(s32[33]{0:T(128)S(1)} %plan.1.plan_ref, bf16[128,512]{1,0:T(8,128)(2,1)S(1)} %get-tuple-element.44.refs_0_, bf16[128,512]{1,0:T(8,128)(2,1)S(1)} %get-tuple-element.45.refs_1_, bf16[256,256]{1,0:T(8,128)(2,1)S(1)} %collective-permute-done.14.refs_2_, f32[1,1,512]{2,1,0:T(1,128)S(1)} %get-tuple-element.48.refs_3_, ...), custom_call_target="tpu_custom_call" | custom-call | flops 33554432 | bytes 393216 | tf_op jit(solution)/shard_map/attend/pallas_call | solution.py:401
  60.3 1.6 %collective-permute-start.18 = (bf16[128,512]{1,0:T(8,128)(2,1)S(1)}, bf16[128,512]{1,0:T(8,128)(2,1)S(1)}, u32[]{:S(2)}, u32[]{:S(2)}) collective-permute-start(bf16[128,512]{1,0:T(8,128)(2,1)S(1)} %attend.6), channel_id=1, source_target_pairs={{0,2},{1,3},{2,0},{3,1},{4,6},{5,7},{6,4},{7,5},{8,10},{9,11},{10,... | collective-permute-start | bytes 393224 | tf_op jit(solution)/shard_map/ppermute | solution.py:28
  61.8 1.0 %attend.7 = bf16[128,512]{1,0:T(8,128)(2,1)S(1)} custom-call(s32[33]{0:T(128)S(1)} %plan.1.plan_ref, bf16[128,512]{1,0:T(8,128)(2,1)S(1)} %get-tuple-element.44.refs_0_, bf16[128,512]{1,0:T(8,128)(2,1)S(1)} %get-tuple-element.45.refs_1_, bf16[256,256]{1,0:T(8,128)(2,1)S(1)} %collective-permute-done.14.refs_2_, f32[1,1,512]{2,1,0:T(1,128)S(1)} %get-tuple-element.51.refs_3_, ...), custom_call_target="tpu_custom_call" | custom-call | flops 33554432 | bytes 393216 | tf_op jit(solution)/shard_map/attend/pallas_call | solution.py:401
  62.9 1.3 %deliver.2.refs_2_ = bf16[1,128,2048]{2,1,0:T(8,128)(2,1)} custom-call(s32[2]{0:T(128)S(1)} %pad_add_fusion.info_ref, bf16[128,512]{1,0:T(8,128)(2,1)S(1)} %get-tuple-element.54.refs_0_, bf16[128,512]{1,0:T(8,128)(2,1)S(1)} %collective-permute-done.10.refs_1_), custom_call_target="tpu_custom_call" | custom-call | tf_op jit(solution)/shard_map/deliver/pallas_call | solution.py:431
  64.2 1.1 %collective-permute-done.18.refs_0_ = bf16[128,512]{1,0:T(8,128)(2,1)S(1)} collective-permute-done((bf16[128,512]{1,0:T(8,128)(2,1)S(1)}, bf16[128,512]{1,0:T(8,128)(2,1)S(1)}, u32[]{:S(2)}, u32[]{:S(2)}) %collective-permute-start.18) | collective-permute-done | bytes 131104 | tf_op jit(solution)/shard_map/ppermute | solution.py:28
  65.3 2.8 %collective-permute-done.19.refs_1_ = bf16[128,512]{1,0:T(8,128)(2,1)S(1)} collective-permute-done((bf16[128,512]{1,0:T(8,128)(2,1)S(1)}, bf16[128,512]{1,0:T(8,128)(2,1)S(1)}, u32[]{:S(2)}, u32[]{:S(2)}) %collective-permute-start.19) | collective-permute-done | bytes 131104 | tf_op jit(solution)/shard_map/ppermute | solution.py:28
  68.1 1.3 %deliver.3 = bf16[1,128,2048]{2,1,0:T(8,128)(2,1)} custom-call(s32[2]{0:T(128)S(1)} %pad_add_fusion.info_ref, bf16[128,512]{1,0:T(8,128)(2,1)S(1)} %collective-permute-done.18.refs_0_, bf16[128,512]{1,0:T(8,128)(2,1)S(1)} %collective-permute-done.19.refs_1_, bf16[1,128,2048]{2,1,0:T(8,128)(2,1)} %deliver.2.refs_2_), custom_call_target="tpu_custom_call", output_to_operand_aliasing={{}: (3, {})} | custom-call | tf_op jit(solution)/shard_map/deliver/pallas_call | solution.py:431
  (39 shorter events, 5.9 us)
Async XLA Ops:
  0.0 3.4 %collective-permute-start.1 = (bf16[128,4096]{1,0:T(8,128)(2,1)}, bf16[128,4096]{1,0:T(8,128)(2,1)S(1)}, u32[]{:S(2)}, u32[]{:S(2)}) collective-permute-start(bf16[128,4096]{1,0:T(8,128)(2,1)} %bitcast.4), channel_id=1, source_target_pairs={{0,1},{1,0},{2,3},{3,2},{4,5},{5,4},{6,7},{7,6},{8,9},{9,8},{10,11... | collective-permute-start | bytes 3145736 | tf_op jit(solution)/shard_map/ppermute | solution.py:28
  0.5 26.5 %collective-permute-start = (bf16[128,4096]{1,0:T(8,128)(2,1)}, bf16[128,4096]{1,0:T(8,128)(2,1)S(1)}, u32[]{:S(2)}, u32[]{:S(2)}) collective-permute-start(bf16[128,4096]{1,0:T(8,128)(2,1)} %bitcast.5), channel_id=1, source_target_pairs={{0,2},{1,3},{2,0},{3,1},{4,6},{5,7},{6,4},{7,5},{8,10},{9,11},{10,... | collective-permute-start | bytes 3145736 | tf_op jit(solution)/shard_map/ppermute | solution.py:28
  3.4 1.0 %copy-start.2 = (bf16[128,4096]{1,0:T(8,128)(2,1)}, bf16[128,4096]{1,0:T(8,128)(2,1)S(1)}, u32[]{:S(2)}) copy-start(bf16[128,4096]{1,0:T(8,128)(2,1)S(1)} %collective-permute-done.1.refs_1_) | copy-start | bytes 3145732
  4.4 1.2 %copy-start.3 = (bf16[128,4096]{1,0:T(8,128)(2,1)S(1)}, bf16[128,4096]{1,0:T(8,128)(2,1)}, u32[]{:S(2)}) copy-start(bf16[128,4096]{1,0:T(8,128)(2,1)} %copy-done.2) | copy-start | bytes 3145732
  5.6 9.8 %copy-start.4 = (s32[4,4,4]{2,1,0:T(4,128)S(1)}, s32[4,4,4]{2,1,0:T(4,128)}, u32[]{:S(2)}) copy-start(s32[4,4,4]{2,1,0:T(4,128)} %vertical_ref.1) | copy-start | bytes 772
  5.6 9.8 %copy-start.5 = (s32[4,4,4]{2,1,0:T(4,128)S(1)}, s32[4,4,4]{2,1,0:T(4,128)}, u32[]{:S(2)}) copy-start(s32[4,4,4]{2,1,0:T(4,128)} %slash_ref.1) | copy-start | bytes 772
  10.2 2.0 %copy-start = (bf16[4096,512]{1,0:T(8,128)(2,1)}, bf16[4096,512]{1,0:T(8,128)(2,1)S(1)}, u32[]{:S(2)}) copy-start(bf16[4096,512]{1,0:T(8,128)(2,1)S(1)} %get-tuple-element.35.refs_2_.refs_3_) | copy-start | bytes 12582916
  12.2 0.7 %copy-start.6 = (bf16[256,512]{1,0:T(8,128)(2,1)}, bf16[256,512]{1,0:T(8,128)(2,1)S(1)}, u32[]{:S(2)}) copy-start(bf16[256,512]{1,0:T(8,128)(2,1)S(1)} %get-tuple-element.42.refs_0_) | copy-start | bytes 786436
  12.9 6.3 %collective-permute-start.2 = (bf16[256,256]{1,0:T(8,128)(2,1)S(1)}, bf16[256,256]{1,0:T(8,128)(2,1)}, u32[]{:S(2)}, u32[]{:S(2)}) collective-permute-start(bf16[256,256]{1,0:T(8,128)(2,1)S(1)} %get-tuple-element.30.refs_1_), channel_id=1, source_target_pairs={{0,8},{8,16},{16,24},{24,28},{28,20},{20,12},{12,4},{4,0},{1,9},{9... | collective-permute-start | bytes 393224 | tf_op jit(solution)/shard_map/ppermute | solution.py:220
  15.4 5.6 %collective-permute-start.5 = (bf16[256,256]{1,0:T(8,128)(2,1)S(1)}, bf16[256,256]{1,0:T(8,128)(2,1)}, u32[]{:S(2)}, u32[]{:S(2)}) collective-permute-start(bf16[256,256]{1,0:T(8,128)(2,1)S(1)} %get-tuple-element.30.refs_1_), channel_id=1, source_target_pairs={{0,4},{8,0},{16,8},{24,16},{28,24},{20,28},{12,20},{4,12},{1,5},{9... | collective-permute-start | bytes 393224 | tf_op jit(solution)/shard_map/ppermute | solution.py:220
  19.2 5.2 %collective-permute-start.3 = (bf16[256,256]{1,0:T(8,128)(2,1)}, bf16[256,256]{1,0:T(8,128)(2,1)S(1)}, u32[]{:S(2)}, u32[]{:S(2)}) collective-permute-start(bf16[256,256]{1,0:T(8,128)(2,1)} %collective-permute-done.2.refs_2_), channel_id=1, source_target_pairs={{0,8},{8,16},{16,24},{24,28},{28,20},{20,12},{12,4},{4,0},{1,9},{9... | collective-permute-start | bytes 393224 | tf_op jit(solution)/shard_map/ppermute | solution.py:220
  21.0 5.2 %collective-permute-start.6 = (bf16[256,256]{1,0:T(8,128)(2,1)}, bf16[256,256]{1,0:T(8,128)(2,1)S(1)}, u32[]{:S(2)}, u32[]{:S(2)}) collective-permute-start(bf16[256,256]{1,0:T(8,128)(2,1)} %collective-permute-done.5.refs_3_), channel_id=1, source_target_pairs={{0,4},{8,0},{16,8},{24,16},{28,24},{20,28},{12,20},{4,12},{1,5},{9... | collective-permute-start | bytes 393224 | tf_op jit(solution)/shard_map/ppermute | solution.py:220
  24.5 5.0 %collective-permute-start.4 = (bf16[256,256]{1,0:T(8,128)(2,1)S(1)}, bf16[256,256]{1,0:T(8,128)(2,1)S(1)}, u32[]{:S(2)}, u32[]{:S(2)}) collective-permute-start(bf16[256,256]{1,0:T(8,128)(2,1)S(1)} %collective-permute-done.3.refs_4_), channel_id=1, source_target_pairs={{0,8},{8,16},{16,24},{24,28},{28,20},{20,12},{12,4},{4,0},{1,9},{9... | collective-permute-start | bytes 393224 | tf_op jit(solution)/shard_map/ppermute | solution.py:220
  26.2 5.0 %collective-permute-start.7 = (bf16[256,256]{1,0:T(8,128)(2,1)S(1)}, bf16[256,256]{1,0:T(8,128)(2,1)S(1)}, u32[]{:S(2)}, u32[]{:S(2)}) collective-permute-start(bf16[256,256]{1,0:T(8,128)(2,1)S(1)} %collective-permute-done.6.refs_5_), channel_id=1, source_target_pairs={{0,4},{8,0},{16,8},{24,16},{28,24},{20,28},{12,20},{4,12},{1,5},{9... | collective-permute-start | bytes 393224 | tf_op jit(solution)/shard_map/ppermute | solution.py:220
  31.2 5.6 %collective-permute-start.8 = (bf16[128,4096]{1,0:T(8,128)(2,1)S(1)}, bf16[128,4096]{1,0:T(8,128)(2,1)S(1)}, u32[]{:S(2)}, u32[]{:S(2)}) collective-permute-start(bf16[128,4096]{1,0:T(8,128)(2,1)S(1)} %collective-permute-done.refs_0_), channel_id=1, source_target_pairs={{0,1},{1,0},{2,3},{3,2},{4,5},{5,4},{6,7},{7,6},{8,9},{9,8},{10,11... | collective-permute-start | bytes 3145736 | tf_op jit(solution)/shard_map/ppermute | solution.py:28
  31.2 9.5 %collective-permute-start.9 = (bf16[256,256]{1,0:T(8,128)(2,1)S(1)}, bf16[256,256]{1,0:T(8,128)(2,1)S(1)}, u32[]{:S(2)}, u32[]{:S(2)}) collective-permute-start(bf16[256,256]{1,0:T(8,128)(2,1)S(1)} %collective-permute-done.4.refs_6_), channel_id=1, source_target_pairs={{0,8},{8,16},{16,24},{24,28},{28,20},{20,12},{12,4},{4,0},{1,9},{9... | collective-permute-start | bytes 393224 | tf_op jit(solution)/shard_map/ppermute | solution.py:220
  32.8 2.2 %copy-start.1 = (bf16[4096,512]{1,0:T(8,128)(2,1)S(1)}, bf16[4096,512]{1,0:T(8,128)(2,1)}, u32[]{:S(2)}) copy-start(bf16[4096,512]{1,0:T(8,128)(2,1)} %copy-done) | copy-start | bytes 12582916
  36.7 3.9 %copy-start.7 = (bf16[256,512]{1,0:T(8,128)(2,1)S(1)}, bf16[256,512]{1,0:T(8,128)(2,1)}, u32[]{:S(2)}) copy-start(bf16[256,512]{1,0:T(8,128)(2,1)} %copy-done.6) | copy-start | bytes 786436
  38.6 5.7 %collective-permute-start.11 = (bf16[256,256]{1,0:T(8,128)(2,1)S(1)}, bf16[256,256]{1,0:T(8,128)(2,1)S(1)}, u32[]{:S(2)}, u32[]{:S(2)}) collective-permute-start(bf16[256,256]{1,0:T(8,128)(2,1)S(1)} %get-tuple-element.41.refs_2_), channel_id=1, source_target_pairs={{0,8},{8,16},{16,24},{24,28},{28,20},{20,12},{12,4},{4,0},{1,9},{9... | collective-permute-start | bytes 393224 | tf_op jit(solution)/shard_map/ppermute | solution.py:220
  40.2 5.6 %collective-permute-start.15 = (bf16[256,256]{1,0:T(8,128)(2,1)S(1)}, bf16[256,256]{1,0:T(8,128)(2,1)S(1)}, u32[]{:S(2)}, u32[]{:S(2)}) collective-permute-start(bf16[256,256]{1,0:T(8,128)(2,1)S(1)} %get-tuple-element.41.refs_2_), channel_id=1, source_target_pairs={{0,4},{8,0},{16,8},{24,16},{28,24},{20,28},{12,20},{4,12},{1,5},{9... | collective-permute-start | bytes 393224 | tf_op jit(solution)/shard_map/ppermute | solution.py:220
  44.3 5.0 %collective-permute-start.12 = (bf16[256,256]{1,0:T(8,128)(2,1)S(1)}, bf16[256,256]{1,0:T(8,128)(2,1)S(1)}, u32[]{:S(2)}, u32[]{:S(2)}) collective-permute-start(bf16[256,256]{1,0:T(8,128)(2,1)S(1)} %collective-permute-done.11.refs_3_), channel_id=1, source_target_pairs={{0,8},{8,16},{16,24},{24,28},{28,20},{20,12},{12,4},{4,0},{1,9},{9... | collective-permute-start | bytes 393224 | tf_op jit(solution)/shard_map/ppermute | solution.py:220
  45.8 5.0 %collective-permute-start.16 = (bf16[256,256]{1,0:T(8,128)(2,1)S(1)}, bf16[256,256]{1,0:T(8,128)(2,1)S(1)}, u32[]{:S(2)}, u32[]{:S(2)}) collective-permute-start(bf16[256,256]{1,0:T(8,128)(2,1)S(1)} %collective-permute-done.15.refs_4_), channel_id=1, source_target_pairs={{0,4},{8,0},{16,8},{24,16},{28,24},{20,28},{12,20},{4,12},{1,5},{9... | collective-permute-start | bytes 393224 | tf_op jit(solution)/shard_map/ppermute | solution.py:220
  49.2 5.0 %collective-permute-start.13 = (bf16[256,256]{1,0:T(8,128)(2,1)S(1)}, bf16[256,256]{1,0:T(8,128)(2,1)S(1)}, u32[]{:S(2)}, u32[]{:S(2)}) collective-permute-start(bf16[256,256]{1,0:T(8,128)(2,1)S(1)} %collective-permute-done.12.refs_5_), channel_id=1, source_target_pairs={{0,8},{8,16},{16,24},{24,28},{28,20},{20,12},{12,4},{4,0},{1,9},{9... | collective-permute-start | bytes 393224 | tf_op jit(solution)/shard_map/ppermute | solution.py:220
  50.8 5.0 %collective-permute-start.10 = (bf16[128,512]{1,0:T(8,128)(2,1)S(1)}, bf16[128,512]{1,0:T(8,128)(2,1)S(1)}, u32[]{:S(2)}, u32[]{:S(2)}) collective-permute-start(bf16[128,512]{1,0:T(8,128)(2,1)S(1)} %get-tuple-element.43), channel_id=1, source_target_pairs={{0,1},{1,0},{2,3},{3,2},{4,5},{5,4},{6,7},{7,6},{8,9},{9,8},{10,11... | collective-permute-start | bytes 393224 | tf_op jit(solution)/shard_map/ppermute | solution.py:28
  50.8 5.9 %collective-permute-start.17 = (bf16[256,256]{1,0:T(8,128)(2,1)S(1)}, bf16[256,256]{1,0:T(8,128)(2,1)S(1)}, u32[]{:S(2)}, u32[]{:S(2)}) collective-permute-start(bf16[256,256]{1,0:T(8,128)(2,1)S(1)} %collective-permute-done.16.refs_6_), channel_id=1, source_target_pairs={{0,4},{8,0},{16,8},{24,16},{28,24},{20,28},{12,20},{4,12},{1,5},{9... | collective-permute-start | bytes 393224 | tf_op jit(solution)/shard_map/ppermute | solution.py:220
  54.3 5.0 %collective-permute-start.14 = (bf16[256,256]{1,0:T(8,128)(2,1)S(1)}, bf16[256,256]{1,0:T(8,128)(2,1)S(1)}, u32[]{:S(2)}, u32[]{:S(2)}) collective-permute-start(bf16[256,256]{1,0:T(8,128)(2,1)S(1)} %collective-permute-done.13.refs_7_), channel_id=1, source_target_pairs={{0,8},{8,16},{16,24},{24,28},{28,20},{20,12},{12,4},{4,0},{1,9},{9... | collective-permute-start | bytes 393224 | tf_op jit(solution)/shard_map/ppermute | solution.py:220
  60.3 5.0 %collective-permute-start.18 = (bf16[128,512]{1,0:T(8,128)(2,1)S(1)}, bf16[128,512]{1,0:T(8,128)(2,1)S(1)}, u32[]{:S(2)}, u32[]{:S(2)}) collective-permute-start(bf16[128,512]{1,0:T(8,128)(2,1)S(1)} %attend.6), channel_id=1, source_target_pairs={{0,2},{1,3},{2,0},{3,1},{4,6},{5,7},{6,4},{7,5},{8,10},{9,11},{10,... | collective-permute-start | bytes 393224 | tf_op jit(solution)/shard_map/ppermute | solution.py:28
  62.8 5.3 %collective-permute-start.19 = (bf16[128,512]{1,0:T(8,128)(2,1)S(1)}, bf16[128,512]{1,0:T(8,128)(2,1)S(1)}, u32[]{:S(2)}, u32[]{:S(2)}) collective-permute-start(bf16[128,512]{1,0:T(8,128)(2,1)S(1)} %attend.7), channel_id=1, source_target_pairs={{0,3},{1,2},{2,1},{3,0},{4,7},{5,6},{6,5},{7,4},{8,11},{9,10},{10,... | collective-permute-start | bytes 393224 | tf_op jit(solution)/shard_map/ppermute | solution.py:28
where the time goes:
time: 69.6 us; the launch traced here: 69.4 us
  waiting for transfers between devices  21.5 us (31%)
  starting transfers between devices  20.4 us (29%)
  Pallas kernels  19.8 us (28%)
  local copies, waits for them, and re-layouts  7.04 us (10%)
    ppermute x14, waiting for transfers between devices, advance(): self.front[way] = lax.ppermute(value, 'seq', pairs)  17 us
    ppermute x14, starting transfers between devices, advance(): self.front[way] = lax.ppermute(value, 'seq', pairs)  15.8 us
    pallas_call x3, Pallas kernels, project(): pl.pallas_call(functools.partial(project_kernel, len(pieces), early, befo...  8.22 us
    pallas_call x4, Pallas kernels, attend(): pl.pallas_call(kernel, in_specs=[SMEM] + [VMEM] * (len(queries) + len(arr...  7.25 us
    unnamed x16, local copies, waits for them, and re-layouts  7.04 us
    ppermute x6, starting transfers between devices, swap(): lax.ppermute(value, axis, [(source, source ^ mask) for source in range(co...  4.58 us
    ppermute x6, waiting for transfers between devices, swap(): lax.ppermute(value, axis, [(source, source ^ mask) for source in range(co...  4.43 us
    pallas_call x2, Pallas kernels, deliver(): pl.pallas_call(functools.partial(deliver_kernel, masks), in_specs=[SMEM]...  2.52 us
  transfers between devices with their start and end apart: 20, of which 12 were waited for; matrix products, arithmetic and copies ran while one was open for 1% of the time, Pallas kernels for 25%

commit v1 on v0

--- a/solution.py
+++ b/solution.py
@@ -158,7 +158,7 @@
         out_specs=[VMEM] * len(shapes),
         out_shape=shapes,
         scratch_shapes=scratch,
-        compiler_params=pltpu.CompilerParams(vmem_limit_bytes=28 * MIB),
+        compiler_params=pltpu.CompilerParams(vmem_limit_bytes=20 * MIB),
         cost_estimate=pl.CostEstimate(
             flops=2 * total * width * (q_cols + 2 * k_cols),
             bytes_accessed=2 * width * (q_cols + 2 * k_cols) + 2 * total * width,
@@ -266,7 +266,7 @@
         in_specs=[SMEM] * 3,
         out_specs=SMEM,
         out_shape=jax.ShapeDtypeStruct((length,), jnp.int32),
-        compiler_params=pltpu.CompilerParams(vmem_limit_bytes=16 * MIB),
+        compiler_params=pltpu.CompilerParams(vmem_limit_bytes=4 * MIB),
         name="plan",
     )(info, vertical, slash)
 
@@ -403,7 +403,9 @@
         in_specs=[SMEM] + [VMEM] * (len(queries) + len(arrays) + len(held)),
         out_specs=[VMEM] * len(shapes),
         out_shape=shapes,
-        compiler_params=pltpu.CompilerParams(vmem_limit_bytes=28 * MIB),
+        compiler_params=pltpu.CompilerParams(
+            vmem_limit_bytes=10 * MIB + 4 * sum(a.size for a in (*queries, *arrays))
+        ),
         cost_estimate=pl.CostEstimate(
             flops=4 * len(lanes) * rows * q_cols * len(slots) * spread.chunks * rows,
             bytes_accessed=2 * sum(a.size for a in arrays) + 4 * len(lanes) * rows * q_cols,
@@ -435,7 +437,7 @@
         out_shape=jax.ShapeDtypeStruct((1, rows, count * cols), jnp.bfloat16),
         input_output_aliases={1 + len(pieces): 0} if begun else {},
         scratch_shapes=[pltpu.SemaphoreType.DMA((len(pieces),))],
-        compiler_params=pltpu.CompilerParams(vmem_limit_bytes=16 * MIB),
+        compiler_params=pltpu.CompilerParams(vmem_limit_bytes=4 * MIB),
         name="deliver",
     )(info, *pieces, *begun)
 

time: 69.6 us -> 69.6 us (level)
  no operation moved by 1% of the time
where the time goes in v1:
time: 69.6 us; the launch traced here: 69.4 us
  waiting for transfers between devices  21.5 us (31%)
  starting transfers between devices  20.4 us (29%)
  Pallas kernels  19.8 us (28%)
  local copies, waits for them, and re-layouts  7.04 us (10%)
    ppermute x14, waiting for transfers between devices, advance(): self.front[way] = lax.ppermute(value, 'seq', pairs)  17 us
    ppermute x14, starting transfers between devices, advance(): self.front[way] = lax.ppermute(value, 'seq', pairs)  15.8 us
    pallas_call x3, Pallas kernels, project(): pl.pallas_call(functools.partial(project_kernel, len(pieces), early, befo...  8.22 us
    pallas_call x4, Pallas kernels, attend(): pl.pallas_call(kernel, in_specs=[SMEM] + [VMEM] * (len(queries) + len(arr...  7.24 us
    unnamed x16, local copies, waits for them, and re-layouts  7.04 us
    ppermute x6, starting transfers between devices, swap(): lax.ppermute(value, axis, [(source, source ^ mask) for source in range(co...  4.58 us
    ppermute x6, waiting for transfers between devices, swap(): lax.ppermute(value, axis, [(source, source ^ mask) for source in range(co...  4.43 us
    pallas_call x2, Pallas kernels, deliver(): pl.pallas_call(functools.partial(deliver_kernel, masks), in_specs=[SMEM]...  2.52 us
  transfers between devices with their start and end apart: 20, of which 12 were waited for; matrix products, arithmetic and copies ran while one was open for 1% of the time, Pallas kernels for 25%

profile of v1, /device:TPU:0, one launch (start us, length us, event | category | flops | bytes accessed | tf_op | source)
XLA Modules:
  0.0 69.4 jit_solution(761625180332142301)
XLA Ops:
  0.5 2.5 %collective-permute-start = (bf16[128,4096]{1,0:T(8,128)(2,1)}, bf16[128,4096]{1,0:T(8,128)(2,1)S(1)}, u32[]{:S(2)}, u32[]{:S(2)}) collective-permute-start(bf16[128,4096]{1,0:T(8,128)(2,1)} %bitcast.5), channel_id=1, source_target_pairs={{0,2},{1,3},{2,0},{3,1},{4,6},{5,7},{6,4},{7,5},{8,10},{9,11},{10,... | collective-permute-start | bytes 3145736 | tf_op jit(solution)/shard_map/ppermute | solution.py:28
  3.4 1.0 %copy-done.2 = bf16[128,4096]{1,0:T(8,128)(2,1)} copy-done((bf16[128,4096]{1,0:T(8,128)(2,1)}, bf16[128,4096]{1,0:T(8,128)(2,1)S(1)}, u32[]{:S(2)}) %copy-start.2) | copy-done | bytes 1048600
  4.4 1.2 %copy-done.3 = bf16[128,4096]{1,0:T(8,128)(2,1)S(1)} copy-done((bf16[128,4096]{1,0:T(8,128)(2,1)S(1)}, bf16[128,4096]{1,0:T(8,128)(2,1)}, u32[]{:S(2)}) %copy-start.3) | copy-done | bytes 1048600
  5.6 4.6 %project.3 = (bf16[256,512]{1,0:T(8,128)(2,1)S(1)}, bf16[256,256]{1,0:T(8,128)(2,1)S(1)}, f32[1,4096]{1,0:T(1,128)S(1)}, bf16[4096,128]{1,0:T(8,128)(2,1)S(1)}, ...) custom-call(bf16[128,4096]{1,0:T(8,128)(2,1)} %bitcast.6, bf16[128,4096]{1,0:T(8,128)(2,1)S(1)} %copy-done.3, ...), custom_call_target="tpu_custom_call" | custom-call | flops 1610612736 | bytes 8388608 | tf_op jit(solution)/shard_map/project/pallas_call | solution.py:155
  10.3 1.9 %copy-done = bf16[4096,512]{1,0:T(8,128)(2,1)} copy-done((bf16[4096,512]{1,0:T(8,128)(2,1)}, bf16[4096,512]{1,0:T(8,128)(2,1)S(1)}, u32[]{:S(2)}) %copy-start) | copy-done | bytes 4194328
  12.9 2.5 %collective-permute-start.2 = (bf16[256,256]{1,0:T(8,128)(2,1)S(1)}, bf16[256,256]{1,0:T(8,128)(2,1)}, u32[]{:S(2)}, u32[]{:S(2)}) collective-permute-start(bf16[256,256]{1,0:T(8,128)(2,1)S(1)} %get-tuple-element.30.refs_1_), channel_id=1, source_target_pairs={{0,8},{8,16},{16,24},{24,28},{28,20},{20,12},{12,4},{4,0},{1,9},{9... | collective-permute-start | bytes 393224 | tf_op jit(solution)/shard_map/ppermute | solution.py:220
  15.5 1.8 %plan.1.plan_ref = s32[33]{0:T(128)S(1)} custom-call(s32[2]{0:T(128)S(1)} %pad_add_fusion.info_ref, s32[4,4,4]{2,1,0:T(4,128)S(1)} %copy-done.4, s32[4,4,4]{2,1,0:T(4,128)S(1)} %copy-done.5), custom_call_target="tpu_custom_call" | custom-call | tf_op jit(solution)/shard_map/plan/pallas_call | solution.py:264
  17.3 1.9 %collective-permute-done.2.refs_2_ = bf16[256,256]{1,0:T(8,128)(2,1)} collective-permute-done((bf16[256,256]{1,0:T(8,128)(2,1)S(1)}, bf16[256,256]{1,0:T(8,128)(2,1)}, u32[]{:S(2)}, u32[]{:S(2)}) %collective-permute-start.2) | collective-permute-done | bytes 131104 | tf_op jit(solution)/shard_map/ppermute | solution.py:220
  19.2 1.8 %collective-permute-start.3 = (bf16[256,256]{1,0:T(8,128)(2,1)}, bf16[256,256]{1,0:T(8,128)(2,1)S(1)}, u32[]{:S(2)}, u32[]{:S(2)}) collective-permute-start(bf16[256,256]{1,0:T(8,128)(2,1)} %collective-permute-done.2.refs_2_), channel_id=1, source_target_pairs={{0,8},{8,16},{16,24},{24,28},{28,20},{20,12},{12,4},{4,0},{1,9},{9... | collective-permute-start | bytes 393224 | tf_op jit(solution)/shard_map/ppermute | solution.py:220
  21.3 3.2 %collective-permute-done.3.refs_4_ = bf16[256,256]{1,0:T(8,128)(2,1)S(1)} collective-permute-done((bf16[256,256]{1,0:T(8,128)(2,1)}, bf16[256,256]{1,0:T(8,128)(2,1)S(1)}, u32[]{:S(2)}, u32[]{:S(2)}) %collective-permute-start.3) | collective-permute-done | bytes 131104 | tf_op jit(solution)/shard_map/ppermute | solution.py:220
  24.5 1.7 %collective-permute-start.4 = (bf16[256,256]{1,0:T(8,128)(2,1)S(1)}, bf16[256,256]{1,0:T(8,128)(2,1)S(1)}, u32[]{:S(2)}, u32[]{:S(2)}) collective-permute-start(bf16[256,256]{1,0:T(8,128)(2,1)S(1)} %collective-permute-done.3.refs_4_), channel_id=1, source_target_pairs={{0,8},{8,16},{16,24},{24,28},{28,20},{20,12},{12,4},{4,0},{1,9},{9... | collective-permute-start | bytes 393224 | tf_op jit(solution)/shard_map/ppermute | solution.py:220
  27.0 2.4 %collective-permute-done.4.refs_6_ = bf16[256,256]{1,0:T(8,128)(2,1)S(1)} collective-permute-done((bf16[256,256]{1,0:T(8,128)(2,1)S(1)}, bf16[256,256]{1,0:T(8,128)(2,1)S(1)}, u32[]{:S(2)}, u32[]{:S(2)}) %collective-permute-start.4) | collective-permute-done | bytes 131104 | tf_op jit(solution)/shard_map/ppermute | solution.py:220
  29.4 1.7 %collective-permute-done.7.refs_7_ = bf16[256,256]{1,0:T(8,128)(2,1)S(1)} collective-permute-done((bf16[256,256]{1,0:T(8,128)(2,1)S(1)}, bf16[256,256]{1,0:T(8,128)(2,1)S(1)}, u32[]{:S(2)}, u32[]{:S(2)}) %collective-permute-start.7) | collective-permute-done | bytes 131104 | tf_op jit(solution)/shard_map/ppermute | solution.py:220
  31.2 1.6 %collective-permute-start.9 = (bf16[256,256]{1,0:T(8,128)(2,1)S(1)}, bf16[256,256]{1,0:T(8,128)(2,1)S(1)}, u32[]{:S(2)}, u32[]{:S(2)}) collective-permute-start(bf16[256,256]{1,0:T(8,128)(2,1)S(1)} %collective-permute-done.4.refs_6_), channel_id=1, source_target_pairs={{0,8},{8,16},{16,24},{24,28},{28,20},{20,12},{12,4},{4,0},{1,9},{9... | collective-permute-start | bytes 393224 | tf_op jit(solution)/shard_map/ppermute | solution.py:220
  32.8 2.2 %copy-done.1 = bf16[4096,512]{1,0:T(8,128)(2,1)S(1)} copy-done((bf16[4096,512]{1,0:T(8,128)(2,1)S(1)}, bf16[4096,512]{1,0:T(8,128)(2,1)}, u32[]{:S(2)}) %copy-start.1) | copy-done | bytes 4194328
  34.9 1.8 %project.4 = (bf16[128,512]{1,0:T(8,128)(2,1)S(1)}, bf16[128,256]{1,0:T(8,128)(2,1)S(1)}) custom-call(bf16[128,4096]{1,0:T(8,128)(2,1)S(1)} %collective-permute-done.refs_0_, f32[1,4096]{1,0:T(1,128)S(1)} %get-tuple-element.34.refs_1_.refs_2_, bf16[4096,512]{1,0:T(8,128)(2,1)S(1)} %copy-done.1, bf16[4096,128]{1,0:T(8,128)(2,1)S(1)} %get-tuple-element.36.refs_3_.refs_4_, ...), custom_call_target="tpu_custom_call" | custom-call | flops 805306368 | bytes 7340032 | tf_op jit(solution)/shard_map/project/pallas_call | solution.py:155
  36.8 1.8 %project.5 = (bf16[128,512]{1,0:T(8,128)(2,1)S(1)}, bf16[256,256]{1,0:T(8,128)(2,1)S(1)}) custom-call(bf16[128,4096]{1,0:T(8,128)(2,1)S(1)} %collective-permute-done.8.refs_0_, bf16[128,256]{1,0:T(8,128)(2,1)S(1)} %get-tuple-element.40.refs_1_, f32[1,4096]{1,0:T(1,128)S(1)} %get-tuple-element.34.refs_1_.refs_2_, bf16[4096,512]{1,0:T(8,128)(2,1)S(1)} %copy-done.1, ...), custom_call_target="tpu_custom_call" | custom-call | flops 805306368 | bytes 7340032 | tf_op jit(solution)/shard_map/project/pallas_call | solution.py:155
  38.6 1.6 %collective-permute-start.11 = (bf16[256,256]{1,0:T(8,128)(2,1)S(1)}, bf16[256,256]{1,0:T(8,128)(2,1)S(1)}, u32[]{:S(2)}, u32[]{:S(2)}) collective-permute-start(bf16[256,256]{1,0:T(8,128)(2,1)S(1)} %get-tuple-element.41.refs_2_), channel_id=1, source_target_pairs={{0,8},{8,16},{16,24},{24,28},{28,20},{20,12},{12,4},{4,0},{1,9},{9... | collective-permute-start | bytes 393224 | tf_op jit(solution)/shard_map/ppermute | solution.py:220
  40.7 2.9 %attend.4 = (bf16[128,512]{1,0:T(8,128)(2,1)S(1)}, bf16[128,512]{1,0:T(8,128)(2,1)S(1)}) custom-call(s32[33]{0:T(128)S(1)} %plan.1.plan_ref, bf16[256,512]{1,0:T(8,128)(2,1)S(1)} %copy-done.7, bf16[256,256]{1,0:T(8,128)(2,1)S(1)} %get-tuple-element.30.refs_1_, bf16[256,256]{1,0:T(8,128)(2,1)} %collective-permute-done.2.refs_2_, ...), custom_call_target="tpu_custom_call" | custom-call | flops 536870912 | bytes 1572864 | tf_op jit(solution)/shard_map/attend/pallas_call | solution.py:401
  44.3 1.6 %collective-permute-start.12 = (bf16[256,256]{1,0:T(8,128)(2,1)S(1)}, bf16[256,256]{1,0:T(8,128)(2,1)S(1)}, u32[]{:S(2)}, u32[]{:S(2)}) collective-permute-start(bf16[256,256]{1,0:T(8,128)(2,1)S(1)} %collective-permute-done.11.refs_3_), channel_id=1, source_target_pairs={{0,8},{8,16},{16,24},{24,28},{28,20},{20,12},{12,4},{4,0},{1,9},{9... | collective-permute-start | bytes 393224 | tf_op jit(solution)/shard_map/ppermute | solution.py:220
  46.3 2.9 %collective-permute-done.12.refs_5_ = bf16[256,256]{1,0:T(8,128)(2,1)S(1)} collective-permute-done((bf16[256,256]{1,0:T(8,128)(2,1)S(1)}, bf16[256,256]{1,0:T(8,128)(2,1)S(1)}, u32[]{:S(2)}, u32[]{:S(2)}) %collective-permute-start.12) | collective-permute-done | bytes 131104 | tf_op jit(solution)/shard_map/ppermute | solution.py:220
  49.2 1.6 %collective-permute-start.13 = (bf16[256,256]{1,0:T(8,128)(2,1)S(1)}, bf16[256,256]{1,0:T(8,128)(2,1)S(1)}, u32[]{:S(2)}, u32[]{:S(2)}) collective-permute-start(bf16[256,256]{1,0:T(8,128)(2,1)S(1)} %collective-permute-done.12.refs_5_), channel_id=1, source_target_pairs={{0,8},{8,16},{16,24},{24,28},{28,20},{20,12},{12,4},{4,0},{1,9},{9... | collective-permute-start | bytes 393224 | tf_op jit(solution)/shard_map/ppermute | solution.py:220
  51.3 3.0 %collective-permute-done.13.refs_7_ = bf16[256,256]{1,0:T(8,128)(2,1)S(1)} collective-permute-done((bf16[256,256]{1,0:T(8,128)(2,1)S(1)}, bf16[256,256]{1,0:T(8,128)(2,1)S(1)}, u32[]{:S(2)}, u32[]{:S(2)}) %collective-permute-start.13) | collective-permute-done | bytes 131104 | tf_op jit(solution)/shard_map/ppermute | solution.py:220
  54.3 1.6 %collective-permute-start.14 = (bf16[256,256]{1,0:T(8,128)(2,1)S(1)}, bf16[256,256]{1,0:T(8,128)(2,1)S(1)}, u32[]{:S(2)}, u32[]{:S(2)}) collective-permute-start(bf16[256,256]{1,0:T(8,128)(2,1)S(1)} %collective-permute-done.13.refs_7_), channel_id=1, source_target_pairs={{0,8},{8,16},{16,24},{24,28},{28,20},{20,12},{12,4},{4,0},{1,9},{9... | collective-permute-start | bytes 393224 | tf_op jit(solution)/shard_map/ppermute | solution.py:220
  56.7 2.3 %attend.5 = (f32[1,1,512]{2,1,0:T(1,128)S(1)}, f32[1,1,512]{2,1,0:T(1,128)S(1)}, f32[1,128,512]{2,1,0:T(8,128)S(1)}, f32[1,1,512]{2,1,0:T(1,128)S(1)}, f32[1,1,5...) custom-call(s32[33]{0:T(128)S(1)} %plan.1.plan_ref, bf16[128,512]{1,0:T(8,128)(2,1)S(1)} %get-tuple-element.44.refs_0_, ...), custom_call_target="tpu_custom_call" | custom-call | flops 469762048 | bytes 1441792 | tf_op jit(solution)/shard_map/attend/pallas_call | solution.py:401
  59.2 1.0 %attend.6 = bf16[128,512]{1,0:T(8,128)(2,1)S(1)} custom-call(s32[33]{0:T(128)S(1)} %plan.1.plan_ref, bf16[128,512]{1,0:T(8,128)(2,1)S(1)} %get-tuple-element.44.refs_0_, bf16[128,512]{1,0:T(8,128)(2,1)S(1)} %get-tuple-element.45.refs_1_, bf16[256,256]{1,0:T(8,128)(2,1)S(1)} %collective-permute-done.14.refs_2_, f32[1,1,512]{2,1,0:T(1,128)S(1)} %get-tuple-element.48.refs_3_, ...), custom_call_target="tpu_custom_call" | custom-call | flops 33554432 | bytes 393216 | tf_op jit(solution)/shard_map/attend/pallas_call | solution.py:401
  60.3 1.6 %collective-permute-start.18 = (bf16[128,512]{1,0:T(8,128)(2,1)S(1)}, bf16[128,512]{1,0:T(8,128)(2,1)S(1)}, u32[]{:S(2)}, u32[]{:S(2)}) collective-permute-start(bf16[128,512]{1,0:T(8,128)(2,1)S(1)} %attend.6), channel_id=1, source_target_pairs={{0,2},{1,3},{2,0},{3,1},{4,6},{5,7},{6,4},{7,5},{8,10},{9,11},{10,... | collective-permute-start | bytes 393224 | tf_op jit(solution)/shard_map/ppermute | solution.py:28
  61.8 1.0 %attend.7 = bf16[128,512]{1,0:T(8,128)(2,1)S(1)} custom-call(s32[33]{0:T(128)S(1)} %plan.1.plan_ref, bf16[128,512]{1,0:T(8,128)(2,1)S(1)} %get-tuple-element.44.refs_0_, bf16[128,512]{1,0:T(8,128)(2,1)S(1)} %get-tuple-element.45.refs_1_, bf16[256,256]{1,0:T(8,128)(2,1)S(1)} %collective-permute-done.14.refs_2_, f32[1,1,512]{2,1,0:T(1,128)S(1)} %get-tuple-element.51.refs_3_, ...), custom_call_target="tpu_custom_call" | custom-call | flops 33554432 | bytes 393216 | tf_op jit(solution)/shard_map/attend/pallas_call | solution.py:401
  62.9 1.3 %deliver.2.refs_2_ = bf16[1,128,2048]{2,1,0:T(8,128)(2,1)} custom-call(s32[2]{0:T(128)S(1)} %pad_add_fusion.info_ref, bf16[128,512]{1,0:T(8,128)(2,1)S(1)} %get-tuple-element.54.refs_0_, bf16[128,512]{1,0:T(8,128)(2,1)S(1)} %collective-permute-done.10.refs_1_), custom_call_target="tpu_custom_call" | custom-call | tf_op jit(solution)/shard_map/deliver/pallas_call | solution.py:433
  64.2 1.1 %collective-permute-done.18.refs_0_ = bf16[128,512]{1,0:T(8,128)(2,1)S(1)} collective-permute-done((bf16[128,512]{1,0:T(8,128)(2,1)S(1)}, bf16[128,512]{1,0:T(8,128)(2,1)S(1)}, u32[]{:S(2)}, u32[]{:S(2)}) %collective-permute-start.18) | collective-permute-done | bytes 131104 | tf_op jit(solution)/shard_map/ppermute | solution.py:28
  65.3 2.8 %collective-permute-done.19.refs_1_ = bf16[128,512]{1,0:T(8,128)(2,1)S(1)} collective-permute-done((bf16[128,512]{1,0:T(8,128)(2,1)S(1)}, bf16[128,512]{1,0:T(8,128)(2,1)S(1)}, u32[]{:S(2)}, u32[]{:S(2)}) %collective-permute-start.19) | collective-permute-done | bytes 131104 | tf_op jit(solution)/shard_map/ppermute | solution.py:28
  68.1 1.3 %deliver.3 = bf16[1,128,2048]{2,1,0:T(8,128)(2,1)} custom-call(s32[2]{0:T(128)S(1)} %pad_add_fusion.info_ref, bf16[128,512]{1,0:T(8,128)(2,1)S(1)} %collective-permute-done.18.refs_0_, bf16[128,512]{1,0:T(8,128)(2,1)S(1)} %collective-permute-done.19.refs_1_, bf16[1,128,2048]{2,1,0:T(8,128)(2,1)} %deliver.2.refs_2_), custom_call_target="tpu_custom_call", output_to_operand_aliasing={{}: (3, {})} | custom-call | tf_op jit(solution)/shard_map/deliver/pallas_call | solution.py:433
  (39 shorter events, 5.9 us)
Async XLA Ops:
  0.0 3.4 %collective-permute-start.1 = (bf16[128,4096]{1,0:T(8,128)(2,1)}, bf16[128,4096]{1,0:T(8,128)(2,1)S(1)}, u32[]{:S(2)}, u32[]{:S(2)}) collective-permute-start(bf16[128,4096]{1,0:T(8,128)(2,1)} %bitcast.4), channel_id=1, source_target_pairs={{0,1},{1,0},{2,3},{3,2},{4,5},{5,4},{6,7},{7,6},{8,9},{9,8},{10,11... | collective-permute-start | bytes 3145736 | tf_op jit(solution)/shard_map/ppermute | solution.py:28
  0.5 26.5 %collective-permute-start = (bf16[128,4096]{1,0:T(8,128)(2,1)}, bf16[128,4096]{1,0:T(8,128)(2,1)S(1)}, u32[]{:S(2)}, u32[]{:S(2)}) collective-permute-start(bf16[128,4096]{1,0:T(8,128)(2,1)} %bitcast.5), channel_id=1, source_target_pairs={{0,2},{1,3},{2,0},{3,1},{4,6},{5,7},{6,4},{7,5},{8,10},{9,11},{10,... | collective-permute-start | bytes 3145736 | tf_op jit(solution)/shard_map/ppermute | solution.py:28
  3.4 1.0 %copy-start.2 = (bf16[128,4096]{1,0:T(8,128)(2,1)}, bf16[128,4096]{1,0:T(8,128)(2,1)S(1)}, u32[]{:S(2)}) copy-start(bf16[128,4096]{1,0:T(8,128)(2,1)S(1)} %collective-permute-done.1.refs_1_) | copy-start | bytes 3145732
  4.4 1.2 %copy-start.3 = (bf16[128,4096]{1,0:T(8,128)(2,1)S(1)}, bf16[128,4096]{1,0:T(8,128)(2,1)}, u32[]{:S(2)}) copy-start(bf16[128,4096]{1,0:T(8,128)(2,1)} %copy-done.2) | copy-start | bytes 3145732
  5.6 9.8 %copy-start.4 = (s32[4,4,4]{2,1,0:T(4,128)S(1)}, s32[4,4,4]{2,1,0:T(4,128)}, u32[]{:S(2)}) copy-start(s32[4,4,4]{2,1,0:T(4,128)} %vertical_ref.1) | copy-start | bytes 772
  5.6 9.8 %copy-start.5 = (s32[4,4,4]{2,1,0:T(4,128)S(1)}, s32[4,4,4]{2,1,0:T(4,128)}, u32[]{:S(2)}) copy-start(s32[4,4,4]{2,1,0:T(4,128)} %slash_ref.1) | copy-start | bytes 772
  10.2 2.0 %copy-start = (bf16[4096,512]{1,0:T(8,128)(2,1)}, bf16[4096,512]{1,0:T(8,128)(2,1)S(1)}, u32[]{:S(2)}) copy-start(bf16[4096,512]{1,0:T(8,128)(2,1)S(1)} %get-tuple-element.35.refs_2_.refs_3_) | copy-start | bytes 12582916
  12.2 0.7 %copy-start.6 = (bf16[256,512]{1,0:T(8,128)(2,1)}, bf16[256,512]{1,0:T(8,128)(2,1)S(1)}, u32[]{:S(2)}) copy-start(bf16[256,512]{1,0:T(8,128)(2,1)S(1)} %get-tuple-element.42.refs_0_) | copy-start | bytes 786436
  12.9 6.3 %collective-permute-start.2 = (bf16[256,256]{1,0:T(8,128)(2,1)S(1)}, bf16[256,256]{1,0:T(8,128)(2,1)}, u32[]{:S(2)}, u32[]{:S(2)}) collective-permute-start(bf16[256,256]{1,0:T(8,128)(2,1)S(1)} %get-tuple-element.30.refs_1_), channel_id=1, source_target_pairs={{0,8},{8,16},{16,24},{24,28},{28,20},{20,12},{12,4},{4,0},{1,9},{9... | collective-permute-start | bytes 393224 | tf_op jit(solution)/shard_map/ppermute | solution.py:220
  15.4 5.6 %collective-permute-start.5 = (bf16[256,256]{1,0:T(8,128)(2,1)S(1)}, bf16[256,256]{1,0:T(8,128)(2,1)}, u32[]{:S(2)}, u32[]{:S(2)}) collective-permute-start(bf16[256,256]{1,0:T(8,128)(2,1)S(1)} %get-tuple-element.30.refs_1_), channel_id=1, source_target_pairs={{0,4},{8,0},{16,8},{24,16},{28,24},{20,28},{12,20},{4,12},{1,5},{9... | collective-permute-start | bytes 393224 | tf_op jit(solution)/shard_map/ppermute | solution.py:220
  19.2 5.2 %collective-permute-start.3 = (bf16[256,256]{1,0:T(8,128)(2,1)}, bf16[256,256]{1,0:T(8,128)(2,1)S(1)}, u32[]{:S(2)}, u32[]{:S(2)}) collective-permute-start(bf16[256,256]{1,0:T(8,128)(2,1)} %collective-permute-done.2.refs_2_), channel_id=1, source_target_pairs={{0,8},{8,16},{16,24},{24,28},{28,20},{20,12},{12,4},{4,0},{1,9},{9... | collective-permute-start | bytes 393224 | tf_op jit(solution)/shard_map/ppermute | solution.py:220
  21.0 5.2 %collective-permute-start.6 = (bf16[256,256]{1,0:T(8,128)(2,1)}, bf16[256,256]{1,0:T(8,128)(2,1)S(1)}, u32[]{:S(2)}, u32[]{:S(2)}) collective-permute-start(bf16[256,256]{1,0:T(8,128)(2,1)} %collective-permute-done.5.refs_3_), channel_id=1, source_target_pairs={{0,4},{8,0},{16,8},{24,16},{28,24},{20,28},{12,20},{4,12},{1,5},{9... | collective-permute-start | bytes 393224 | tf_op jit(solution)/shard_map/ppermute | solution.py:220
  24.5 5.0 %collective-permute-start.4 = (bf16[256,256]{1,0:T(8,128)(2,1)S(1)}, bf16[256,256]{1,0:T(8,128)(2,1)S(1)}, u32[]{:S(2)}, u32[]{:S(2)}) collective-permute-start(bf16[256,256]{1,0:T(8,128)(2,1)S(1)} %collective-permute-done.3.refs_4_), channel_id=1, source_target_pairs={{0,8},{8,16},{16,24},{24,28},{28,20},{20,12},{12,4},{4,0},{1,9},{9... | collective-permute-start | bytes 393224 | tf_op jit(solution)/shard_map/ppermute | solution.py:220
  26.2 5.0 %collective-permute-start.7 = (bf16[256,256]{1,0:T(8,128)(2,1)S(1)}, bf16[256,256]{1,0:T(8,128)(2,1)S(1)}, u32[]{:S(2)}, u32[]{:S(2)}) collective-permute-start(bf16[256,256]{1,0:T(8,128)(2,1)S(1)} %collective-permute-done.6.refs_5_), channel_id=1, source_target_pairs={{0,4},{8,0},{16,8},{24,16},{28,24},{20,28},{12,20},{4,12},{1,5},{9... | collective-permute-start | bytes 393224 | tf_op jit(solution)/shard_map/ppermute | solution.py:220
  31.2 5.6 %collective-permute-start.8 = (bf16[128,4096]{1,0:T(8,128)(2,1)S(1)}, bf16[128,4096]{1,0:T(8,128)(2,1)S(1)}, u32[]{:S(2)}, u32[]{:S(2)}) collective-permute-start(bf16[128,4096]{1,0:T(8,128)(2,1)S(1)} %collective-permute-done.refs_0_), channel_id=1, source_target_pairs={{0,1},{1,0},{2,3},{3,2},{4,5},{5,4},{6,7},{7,6},{8,9},{9,8},{10,11... | collective-permute-start | bytes 3145736 | tf_op jit(solution)/shard_map/ppermute | solution.py:28
  31.2 9.5 %collective-permute-start.9 = (bf16[256,256]{1,0:T(8,128)(2,1)S(1)}, bf16[256,256]{1,0:T(8,128)(2,1)S(1)}, u32[]{:S(2)}, u32[]{:S(2)}) collective-permute-start(bf16[256,256]{1,0:T(8,128)(2,1)S(1)} %collective-permute-done.4.refs_6_), channel_id=1, source_target_pairs={{0,8},{8,16},{16,24},{24,28},{28,20},{20,12},{12,4},{4,0},{1,9},{9... | collective-permute-start | bytes 393224 | tf_op jit(solution)/shard_map/ppermute | solution.py:220
  32.8 2.2 %copy-start.1 = (bf16[4096,512]{1,0:T(8,128)(2,1)S(1)}, bf16[4096,512]{1,0:T(8,128)(2,1)}, u32[]{:S(2)}) copy-start(bf16[4096,512]{1,0:T(8,128)(2,1)} %copy-done) | copy-start | bytes 12582916
  36.7 3.9 %copy-start.7 = (bf16[256,512]{1,0:T(8,128)(2,1)S(1)}, bf16[256,512]{1,0:T(8,128)(2,1)}, u32[]{:S(2)}) copy-start(bf16[256,512]{1,0:T(8,128)(2,1)} %copy-done.6) | copy-start | bytes 786436
  38.6 5.7 %collective-permute-start.11 = (bf16[256,256]{1,0:T(8,128)(2,1)S(1)}, bf16[256,256]{1,0:T(8,128)(2,1)S(1)}, u32[]{:S(2)}, u32[]{:S(2)}) collective-permute-start(bf16[256,256]{1,0:T(8,128)(2,1)S(1)} %get-tuple-element.41.refs_2_), channel_id=1, source_target_pairs={{0,8},{8,16},{16,24},{24,28},{28,20},{20,12},{12,4},{4,0},{1,9},{9... | collective-permute-start | bytes 393224 | tf_op jit(solution)/shard_map/ppermute | solution.py:220
  40.2 5.6 %collective-permute-start.15 = (bf16[256,256]{1,0:T(8,128)(2,1)S(1)}, bf16[256,256]{1,0:T(8,128)(2,1)S(1)}, u32[]{:S(2)}, u32[]{:S(2)}) collective-permute-start(bf16[256,256]{1,0:T(8,128)(2,1)S(1)} %get-tuple-element.41.refs_2_), channel_id=1, source_target_pairs={{0,4},{8,0},{16,8},{24,16},{28,24},{20,28},{12,20},{4,12},{1,5},{9... | collective-permute-start | bytes 393224 | tf_op jit(solution)/shard_map/ppermute | solution.py:220
  44.3 5.0 %collective-permute-start.12 = (bf16[256,256]{1,0:T(8,128)(2,1)S(1)}, bf16[256,256]{1,0:T(8,128)(2,1)S(1)}, u32[]{:S(2)}, u32[]{:S(2)}) collective-permute-start(bf16[256,256]{1,0:T(8,128)(2,1)S(1)} %collective-permute-done.11.refs_3_), channel_id=1, source_target_pairs={{0,8},{8,16},{16,24},{24,28},{28,20},{20,12},{12,4},{4,0},{1,9},{9... | collective-permute-start | bytes 393224 | tf_op jit(solution)/shard_map/ppermute | solution.py:220
  45.8 5.0 %collective-permute-start.16 = (bf16[256,256]{1,0:T(8,128)(2,1)S(1)}, bf16[256,256]{1,0:T(8,128)(2,1)S(1)}, u32[]{:S(2)}, u32[]{:S(2)}) collective-permute-start(bf16[256,256]{1,0:T(8,128)(2,1)S(1)} %collective-permute-done.15.refs_4_), channel_id=1, source_target_pairs={{0,4},{8,0},{16,8},{24,16},{28,24},{20,28},{12,20},{4,12},{1,5},{9... | collective-permute-start | bytes 393224 | tf_op jit(solution)/shard_map/ppermute | solution.py:220
  49.2 5.0 %collective-permute-start.13 = (bf16[256,256]{1,0:T(8,128)(2,1)S(1)}, bf16[256,256]{1,0:T(8,128)(2,1)S(1)}, u32[]{:S(2)}, u32[]{:S(2)}) collective-permute-start(bf16[256,256]{1,0:T(8,128)(2,1)S(1)} %collective-permute-done.12.refs_5_), channel_id=1, source_target_pairs={{0,8},{8,16},{16,24},{24,28},{28,20},{20,12},{12,4},{4,0},{1,9},{9... | collective-permute-start | bytes 393224 | tf_op jit(solution)/shard_map/ppermute | solution.py:220
  50.8 5.0 %collective-permute-start.10 = (bf16[128,512]{1,0:T(8,128)(2,1)S(1)}, bf16[128,512]{1,0:T(8,128)(2,1)S(1)}, u32[]{:S(2)}, u32[]{:S(2)}) collective-permute-start(bf16[128,512]{1,0:T(8,128)(2,1)S(1)} %get-tuple-element.43), channel_id=1, source_target_pairs={{0,1},{1,0},{2,3},{3,2},{4,5},{5,4},{6,7},{7,6},{8,9},{9,8},{10,11... | collective-permute-start | bytes 393224 | tf_op jit(solution)/shard_map/ppermute | solution.py:28
  50.8 5.9 %collective-permute-start.17 = (bf16[256,256]{1,0:T(8,128)(2,1)S(1)}, bf16[256,256]{1,0:T(8,128)(2,1)S(1)}, u32[]{:S(2)}, u32[]{:S(2)}) collective-permute-start(bf16[256,256]{1,0:T(8,128)(2,1)S(1)} %collective-permute-done.16.refs_6_), channel_id=1, source_target_pairs={{0,4},{8,0},{16,8},{24,16},{28,24},{20,28},{12,20},{4,12},{1,5},{9... | collective-permute-start | bytes 393224 | tf_op jit(solution)/shard_map/ppermute | solution.py:220
  54.3 5.0 %collective-permute-start.14 = (bf16[256,256]{1,0:T(8,128)(2,1)S(1)}, bf16[256,256]{1,0:T(8,128)(2,1)S(1)}, u32[]{:S(2)}, u32[]{:S(2)}) collective-permute-start(bf16[256,256]{1,0:T(8,128)(2,1)S(1)} %collective-permute-done.13.refs_7_), channel_id=1, source_target_pairs={{0,8},{8,16},{16,24},{24,28},{28,20},{20,12},{12,4},{4,0},{1,9},{9... | collective-permute-start | bytes 393224 | tf_op jit(solution)/shard_map/ppermute | solution.py:220
  60.3 5.0 %collective-permute-start.18 = (bf16[128,512]{1,0:T(8,128)(2,1)S(1)}, bf16[128,512]{1,0:T(8,128)(2,1)S(1)}, u32[]{:S(2)}, u32[]{:S(2)}) collective-permute-start(bf16[128,512]{1,0:T(8,128)(2,1)S(1)} %attend.6), channel_id=1, source_target_pairs={{0,2},{1,3},{2,0},{3,1},{4,6},{5,7},{6,4},{7,5},{8,10},{9,11},{10,... | collective-permute-start | bytes 393224 | tf_op jit(solution)/shard_map/ppermute | solution.py:28
  62.8 5.3 %collective-permute-start.19 = (bf16[128,512]{1,0:T(8,128)(2,1)S(1)}, bf16[128,512]{1,0:T(8,128)(2,1)S(1)}, u32[]{:S(2)}, u32[]{:S(2)}) collective-permute-start(bf16[128,512]{1,0:T(8,128)(2,1)S(1)} %attend.7), channel_id=1, source_target_pairs={{0,3},{1,2},{2,1},{3,0},{4,7},{5,6},{6,5},{7,4},{8,11},{9,10},{10,... | collective-permute-start | bytes 393224 | tf_op jit(solution)/shard_map/ppermute | solution.py:28

commit v2 on v1

--- a/solution.py
+++ b/solution.py
@@ -447,10 +447,10 @@
     assert lax.axis_size("doc") == 4
     place = lax.axis_index("seq")
     doc_place = lax.axis_index("doc")
-    info = jnp.stack([place, doc_place]).astype(jnp.int32)
-    cosine, sine = rope_table(place * rows + jnp.arange(rows, dtype=jnp.int32), HEAD_WIDTH)
+    info = after(jnp.stack([place, doc_place, place * rows]).astype(jnp.int32))
+    cosine, sine = rope_table(info[2:] + jnp.arange(rows, dtype=jnp.int32), HEAD_WIDTH)
     table = jnp.concatenate([cosine, cosine, -sine, sine], axis=1)
-    own = tokens[0]
+    own = after(tokens, info)[0]
     gain = norm_gain.reshape(1, width)
     long = lax.axis_size("seq") > 8 or lax.axis_size("seq") % 2 == 1
     ring = Gathered if long else Ring

time: 69.6 us -> 64.3 us (0.924)
  local copies, waits for them, and re-layouts: 7.04 us -> 0.6 us
  waiting for transfers between devices: 21.5 us -> 22.5 us
    unnamed x16 -> x4, local copies, waits for them, and re-layouts: 7.04 us -> 0.01 us
    ppermute x6, waiting for transfers between devices: 4.43 us -> 9.76 us  [swap(): lax.ppermute(value, axis, [(source, source ^ mask) for source in range(co...]
    ppermute x14, waiting for transfers between devices: 17 us -> 12.8 us  [advance(): self.front[way] = lax.ppermute(value, 'seq', pairs)]
  transfers between devices with their start and end apart: 20 -> 20, of which waited for: 12 -> 10; matrix products, arithmetic and copies ran while one was open for 1% -> 3% of each run, Pallas kernels for 25% -> 27%
where the time goes in v2:
time: 64.3 us; the launch traced here: 64.1 us
  waiting for transfers between devices  22.5 us (35%)
  starting transfers between devices  20.4 us (32%)
  Pallas kernels  19.3 us (30%)
  other arithmetic  1.16 us (2%)
    ppermute x14, starting transfers between devices, advance(): self.front[way] = lax.ppermute(value, 'seq', pairs)  15.7 us
    ppermute x14, waiting for transfers between devices, advance(): self.front[way] = lax.ppermute(value, 'seq', pairs)  12.8 us
    ppermute x6, waiting for transfers between devices, swap(): lax.ppermute(value, axis, [(source, source ^ mask) for source in range(co...  9.76 us
    pallas_call x3, Pallas kernels, project(): pl.pallas_call(functools.partial(project_kernel, len(pieces), early, befo...  8.21 us
    pallas_call x4, Pallas kernels, attend(): pl.pallas_call(kernel, in_specs=[SMEM] + [VMEM] * (len(queries) + len(arr...  6.78 us
    ppermute x6, starting transfers between devices, swap(): lax.ppermute(value, axis, [(source, source ^ mask) for source in range(co...  4.66 us
    pallas_call x2, Pallas kernels, deliver(): pl.pallas_call(functools.partial(deliver_kernel, masks), in_specs=[SMEM]...  2.52 us
    pallas_call x1, Pallas kernels, plan(): pl.pallas_call(functools.partial(plan_kernel, ring, lanes, heads, count,...  1.82 us
  transfers between devices with their start and end apart: 20, of which 10 were waited for; matrix products, arithmetic and copies ran while one was open for 3% of the time, Pallas kernels for 27%

profile of v2, /device:TPU:0, one launch (start us, length us, event | category | flops | bytes accessed | tf_op | source)
XLA Modules:
  0.0 64.1 jit_solution(13078286896006454833)
XLA Ops:
  0.5 2.6 %collective-permute-start = (bf16[128,4096]{1,0:T(8,128)(2,1)}, bf16[128,4096]{1,0:T(8,128)(2,1)S(1)}, u32[]{:S(2)}, u32[]{:S(2)}) collective-permute-start(bf16[128,4096]{1,0:T(8,128)(2,1)} %bitcast.7), channel_id=1, source_target_pairs={{0,2},{1,3},{2,0},{3,1},{4,6},{5,7},{6,4},{7,5},{8,10},{9,11},{10,... | collective-permute-start | bytes 3145736 | tf_op jit(solution)/shard_map/ppermute | solution.py:28
  3.1 0.6 slice.3
  3.7 0.6 %add_convert_fusion = f32[128]{0:T(128)S(1)} fusion(s32[]{:T(128)} %bitcast.5), kind=kLoop, calls=%fused_computation.6 | loop fusion | flops 256 | bytes 516 | tf_op jit(solution)/shard_map/convert_element_type | solution.py:41
  4.8 4.6 %project.3 = (bf16[256,512]{1,0:T(8,128)(2,1)S(1)}, bf16[256,256]{1,0:T(8,128)(2,1)S(1)}, f32[1,4096]{1,0:T(1,128)S(1)}, bf16[4096,128]{1,0:T(8,128)(2,1)S(1)}, ...) custom-call(bf16[128,4096]{1,0:T(8,128)(2,1)} %bitcast.8, ...), custom_call_target="tpu_custom_call" | custom-call | flops 1610612736 | bytes 8388608 | tf_op jit(solution)/shard_map/project/pallas_call | solution.py:155
  9.4 1.6 %collective-permute-start.2 = (bf16[256,256]{1,0:T(8,128)(2,1)S(1)}, bf16[256,256]{1,0:T(8,128)(2,1)S(1)}, u32[]{:S(2)}, u32[]{:S(2)}) collective-permute-start(bf16[256,256]{1,0:T(8,128)(2,1)S(1)} %get-tuple-element.32.refs_1_), channel_id=1, source_target_pairs={{0,8},{8,16},{16,24},{24,28},{28,20},{20,12},{12,4},{4,0},{1,9},{9... | collective-permute-start | bytes 393224 | tf_op jit(solution)/shard_map/ppermute | solution.py:220
  11.5 1.8 %plan.1.plan_ref = s32[33]{0:T(128)S(1)} custom-call(s32[3]{0:T(128)S(1)} %pad_add_fusion.info_ref, s32[4,4,4]{2,1,0:T(4,128)S(1)} %copy-done, s32[4,4,4]{2,1,0:T(4,128)S(1)} %copy-done.1), custom_call_target="tpu_custom_call" | custom-call | tf_op jit(solution)/shard_map/plan/pallas_call | solution.py:264
  13.3 1.7 %collective-permute-done.2.refs_2_ = bf16[256,256]{1,0:T(8,128)(2,1)S(1)} collective-permute-done((bf16[256,256]{1,0:T(8,128)(2,1)S(1)}, bf16[256,256]{1,0:T(8,128)(2,1)S(1)}, u32[]{:S(2)}, u32[]{:S(2)}) %collective-permute-start.2) | collective-permute-done | bytes 131104 | tf_op jit(solution)/shard_map/ppermute | solution.py:220
  15.1 1.6 %collective-permute-start.3 = (bf16[256,256]{1,0:T(8,128)(2,1)S(1)}, bf16[256,256]{1,0:T(8,128)(2,1)S(1)}, u32[]{:S(2)}, u32[]{:S(2)}) collective-permute-start(bf16[256,256]{1,0:T(8,128)(2,1)S(1)} %collective-permute-done.2.refs_2_), channel_id=1, source_target_pairs={{0,8},{8,16},{16,24},{24,28},{28,20},{20,12},{12,4},{4,0},{1,9},{9... | collective-permute-start | bytes 393224 | tf_op jit(solution)/shard_map/ppermute | solution.py:220
  17.1 2.9 %collective-permute-done.3.refs_4_ = bf16[256,256]{1,0:T(8,128)(2,1)S(1)} collective-permute-done((bf16[256,256]{1,0:T(8,128)(2,1)S(1)}, bf16[256,256]{1,0:T(8,128)(2,1)S(1)}, u32[]{:S(2)}, u32[]{:S(2)}) %collective-permute-start.3) | collective-permute-done | bytes 131104 | tf_op jit(solution)/shard_map/ppermute | solution.py:220
  20.0 1.6 %collective-permute-start.4 = (bf16[256,256]{1,0:T(8,128)(2,1)S(1)}, bf16[256,256]{1,0:T(8,128)(2,1)S(1)}, u32[]{:S(2)}, u32[]{:S(2)}) collective-permute-start(bf16[256,256]{1,0:T(8,128)(2,1)S(1)} %collective-permute-done.3.refs_4_), channel_id=1, source_target_pairs={{0,8},{8,16},{16,24},{24,28},{28,20},{20,12},{12,4},{4,0},{1,9},{9... | collective-permute-start | bytes 393224 | tf_op jit(solution)/shard_map/ppermute | solution.py:220
  22.1 5.0 %collective-permute-done.refs_0_ = bf16[128,4096]{1,0:T(8,128)(2,1)S(1)} collective-permute-done((bf16[128,4096]{1,0:T(8,128)(2,1)}, bf16[128,4096]{1,0:T(8,128)(2,1)S(1)}, u32[]{:S(2)}, u32[]{:S(2)}) %collective-permute-start) | collective-permute-done | bytes 1048608 | tf_op jit(solution)/shard_map/ppermute | solution.py:28
  27.1 1.9 %collective-permute-start.9 = (bf16[256,256]{1,0:T(8,128)(2,1)S(1)}, bf16[256,256]{1,0:T(8,128)(2,1)S(1)}, u32[]{:S(2)}, u32[]{:S(2)}) collective-permute-start(bf16[256,256]{1,0:T(8,128)(2,1)S(1)} %collective-permute-done.4.refs_6_), channel_id=1, source_target_pairs={{0,8},{8,16},{16,24},{24,28},{28,20},{20,12},{12,4},{4,0},{1,9},{9... | collective-permute-start | bytes 393224 | tf_op jit(solution)/shard_map/ppermute | solution.py:220
  29.0 1.8 %project.4 = (bf16[128,512]{1,0:T(8,128)(2,1)S(1)}, bf16[128,256]{1,0:T(8,128)(2,1)S(1)}) custom-call(bf16[128,4096]{1,0:T(8,128)(2,1)S(1)} %collective-permute-done.refs_0_, f32[1,4096]{1,0:T(1,128)S(1)} %get-tuple-element.36.refs_1_.refs_2_, bf16[4096,512]{1,0:T(8,128)(2,1)S(1)} %get-tuple-element.37.refs_2_.refs_3_, ...), custom_call_target="tpu_custom_call" | custom-call | flops 805306368 | bytes 7340032 | tf_op jit(solution)/shard_map/project/pallas_call | solution.py:155
  30.8 1.8 %project.5 = (bf16[128,512]{1,0:T(8,128)(2,1)S(1)}, bf16[256,256]{1,0:T(8,128)(2,1)S(1)}) custom-call(bf16[128,4096]{1,0:T(8,128)(2,1)S(1)} %collective-permute-done.8.refs_0_, bf16[128,256]{1,0:T(8,128)(2,1)S(1)} %get-tuple-element.42.refs_1_, f32[1,4096]{1,0:T(1,128)S(1)} %get-tuple-element.36.refs_1_.refs_2_, ...), custom_call_target="tpu_custom_call" | custom-call | flops 805306368 | bytes 7340032 | tf_op jit(solution)/shard_map/project/pallas_call | solution.py:155
  32.6 1.6 %collective-permute-start.11 = (bf16[256,256]{1,0:T(8,128)(2,1)S(1)}, bf16[256,256]{1,0:T(8,128)(2,1)S(1)}, u32[]{:S(2)}, u32[]{:S(2)}) collective-permute-start(bf16[256,256]{1,0:T(8,128)(2,1)S(1)} %get-tuple-element.43.refs_2_), channel_id=1, source_target_pairs={{0,8},{8,16},{16,24},{24,28},{28,20},{20,12},{12,4},{4,0},{1,9},{9... | collective-permute-start | bytes 393224 | tf_op jit(solution)/shard_map/ppermute | solution.py:220
  34.7 2.5 %attend.4 = (bf16[128,512]{1,0:T(8,128)(2,1)S(1)}, bf16[128,512]{1,0:T(8,128)(2,1)S(1)}) custom-call(s32[33]{0:T(128)S(1)} %plan.1.plan_ref, bf16[256,512]{1,0:T(8,128)(2,1)S(1)} %get-tuple-element.44.refs_0_, bf16[256,256]{1,0:T(8,128)(2,1)S(1)} %get-tuple-element.32.refs_1_, bf16[256,256]{1,0:T(8,128)(2,1)S(1)} %collective-permute-done.2.refs_2_, ...), custom_call_target="tpu_custom_call" | custom-call | flops 536870912 | bytes 1572864 | tf_op jit(solution)/shard_map/attend/pallas_call | solution.py:401
  37.2 1.1 %collective-permute-done.11.refs_3_ = bf16[256,256]{1,0:T(8,128)(2,1)S(1)} collective-permute-done((bf16[256,256]{1,0:T(8,128)(2,1)S(1)}, bf16[256,256]{1,0:T(8,128)(2,1)S(1)}, u32[]{:S(2)}, u32[]{:S(2)}) %collective-permute-start.11) | collective-permute-done | bytes 131104 | tf_op jit(solution)/shard_map/ppermute | solution.py:220
  38.2 1.6 %collective-permute-start.12 = (bf16[256,256]{1,0:T(8,128)(2,1)S(1)}, bf16[256,256]{1,0:T(8,128)(2,1)S(1)}, u32[]{:S(2)}, u32[]{:S(2)}) collective-permute-start(bf16[256,256]{1,0:T(8,128)(2,1)S(1)} %collective-permute-done.11.refs_3_), channel_id=1, source_target_pairs={{0,8},{8,16},{16,24},{24,28},{28,20},{20,12},{12,4},{4,0},{1,9},{9... | collective-permute-start | bytes 393224 | tf_op jit(solution)/shard_map/ppermute | solution.py:220
  40.3 2.9 %collective-permute-done.12.refs_5_ = bf16[256,256]{1,0:T(8,128)(2,1)S(1)} collective-permute-done((bf16[256,256]{1,0:T(8,128)(2,1)S(1)}, bf16[256,256]{1,0:T(8,128)(2,1)S(1)}, u32[]{:S(2)}, u32[]{:S(2)}) %collective-permute-start.12) | collective-permute-done | bytes 131104 | tf_op jit(solution)/shard_map/ppermute | solution.py:220
  43.2 1.6 %collective-permute-start.13 = (bf16[256,256]{1,0:T(8,128)(2,1)S(1)}, bf16[256,256]{1,0:T(8,128)(2,1)S(1)}, u32[]{:S(2)}, u32[]{:S(2)}) collective-permute-start(bf16[256,256]{1,0:T(8,128)(2,1)S(1)} %collective-permute-done.12.refs_5_), channel_id=1, source_target_pairs={{0,8},{8,16},{16,24},{24,28},{28,20},{20,12},{12,4},{4,0},{1,9},{9... | collective-permute-start | bytes 393224 | tf_op jit(solution)/shard_map/ppermute | solution.py:220
  45.2 3.0 %collective-permute-done.13.refs_7_ = bf16[256,256]{1,0:T(8,128)(2,1)S(1)} collective-permute-done((bf16[256,256]{1,0:T(8,128)(2,1)S(1)}, bf16[256,256]{1,0:T(8,128)(2,1)S(1)}, u32[]{:S(2)}, u32[]{:S(2)}) %collective-permute-start.13) | collective-permute-done | bytes 131104 | tf_op jit(solution)/shard_map/ppermute | solution.py:220
  48.2 1.6 %collective-permute-start.14 = (bf16[256,256]{1,0:T(8,128)(2,1)S(1)}, bf16[256,256]{1,0:T(8,128)(2,1)S(1)}, u32[]{:S(2)}, u32[]{:S(2)}) collective-permute-start(bf16[256,256]{1,0:T(8,128)(2,1)S(1)} %collective-permute-done.13.refs_7_), channel_id=1, source_target_pairs={{0,8},{8,16},{16,24},{24,28},{28,20},{20,12},{12,4},{4,0},{1,9},{9... | collective-permute-start | bytes 393224 | tf_op jit(solution)/shard_map/ppermute | solution.py:220
  49.8 0.9 %collective-permute-done.17.refs_8_ = bf16[256,256]{1,0:T(8,128)(2,1)S(1)} collective-permute-done((bf16[256,256]{1,0:T(8,128)(2,1)S(1)}, bf16[256,256]{1,0:T(8,128)(2,1)S(1)}, u32[]{:S(2)}, u32[]{:S(2)}) %collective-permute-start.17) | collective-permute-done | bytes 131104 | tf_op jit(solution)/shard_map/ppermute | solution.py:220
  50.7 2.3 %attend.5 = (f32[1,1,512]{2,1,0:T(1,128)S(1)}, f32[1,1,512]{2,1,0:T(1,128)S(1)}, f32[1,128,512]{2,1,0:T(8,128)S(1)}, f32[1,1,512]{2,1,0:T(1,128)S(1)}, f32[1,1,5...) custom-call(s32[33]{0:T(128)S(1)} %plan.1.plan_ref, bf16[128,512]{1,0:T(8,128)(2,1)S(1)} %get-tuple-element.46.refs_0_, ...), custom_call_target="tpu_custom_call" | custom-call | flops 469762048 | bytes 1441792 | tf_op jit(solution)/shard_map/attend/pallas_call | solution.py:401
  53.2 1.0 %attend.7 = bf16[128,512]{1,0:T(8,128)(2,1)S(1)} custom-call(s32[33]{0:T(128)S(1)} %plan.1.plan_ref, bf16[128,512]{1,0:T(8,128)(2,1)S(1)} %get-tuple-element.46.refs_0_, bf16[128,512]{1,0:T(8,128)(2,1)S(1)} %get-tuple-element.47.refs_1_, bf16[256,256]{1,0:T(8,128)(2,1)S(1)} %collective-permute-done.14.refs_2_, f32[1,1,512]{2,1,0:T(1,128)S(1)} %get-tuple-element.53.refs_3_, ...), custom_call_target="tpu_custom_call" | custom-call | flops 33554432 | bytes 393216 | tf_op jit(solution)/shard_map/attend/pallas_call | solution.py:401
  54.2 0.7 %collective-permute-start.19 = (bf16[128,512]{1,0:T(8,128)(2,1)S(1)}, bf16[128,512]{1,0:T(8,128)(2,1)S(1)}, u32[]{:S(2)}, u32[]{:S(2)}) collective-permute-start(bf16[128,512]{1,0:T(8,128)(2,1)S(1)} %attend.7), channel_id=1, source_target_pairs={{0,3},{1,2},{2,1},{3,0},{4,7},{5,6},{6,5},{7,4},{8,11},{9,10},{10,... | collective-permute-start | bytes 393224 | tf_op jit(solution)/shard_map/ppermute | solution.py:28
  54.9 1.0 %attend.6 = bf16[128,512]{1,0:T(8,128)(2,1)S(1)} custom-call(s32[33]{0:T(128)S(1)} %plan.1.plan_ref, bf16[128,512]{1,0:T(8,128)(2,1)S(1)} %get-tuple-element.46.refs_0_, bf16[128,512]{1,0:T(8,128)(2,1)S(1)} %get-tuple-element.47.refs_1_, bf16[256,256]{1,0:T(8,128)(2,1)S(1)} %collective-permute-done.14.refs_2_, f32[1,1,512]{2,1,0:T(1,128)S(1)} %get-tuple-element.50.refs_3_, ...), custom_call_target="tpu_custom_call" | custom-call | flops 33554432 | bytes 393216 | tf_op jit(solution)/shard_map/attend/pallas_call | solution.py:401
  55.9 1.0 %collective-permute-start.18 = (bf16[128,512]{1,0:T(8,128)(2,1)S(1)}, bf16[128,512]{1,0:T(8,128)(2,1)S(1)}, u32[]{:S(2)}, u32[]{:S(2)}) collective-permute-start(bf16[128,512]{1,0:T(8,128)(2,1)S(1)} %attend.6), channel_id=1, source_target_pairs={{0,2},{1,3},{2,0},{3,1},{4,6},{5,7},{6,4},{7,5},{8,10},{9,11},{10,... | collective-permute-start | bytes 393224 | tf_op jit(solution)/shard_map/ppermute | solution.py:28
  56.9 1.3 %deliver.2.refs_2_ = bf16[1,128,2048]{2,1,0:T(8,128)(2,1)} custom-call(s32[3]{0:T(128)S(1)} %pad_add_fusion.info_ref, bf16[128,512]{1,0:T(8,128)(2,1)S(1)} %get-tuple-element.56.refs_0_, bf16[128,512]{1,0:T(8,128)(2,1)S(1)} %collective-permute-done.10.refs_1_), custom_call_target="tpu_custom_call" | custom-call | tf_op jit(solution)/shard_map/deliver/pallas_call | solution.py:433
  58.1 1.9 %collective-permute-done.19.refs_1_ = bf16[128,512]{1,0:T(8,128)(2,1)S(1)} collective-permute-done((bf16[128,512]{1,0:T(8,128)(2,1)S(1)}, bf16[128,512]{1,0:T(8,128)(2,1)S(1)}, u32[]{:S(2)}, u32[]{:S(2)}) %collective-permute-start.19) | collective-permute-done | bytes 131104 | tf_op jit(solution)/shard_map/ppermute | solution.py:28
  60.0 2.9 %collective-permute-done.18.refs_0_ = bf16[128,512]{1,0:T(8,128)(2,1)S(1)} collective-permute-done((bf16[128,512]{1,0:T(8,128)(2,1)S(1)}, bf16[128,512]{1,0:T(8,128)(2,1)S(1)}, u32[]{:S(2)}, u32[]{:S(2)}) %collective-permute-start.18) | collective-permute-done | bytes 131104 | tf_op jit(solution)/shard_map/ppermute | solution.py:28
  62.9 1.3 %deliver.3 = bf16[1,128,2048]{2,1,0:T(8,128)(2,1)} custom-call(s32[3]{0:T(128)S(1)} %pad_add_fusion.info_ref, bf16[128,512]{1,0:T(8,128)(2,1)S(1)} %collective-permute-done.18.refs_0_, bf16[128,512]{1,0:T(8,128)(2,1)S(1)} %collective-permute-done.19.refs_1_, bf16[1,128,2048]{2,1,0:T(8,128)(2,1)} %deliver.2.refs_2_), custom_call_target="tpu_custom_call", output_to_operand_aliasing={{}: (3, {})} | custom-call | tf_op jit(solution)/shard_map/deliver/pallas_call | solution.py:433
  (28 shorter events, 3.9 us)
Async XLA Ops:
  0.1 4.7 %collective-permute-start.1 = (bf16[128,4096]{1,0:T(8,128)(2,1)}, bf16[128,4096]{1,0:T(8,128)(2,1)S(1)}, u32[]{:S(2)}, u32[]{:S(2)}) collective-permute-start(bf16[128,4096]{1,0:T(8,128)(2,1)} %bitcast.6), channel_id=1, source_target_pairs={{0,1},{1,0},{2,3},{3,2},{4,5},{5,4},{6,7},{7,6},{8,9},{9,8},{10,11... | collective-permute-start | bytes 3145736 | tf_op jit(solution)/shard_map/ppermute | solution.py:28
  0.5 26.5 %collective-permute-start = (bf16[128,4096]{1,0:T(8,128)(2,1)}, bf16[128,4096]{1,0:T(8,128)(2,1)S(1)}, u32[]{:S(2)}, u32[]{:S(2)}) collective-permute-start(bf16[128,4096]{1,0:T(8,128)(2,1)} %bitcast.7), channel_id=1, source_target_pairs={{0,2},{1,3},{2,0},{3,1},{4,6},{5,7},{6,4},{7,5},{8,10},{9,11},{10,... | collective-permute-start | bytes 3145736 | tf_op jit(solution)/shard_map/ppermute | solution.py:28
  4.8 6.7 %copy-start = (s32[4,4,4]{2,1,0:T(4,128)S(1)}, s32[4,4,4]{2,1,0:T(4,128)}, u32[]{:S(2)}) copy-start(s32[4,4,4]{2,1,0:T(4,128)} %vertical_ref.1) | copy-start | bytes 772
  4.8 6.7 %copy-start.1 = (s32[4,4,4]{2,1,0:T(4,128)S(1)}, s32[4,4,4]{2,1,0:T(4,128)}, u32[]{:S(2)}) copy-start(s32[4,4,4]{2,1,0:T(4,128)} %slash_ref.1) | copy-start | bytes 772
  9.4 5.6 %collective-permute-start.2 = (bf16[256,256]{1,0:T(8,128)(2,1)S(1)}, bf16[256,256]{1,0:T(8,128)(2,1)S(1)}, u32[]{:S(2)}, u32[]{:S(2)}) collective-permute-start(bf16[256,256]{1,0:T(8,128)(2,1)S(1)} %get-tuple-element.32.refs_1_), channel_id=1, source_target_pairs={{0,8},{8,16},{16,24},{24,28},{28,20},{20,12},{12,4},{4,0},{1,9},{9... | collective-permute-start | bytes 393224 | tf_op jit(solution)/shard_map/ppermute | solution.py:220
  11.1 5.6 %collective-permute-start.5 = (bf16[256,256]{1,0:T(8,128)(2,1)S(1)}, bf16[256,256]{1,0:T(8,128)(2,1)S(1)}, u32[]{:S(2)}, u32[]{:S(2)}) collective-permute-start(bf16[256,256]{1,0:T(8,128)(2,1)S(1)} %get-tuple-element.32.refs_1_), channel_id=1, source_target_pairs={{0,4},{8,0},{16,8},{24,16},{28,24},{20,28},{12,20},{4,12},{1,5},{9... | collective-permute-start | bytes 393224 | tf_op jit(solution)/shard_map/ppermute | solution.py:220
  15.1 5.0 %collective-permute-start.3 = (bf16[256,256]{1,0:T(8,128)(2,1)S(1)}, bf16[256,256]{1,0:T(8,128)(2,1)S(1)}, u32[]{:S(2)}, u32[]{:S(2)}) collective-permute-start(bf16[256,256]{1,0:T(8,128)(2,1)S(1)} %collective-permute-done.2.refs_2_), channel_id=1, source_target_pairs={{0,8},{8,16},{16,24},{24,28},{28,20},{20,12},{12,4},{4,0},{1,9},{9... | collective-permute-start | bytes 393224 | tf_op jit(solution)/shard_map/ppermute | solution.py:220
  16.6 5.0 %collective-permute-start.6 = (bf16[256,256]{1,0:T(8,128)(2,1)S(1)}, bf16[256,256]{1,0:T(8,128)(2,1)S(1)}, u32[]{:S(2)}, u32[]{:S(2)}) collective-permute-start(bf16[256,256]{1,0:T(8,128)(2,1)S(1)} %collective-permute-done.5.refs_3_), channel_id=1, source_target_pairs={{0,4},{8,0},{16,8},{24,16},{28,24},{20,28},{12,20},{4,12},{1,5},{9... | collective-permute-start | bytes 393224 | tf_op jit(solution)/shard_map/ppermute | solution.py:220
  20.0 7.0 %collective-permute-start.4 = (bf16[256,256]{1,0:T(8,128)(2,1)S(1)}, bf16[256,256]{1,0:T(8,128)(2,1)S(1)}, u32[]{:S(2)}, u32[]{:S(2)}) collective-permute-start(bf16[256,256]{1,0:T(8,128)(2,1)S(1)} %collective-permute-done.3.refs_4_), channel_id=1, source_target_pairs={{0,8},{8,16},{16,24},{24,28},{28,20},{20,12},{12,4},{4,0},{1,9},{9... | collective-permute-start | bytes 393224 | tf_op jit(solution)/shard_map/ppermute | solution.py:220
  21.6 5.5 %collective-permute-start.7 = (bf16[256,256]{1,0:T(8,128)(2,1)S(1)}, bf16[256,256]{1,0:T(8,128)(2,1)S(1)}, u32[]{:S(2)}, u32[]{:S(2)}) collective-permute-start(bf16[256,256]{1,0:T(8,128)(2,1)S(1)} %collective-permute-done.6.refs_5_), channel_id=1, source_target_pairs={{0,4},{8,0},{16,8},{24,16},{28,24},{20,28},{12,20},{4,12},{1,5},{9... | collective-permute-start | bytes 393224 | tf_op jit(solution)/shard_map/ppermute | solution.py:220
  27.1 3.7 %collective-permute-start.8 = (bf16[128,4096]{1,0:T(8,128)(2,1)S(1)}, bf16[128,4096]{1,0:T(8,128)(2,1)S(1)}, u32[]{:S(2)}, u32[]{:S(2)}) collective-permute-start(bf16[128,4096]{1,0:T(8,128)(2,1)S(1)} %collective-permute-done.refs_0_), channel_id=1, source_target_pairs={{0,1},{1,0},{2,3},{3,2},{4,5},{5,4},{6,7},{7,6},{8,9},{9,8},{10,11... | collective-permute-start | bytes 3145736 | tf_op jit(solution)/shard_map/ppermute | solution.py:28
  27.1 7.6 %collective-permute-start.9 = (bf16[256,256]{1,0:T(8,128)(2,1)S(1)}, bf16[256,256]{1,0:T(8,128)(2,1)S(1)}, u32[]{:S(2)}, u32[]{:S(2)}) collective-permute-start(bf16[256,256]{1,0:T(8,128)(2,1)S(1)} %collective-permute-done.4.refs_6_), channel_id=1, source_target_pairs={{0,8},{8,16},{16,24},{24,28},{28,20},{20,12},{12,4},{4,0},{1,9},{9... | collective-permute-start | bytes 393224 | tf_op jit(solution)/shard_map/ppermute | solution.py:220
  32.6 5.6 %collective-permute-start.11 = (bf16[256,256]{1,0:T(8,128)(2,1)S(1)}, bf16[256,256]{1,0:T(8,128)(2,1)S(1)}, u32[]{:S(2)}, u32[]{:S(2)}) collective-permute-start(bf16[256,256]{1,0:T(8,128)(2,1)S(1)} %get-tuple-element.43.refs_2_), channel_id=1, source_target_pairs={{0,8},{8,16},{16,24},{24,28},{28,20},{20,12},{12,4},{4,0},{1,9},{9... | collective-permute-start | bytes 393224 | tf_op jit(solution)/shard_map/ppermute | solution.py:220
  34.2 5.6 %collective-permute-start.15 = (bf16[256,256]{1,0:T(8,128)(2,1)S(1)}, bf16[256,256]{1,0:T(8,128)(2,1)S(1)}, u32[]{:S(2)}, u32[]{:S(2)}) collective-permute-start(bf16[256,256]{1,0:T(8,128)(2,1)S(1)} %get-tuple-element.43.refs_2_), channel_id=1, source_target_pairs={{0,4},{8,0},{16,8},{24,16},{28,24},{20,28},{12,20},{4,12},{1,5},{9... | collective-permute-start | bytes 393224 | tf_op jit(solution)/shard_map/ppermute | solution.py:220
  38.2 5.0 %collective-permute-start.12 = (bf16[256,256]{1,0:T(8,128)(2,1)S(1)}, bf16[256,256]{1,0:T(8,128)(2,1)S(1)}, u32[]{:S(2)}, u32[]{:S(2)}) collective-permute-start(bf16[256,256]{1,0:T(8,128)(2,1)S(1)} %collective-permute-done.11.refs_3_), channel_id=1, source_target_pairs={{0,8},{8,16},{16,24},{24,28},{28,20},{20,12},{12,4},{4,0},{1,9},{9... | collective-permute-start | bytes 393224 | tf_op jit(solution)/shard_map/ppermute | solution.py:220
  39.8 5.0 %collective-permute-start.16 = (bf16[256,256]{1,0:T(8,128)(2,1)S(1)}, bf16[256,256]{1,0:T(8,128)(2,1)S(1)}, u32[]{:S(2)}, u32[]{:S(2)}) collective-permute-start(bf16[256,256]{1,0:T(8,128)(2,1)S(1)} %collective-permute-done.15.refs_4_), channel_id=1, source_target_pairs={{0,4},{8,0},{16,8},{24,16},{28,24},{20,28},{12,20},{4,12},{1,5},{9... | collective-permute-start | bytes 393224 | tf_op jit(solution)/shard_map/ppermute | solution.py:220
  43.2 5.0 %collective-permute-start.13 = (bf16[256,256]{1,0:T(8,128)(2,1)S(1)}, bf16[256,256]{1,0:T(8,128)(2,1)S(1)}, u32[]{:S(2)}, u32[]{:S(2)}) collective-permute-start(bf16[256,256]{1,0:T(8,128)(2,1)S(1)} %collective-permute-done.12.refs_5_), channel_id=1, source_target_pairs={{0,8},{8,16},{16,24},{24,28},{28,20},{20,12},{12,4},{4,0},{1,9},{9... | collective-permute-start | bytes 393224 | tf_op jit(solution)/shard_map/ppermute | solution.py:220
  44.8 5.0 %collective-permute-start.10 = (bf16[128,512]{1,0:T(8,128)(2,1)S(1)}, bf16[128,512]{1,0:T(8,128)(2,1)S(1)}, u32[]{:S(2)}, u32[]{:S(2)}) collective-permute-start(bf16[128,512]{1,0:T(8,128)(2,1)S(1)} %get-tuple-element.45), channel_id=1, source_target_pairs={{0,1},{1,0},{2,3},{3,2},{4,5},{5,4},{6,7},{7,6},{8,9},{9,8},{10,11... | collective-permute-start | bytes 393224 | tf_op jit(solution)/shard_map/ppermute | solution.py:28
  44.8 5.9 %collective-permute-start.17 = (bf16[256,256]{1,0:T(8,128)(2,1)S(1)}, bf16[256,256]{1,0:T(8,128)(2,1)S(1)}, u32[]{:S(2)}, u32[]{:S(2)}) collective-permute-start(bf16[256,256]{1,0:T(8,128)(2,1)S(1)} %collective-permute-done.16.refs_6_), channel_id=1, source_target_pairs={{0,4},{8,0},{16,8},{24,16},{28,24},{20,28},{12,20},{4,12},{1,5},{9... | collective-permute-start | bytes 393224 | tf_op jit(solution)/shard_map/ppermute | solution.py:220
  48.2 5.0 %collective-permute-start.14 = (bf16[256,256]{1,0:T(8,128)(2,1)S(1)}, bf16[256,256]{1,0:T(8,128)(2,1)S(1)}, u32[]{:S(2)}, u32[]{:S(2)}) collective-permute-start(bf16[256,256]{1,0:T(8,128)(2,1)S(1)} %collective-permute-done.13.refs_7_), channel_id=1, source_target_pairs={{0,8},{8,16},{16,24},{24,28},{28,20},{20,12},{12,4},{4,0},{1,9},{9... | collective-permute-start | bytes 393224 | tf_op jit(solution)/shard_map/ppermute | solution.py:220
  54.2 5.8 %collective-permute-start.19 = (bf16[128,512]{1,0:T(8,128)(2,1)S(1)}, bf16[128,512]{1,0:T(8,128)(2,1)S(1)}, u32[]{:S(2)}, u32[]{:S(2)}) collective-permute-start(bf16[128,512]{1,0:T(8,128)(2,1)S(1)} %attend.7), channel_id=1, source_target_pairs={{0,3},{1,2},{2,1},{3,0},{4,7},{5,6},{6,5},{7,4},{8,11},{9,10},{10,... | collective-permute-start | bytes 393224 | tf_op jit(solution)/shard_map/ppermute | solution.py:28
  55.9 7.0 %collective-permute-start.18 = (bf16[128,512]{1,0:T(8,128)(2,1)S(1)}, bf16[128,512]{1,0:T(8,128)(2,1)S(1)}, u32[]{:S(2)}, u32[]{:S(2)}) collective-permute-start(bf16[128,512]{1,0:T(8,128)(2,1)S(1)} %attend.6), channel_id=1, source_target_pairs={{0,2},{1,3},{2,0},{3,1},{4,6},{5,7},{6,4},{7,5},{8,10},{9,11},{10,... | collective-permute-start | bytes 393224 | tf_op jit(solution)/shard_map/ppermute | solution.py:28

commit v3 on v2

--- a/solution.py
+++ b/solution.py
@@ -42,130 +42,177 @@
     return (jnp.cos(angles), jnp.sin(angles))
 
 
-def project_kernel(pieces, early, before, *refs):
-    token_refs, refs = list(refs[:pieces]), list(refs[pieces:])
-    ahead = 0
-    if before:
-        before_ref, refs = refs[0], refs[1:]
-        ahead = before_ref.shape[0]
-    gain_ref, wq_ref, wk_ref, wv_ref, table_ref, q_ref, kv_ref = refs[:7]
-    refs = refs[7:]
-    if before:
-        kv_ref[:ahead, :] = before_ref[...]
-    copies = []
-    if early:
-        sources = (gain_ref, token_refs[0], wk_ref, wv_ref, wq_ref)
-        held, refs = refs[:1] + refs[5:6] + refs[1:4], refs[4:5] + refs[6:]
-        sems = refs[1]
-        gain_ref, token_refs[0], wk_ref, wv_ref, wq_ref = held
-        for at, (source, target) in enumerate(zip(sources, held)):
-            copies.append(pltpu.make_async_copy(source, target, sems.at[at]))
-            copies[-1].start()
-        copies[0].wait()
-    normed = refs[0]
-    width = gain_ref.shape[1]
-    heads = wk_ref.shape[1] // HEAD_WIDTH
+def normalize(token_ref, gain_ref, normed_ref, first):
+    def norm_band(index, carry):
+        at = pl.ds(pl.multiple_of(index * BAND, BAND), BAND)
+        wide = token_ref[at, :].astype(jnp.float32)
+        scale = lax.rsqrt(jnp.mean(wide * wide, axis=-1, keepdims=True) + EPSILON)
+        normed_ref[pl.ds(pl.multiple_of(first + index * BAND, BAND), BAND), :] = (
+            wide * scale * gain_ref[...]
+        ).astype(jnp.bfloat16)
+        return carry
+
+    lax.fori_loop(0, token_ref.shape[0] // BAND, norm_band, 0, unroll=2)
+
+
+def rotate(value, table_ref):
+    half = HEAD_WIDTH // 2
+    turned = jnp.concatenate([value[:, half:], value[:, :half]], axis=1)
+    return (value * table_ref[:, :HEAD_WIDTH] + turned * table_ref[:, HEAD_WIDTH:]).astype(
+        jnp.bfloat16
+    )
+
+
+def multiply(normed_ref, weight_of):
+    width = normed_ref.shape[1]
     deep = min(1024, width)
-
-    rows = token_refs[0].shape[0]
-    for piece in reversed(range(pieces)):
-        if piece == 0 and early:
-            copies[1].wait()
-        ref, first = token_refs[piece], piece * rows
-
-        def norm_band(index, carry, ref=ref, first=first):
-            at = pl.ds(pl.multiple_of(index * BAND, BAND), BAND)
-            wide = ref[at, :].astype(jnp.float32)
-            scale = lax.rsqrt(jnp.mean(wide * wide, axis=-1, keepdims=True) + EPSILON)
-            normed[pl.ds(pl.multiple_of(first + index * BAND, BAND), BAND), :] = (
-                wide * scale * gain_ref[...]
-            ).astype(jnp.bfloat16)
-            return carry
-
-        lax.fori_loop(0, rows // BAND, norm_band, 0, unroll=2)
-
-    half = HEAD_WIDTH // 2
-
-    def rotate(value):
-        turned = jnp.concatenate([value[:, half:], value[:, :half]], axis=1)
-        return (
-            value * table_ref[:, :HEAD_WIDTH] + turned * table_ref[:, HEAD_WIDTH:]
-        ).astype(jnp.bfloat16)
-
-    def multiply(weight_of):
-        total = None
-        for start in range(0, width, deep):
-            part = jnp.dot(
-                normed[:, start:start + deep],
-                weight_of(slice(start, start + deep)),
-                preferred_element_type=jnp.float32,
-            )
-            total = part if total is None else total + part
-        return total
-
-    if early:
-        copies[2].wait()
-        copies[3].wait()
-    for head in range(heads):
+    total = None
+    for start in range(0, width, deep):
+        part = jnp.dot(
+            normed_ref[:, start:start + deep],
+            weight_of(slice(start, start + deep)),
+            preferred_element_type=jnp.float32,
+        )
+        total = part if total is None else total + part
+    return total
+
+
+def write_keys_values(normed_ref, wk_ref, wv_ref, table_ref, kv_ref, ahead):
+    rows = table_ref.shape[0]
+    for head in range(wk_ref.shape[1] // HEAD_WIDTH):
         at = slice(head * HEAD_WIDTH, (head + 1) * HEAD_WIDTH)
-        both = multiply(lambda k: jnp.concatenate([wk_ref[k, at], wv_ref[k, at]], axis=1))
+        both = multiply(
+            normed_ref, lambda k: jnp.concatenate([wk_ref[k, at], wv_ref[k, at]], axis=1)
+        )
         out = 2 * head * HEAD_WIDTH
-        for piece in range(pieces):
-            mine = both[piece * rows:(piece + 1) * rows]
-            band = slice(ahead + piece * rows, ahead + (piece + 1) * rows)
-            kv_ref[band, out:out + HEAD_WIDTH] = rotate(mine[:, :HEAD_WIDTH])
+        for first in range(0, normed_ref.shape[0], rows):
+            mine = both[first:first + rows]
+            band = slice(ahead + first, ahead + first + rows)
+            kv_ref[band, out:out + HEAD_WIDTH] = rotate(mine[:, :HEAD_WIDTH], table_ref)
             kv_ref[band, out + HEAD_WIDTH:out + 2 * HEAD_WIDTH] = mine[:, HEAD_WIDTH:].astype(
                 jnp.bfloat16
             )
-    if early:
-        copies[4].wait()
-    pair = 2 * HEAD_WIDTH
+
+
+def write_queries(normed_ref, wq_ref, table_ref, q_ref, ahead):
+    rows, pair = table_ref.shape[0], 2 * HEAD_WIDTH
     for start in range(0, wq_ref.shape[1], pair):
-        both = multiply(lambda k: wq_ref[k, start:start + pair])
-        for piece in range(pieces):
-            band = slice(piece * rows, (piece + 1) * rows)
+        both = multiply(normed_ref, lambda k: wq_ref[k, start:start + pair])
+        for first in range(0, normed_ref.shape[0], rows):
+            band = slice(ahead + first, ahead + first + rows)
             for at in (0, HEAD_WIDTH):
                 q_ref[band, start + at:start + at + HEAD_WIDTH] = rotate(
-                    both[band, at:at + HEAD_WIDTH]
+                    both[first:first + rows, at:at + HEAD_WIDTH], table_ref
                 )
 
 
-def project(pieces, gain, w_query, key_weight, value_weight, table, early=False, before=None):
-    width = gain.shape[1]
-    q_cols, k_cols = w_query.shape[1], key_weight.shape[1]
-    total = len(pieces) * pieces[0].shape[0]
-    params = (gain, w_query, key_weight, value_weight)
-    held = () if before is None else (before,)
-    scratch = [pltpu.VMEM((total, width), jnp.bfloat16)]
-    kind = [VMEM] * (len(pieces) + len(held) + len(params))
-    shapes = [
-        jax.ShapeDtypeStruct((total, q_cols), jnp.bfloat16),
-        jax.ShapeDtypeStruct((total + sum(a.shape[0] for a in held), 2 * k_cols), jnp.bfloat16),
-    ]
-    if early:
-        scratch.append(pltpu.VMEM(pieces[0].shape, pieces[0].dtype))
-        scratch.append(pltpu.SemaphoreType.DMA((5,)))
-        params = tuple(in_hbm(array) for array in params)
-        shapes += [
-            jax.ShapeDtypeStruct(array.shape, array.dtype)
-            for array in (gain, key_weight, value_weight, w_query)
-        ]
-        pieces = [in_hbm(pieces[0])] + list(pieces[1:])
-        kind = [HBM] + [VMEM] * (len(pieces) - 1) + [HBM] * len(params)
+def near_kernel(
+    own_hbm, twin_ref, gain_hbm, wq_hbm, wk_hbm, wv_hbm, table_ref,
+    q_ref, kv_ref, gain_ref, wq_ref, wk_ref, wv_ref, own_ref, normed_ref, sems,
+):
+    copies = []
+    for source, target in (
+        (gain_hbm, gain_ref), (own_hbm, own_ref), (wk_hbm, wk_ref), (wv_hbm, wv_ref), (wq_hbm, wq_ref)
+    ):
+        copies.append(pltpu.make_async_copy(source, target, sems.at[len(copies)]))
+        copies[-1].start()
+    copies[0].wait()
+    normalize(twin_ref, gain_ref, normed_ref, own_ref.shape[0])
+    copies[1].wait()
+    normalize(own_ref, gain_ref, normed_ref, 0)
+    copies[2].wait()
+    copies[3].wait()
+    write_keys_values(normed_ref, wk_ref, wv_ref, table_ref, kv_ref, 0)
+    copies[4].wait()
+    write_queries(normed_ref, wq_ref, table_ref, q_ref, 0)
+
+
+def keys_values_kernel(before, token_ref, gain_ref, wk_ref, wv_ref, table_ref, *refs):
+    kv_ref, normed_ref = refs[-2:]
+    ahead = 0
+    if before:
+        ahead = refs[0].shape[0]
+        kv_ref[:ahead, :] = refs[0][...]
+    normalize(token_ref, gain_ref, normed_ref, 0)
+    write_keys_values(normed_ref, wk_ref, wv_ref, table_ref, kv_ref, ahead)
+
+
+def queries_kernel(pieces, wq_ref, table_ref, *refs):
+    for at, normed_ref in enumerate(refs[:pieces]):
+        write_queries(normed_ref, wq_ref, table_ref, refs[pieces], at * normed_ref.shape[0])
+
+
+def project_call(kernel, name, operands, kinds, shapes, scratch, rows, columns):
+    width = max(array.shape[0] for array in operands)
     return pl.pallas_call(
-        functools.partial(project_kernel, len(pieces), early, before is not None),
-        in_specs=kind + [VMEM],
+        kernel,
+        in_specs=kinds,
         out_specs=[VMEM] * len(shapes),
-        out_shape=shapes,
+        out_shape=[jax.ShapeDtypeStruct(shape, dtype) for shape, dtype in shapes],
         scratch_shapes=scratch,
         compiler_params=pltpu.CompilerParams(vmem_limit_bytes=20 * MIB),
         cost_estimate=pl.CostEstimate(
-            flops=2 * total * width * (q_cols + 2 * k_cols),
-            bytes_accessed=2 * width * (q_cols + 2 * k_cols) + 2 * total * width,
+            flops=2 * rows * width * columns,
+            bytes_accessed=2 * width * (columns + rows),
             transcendentals=0,
         ),
-        name="project",
-    )(*pieces, *held, *params, table)
+        name=name,
+    )(*operands)
+
+
+def project_near(own, twin, gain, w_query, key_weight, value_weight, table):
+    rows, width = own.shape
+    q_cols, k_cols = w_query.shape[1], key_weight.shape[1]
+    params = (gain, w_query, key_weight, value_weight)
+    shapes = [((2 * rows, q_cols), jnp.bfloat16), ((2 * rows, 2 * k_cols), jnp.bfloat16)]
+    shapes += [(array.shape, array.dtype) for array in params]
+    return project_call(
+        near_kernel,
+        "project_near",
+        (in_hbm(own), twin, *(in_hbm(array) for array in params), table),
+        [HBM, VMEM] + [HBM] * 4 + [VMEM],
+        shapes,
+        [
+            pltpu.VMEM(own.shape, own.dtype),
+            pltpu.VMEM((2 * rows, width), jnp.bfloat16),
+            pltpu.SemaphoreType.DMA((5,)),
+        ],
+        2 * rows,
+        q_cols + 2 * k_cols,
+    )
+
+
+def project_keys_values(tokens, gain, key_weight, value_weight, table, before=None):
+    held = () if before is None else (before,)
+    rows, cols = tokens.shape[0], 2 * key_weight.shape[1]
+    total = rows + sum(array.shape[0] for array in held)
+    operands = (tokens, gain, key_weight, value_weight, table, *held)
+    return project_call(
+        functools.partial(keys_values_kernel, len(held)),
+        "project_keys_values",
+        operands,
+        [VMEM] * len(operands),
+        [((total, cols), jnp.bfloat16), (tokens.shape, jnp.bfloat16)],
+        [],
+        rows,
+        cols,
+    )
+
+
+def project_queries(normed, w_query, table):
+    operands = (w_query, table, *normed)
+    rows = sum(array.shape[0] for array in normed)
+    (queries,) = project_call(
+        functools.partial(queries_kernel, len(normed)),
+        "project_queries",
+        operands,
+        [VMEM] * len(operands),
+        [((rows, w_query.shape[1]), jnp.bfloat16)],
+        [],
+        rows,
+        w_query.shape[1],
+    )
+    return queries
 
 
 def ring_order(count):
@@ -206,6 +253,10 @@
     def hold(self, array):
         self.slots.append(lambda index, r=len(self.arrays): (r, 0))
         self.arrays.append(array)
+
+    def last(self, array):
+        pairs = [(s, self.order[(at + 1) % self.count]) for at, s in enumerate(self.order)]
+        return lax.ppermute(array, "seq", pairs)
 
     def advance(self, *others):
         if self.stage >= self.count // 2:
@@ -370,13 +421,9 @@
                 out_refs[lane][:, cols] = result[:, h * rows:(h + 1) * rows].T.astype(jnp.bfloat16)
 
 
-def attend(table, lanes, queries, spread, span=None, states=None, end=True):
-    first, last = span or (0, len(spread.slots))
+def attend(table, lanes, queries, arrays, slots, chunks=1, first=0, states=None, end=True):
     q_cols = queries[0].shape[1]
     rows = lanes[0][3]
-    arrays, slots = spread.arrays, spread.slots[first:last]
-    if span:
-        arrays, slots = arrays[first:last], spread.slots[:last - first]
     held = [array for state in states for array in state] if states else []
     if end:
         shapes = [jax.ShapeDtypeStruct((rows, q_cols), jnp.bfloat16)] * len(lanes)
@@ -392,7 +439,7 @@
         lax.axis_size("seq"),
         first,
         slots,
-        spread.chunks,
+        chunks,
         len(queries),
         len(arrays),
         not states,
@@ -407,9 +454,9 @@
             vmem_limit_bytes=10 * MIB + 4 * sum(a.size for a in (*queries, *arrays))
         ),
         cost_estimate=pl.CostEstimate(
-            flops=4 * len(lanes) * rows * q_cols * len(slots) * spread.chunks * rows,
+            flops=4 * len(lanes) * rows * q_cols * len(slots) * chunks * rows,
             bytes_accessed=2 * sum(a.size for a in arrays) + 4 * len(lanes) * rows * q_cols,
-            transcendentals=len(lanes) * rows * len(slots) * spread.chunks * rows * QUERY_GROUP,
+            transcendentals=len(lanes) * rows * len(slots) * chunks * rows * QUERY_GROUP,
         ),
         name="attend",
     )(table, *queries, *arrays, *held)
@@ -458,50 +505,58 @@
 
     twin = swap(own, "doc", 1)
     across = swap(own, "doc", 2)
-    q_near, kv_near, gain_in, wk_in, wv_in, wq_in = project(
-        [own, twin], gain, w_query, key_weight, value_weight, table, early=True
-    )
-    params = (gain_in, wq_in, wk_in, wv_in, table)
+    q_near, kv_near, gain_in, wq_in, wk_in, wv_in = project_near(
+        own, twin, gain, w_query, key_weight, value_weight, table
+    )
     near = ring(kv_near)
     near.advance()
     near.advance(table_of)
     near.advance()
 
     across = after(across, *near.latest)
-    near.advance()
     crossed = swap(across, "doc", 1)
-    q_across, kv_across = project([across], *params)
-    q_crossed, kv_far = project([crossed], *params, before=kv_across)
+    kv_across, across_in = project_keys_values(across, gain_in, wk_in, wv_in, table)
+    kv_far, crossed_in = project_keys_values(crossed, gain_in, wk_in, wv_in, table, before=kv_across)
     far = ring(kv_far)
     far.advance()
+    near.advance(kv_far)
+    q_far = project_queries([across_in, after(crossed_in, kv_far)], wq_in, table)
     mixed_own, mixed_twin = attend(
         table_of,
         [(0, (0, 0), 0, rows), (1, (0, rows), rows, rows)],
-        [after(q_near, kv_far)],
-        near,
+        [after(q_near, *far.latest)],
+        near.arrays,
+        near.slots,
+        near.chunks,
     )
     out_twin = swap(mixed_twin, "doc", 1)
+    far.advance(q_far)
     far.advance(mixed_twin)
-    far.advance()
-    remote = [(2, (0, 0), 0, rows), (3, (1, 0), rows, rows)]
-    queries = [after(q_across, out_twin), q_crossed]
-    home = []
+    q_far = after(q_far, out_twin)
+    remote = [(2, (0, 0), 0, rows), (3, (0, rows), rows, rows)]
     if long:
-        for at, mixed in enumerate(attend(table_of, remote, queries, far)):
-            home.append(swap(mixed, "doc", 2 + at))
+        mixed = attend(table_of, remote, [q_far], far.arrays, far.slots, far.chunks)
+        home = [swap(value, "doc", 2 + at) for at, value in enumerate(mixed)]
     else:
-        far.advance()
-        last = len(far.slots) - 1
-        states = attend(table_of, remote, queries, far, span=(0, last), end=False)
-        for at, lane in enumerate(remote):
-            state = states[3 * at:3 * at + 3]
-            (mixed,) = attend(
-                table_of, [lane], queries, far, span=(last, last + 1), states=[state]
-            )
-            home.append(swap(mixed, "doc", 2 + at))
+        ends = [far.last(far.front[1][at * rows:(at + 1) * rows]) for at in range(2)]
+        count = len(far.slots)
+        state = attend(table_of, remote[:1], [q_far], far.arrays, far.slots, end=False)
+        (mixed,) = attend(
+            table_of, remote[:1], [q_far], ends[:1], [lambda index: (0, 0)], first=count, states=[state]
+        )
+        home = [swap(mixed, "doc", 2)]
+        (mixed,) = attend(
+            table_of,
+            remote[1:],
+            [q_far],
+            [*far.arrays, ends[1]],
+            [*far.slots, lambda index: (count, -rows)],
+        )
+        home.append(swap(mixed, "doc", 3))
     count = lax.axis_size("doc")
     result = deliver(info, (0, 1), [mixed_own, out_twin], count)
-    return deliver(info, (2, 3), home, count, before=result)
+    result = deliver(info, (2,), home[:1], count, before=result)
+    return deliver(info, (3,), home[1:], count, before=result)
 
 
 def solution(mesh):

time: 64.3 us -> 63.2 us (0.983)
  waiting for transfers between devices: 22.5 us -> 18.3 us
  starting transfers between devices: 20.4 us -> 22.3 us
  Pallas kernels: 19.3 us -> 20.5 us
    ppermute x0 -> x2, starting transfers between devices: none -> 3.48 us  [last(): return lax.ppermute(array, 'seq', pairs)]
    ppermute x14 -> x13, waiting for transfers between devices: 12.8 us -> 9.47 us  [advance(): self.front[way] = lax.ppermute(value, 'seq', pairs)]
    ppermute x14 -> x13, starting transfers between devices: 15.7 us -> 14.2 us  [advance(): self.front[way] = lax.ppermute(value, 'seq', pairs)]
    pallas_call x2 -> x3, Pallas kernels: 2.52 us -> 3.68 us  [deliver(): pl.pallas_call(functools.partial(deliver_kernel, masks), in_specs=[SMEM]...]
    ppermute x6, waiting for transfers between devices: 9.76 us -> 8.83 us  [swap(): lax.ppermute(value, axis, [(source, source ^ mask) for source in range(co...]
    pallas_call x3 -> x4, Pallas kernels: 8.21 us -> 8.42 us  [project_call(): pl.pallas_call(kernel, in_specs=kinds, out_specs=[VMEM] * len(shapes), ou...]
  transfers between devices with their start and end apart: 20 -> 21, of which waited for: 10 -> 9; matrix products, arithmetic and copies ran while one was open for 3% -> 3% of each run, Pallas kernels for 27% -> 29%
where the time goes in v3:
time: 63.2 us; the launch traced here: 63 us
  starting transfers between devices  22.3 us (35%)
  Pallas kernels  20.5 us (32%)
  waiting for transfers between devices  18.3 us (29%)
  other arithmetic  1.16 us (2%)
    ppermute x13, starting transfers between devices, advance(): self.front[way] = lax.ppermute(value, 'seq', pairs)  14.2 us
    ppermute x13, waiting for transfers between devices, advance(): self.front[way] = lax.ppermute(value, 'seq', pairs)  9.47 us
    ppermute x6, waiting for transfers between devices, swap(): lax.ppermute(value, axis, [(source, source ^ mask) for source in range(co...  8.83 us
    pallas_call x4, Pallas kernels, project_call(): pl.pallas_call(kernel, in_specs=kinds, out_specs=[VMEM] * len(shapes), ou...  8.42 us
    pallas_call x4, Pallas kernels, attend(): pl.pallas_call(kernel, in_specs=[SMEM] + [VMEM] * (len(queries) + len(arr...  6.58 us
    ppermute x6, starting transfers between devices, swap(): lax.ppermute(value, axis, [(source, source ^ mask) for source in range(co...  4.64 us
    pallas_call x3, Pallas kernels, deliver(): pl.pallas_call(functools.partial(deliver_kernel, masks), in_specs=[SMEM]...  3.68 us
    ppermute x2, starting transfers between devices, last(): return lax.ppermute(array, 'seq', pairs)  3.48 us
  transfers between devices with their start and end apart: 21, of which 9 were waited for; matrix products, arithmetic and copies ran while one was open for 3% of the time, Pallas kernels for 29%

profile of v3, /device:TPU:0, one launch (start us, length us, event | category | flops | bytes accessed | tf_op | source)
XLA Modules:
  0.0 63.0 jit_solution(9342692591206819891)
XLA Ops:
  0.5 2.6 %collective-permute-start.1 = (bf16[128,4096]{1,0:T(8,128)(2,1)}, bf16[128,4096]{1,0:T(8,128)(2,1)S(1)}, u32[]{:S(2)}, u32[]{:S(2)}) collective-permute-start(bf16[128,4096]{1,0:T(8,128)(2,1)} %bitcast.7), channel_id=1, source_target_pairs={{0,2},{1,3},{2,0},{3,1},{4,6},{5,7},{6,4},{7,5},{8,10},{9,11},{10,... | collective-permute-start | bytes 3145736 | tf_op jit(solution)/shard_map/ppermute | solution.py:28
  3.7 0.6 %add_convert_fusion = f32[128]{0:T(128)S(1)} fusion(s32[]{:T(128)} %bitcast.5), kind=kLoop, calls=%fused_computation.6 | loop fusion | flops 256 | bytes 516 | tf_op jit(solution)/shard_map/convert_element_type | solution.py:41
  4.8 4.6 %project_near.1 = (bf16[256,512]{1,0:T(8,128)(2,1)S(1)}, bf16[256,256]{1,0:T(8,128)(2,1)S(1)}, f32[1,4096]{1,0:T(1,128)S(1)}, bf16[4096,512]{1,0:T(8,128)(2,1)S(...) custom-call(bf16[128,4096]{1,0:T(8,128)(2,1)} %bitcast.8, ...), custom_call_target="tpu_custom_call" | custom-call | flops 1610612736 | bytes 8388608 | tf_op jit(solution)/shard_map/project_near/pallas_call | solution.py:147
  9.4 1.6 %collective-permute-start.5 = (bf16[256,256]{1,0:T(8,128)(2,1)S(1)}, bf16[256,256]{1,0:T(8,128)(2,1)S(1)}, u32[]{:S(2)}, u32[]{:S(2)}) collective-permute-start(bf16[256,256]{1,0:T(8,128)(2,1)S(1)} %get-tuple-element.34.refs_1_), channel_id=1, source_target_pairs={{0,4},{8,0},{16,8},{24,16},{28,24},{20,28},{12,20},{4,12},{1,5},{9... | collective-permute-start | bytes 393224 | tf_op jit(solution)/shard_map/ppermute | solution.py:271
  11.5 1.8 %plan.1.plan_ref = s32[33]{0:T(128)S(1)} custom-call(s32[3]{0:T(128)S(1)} %pad_add_fusion.info_ref, s32[4,4,4]{2,1,0:T(4,128)S(1)} %copy-done, s32[4,4,4]{2,1,0:T(4,128)S(1)} %copy-done.1), custom_call_target="tpu_custom_call" | custom-call | tf_op jit(solution)/shard_map/plan/pallas_call | solution.py:315
  13.3 1.7 %collective-permute-done.5.refs_3_ = bf16[256,256]{1,0:T(8,128)(2,1)S(1)} collective-permute-done((bf16[256,256]{1,0:T(8,128)(2,1)S(1)}, bf16[256,256]{1,0:T(8,128)(2,1)S(1)}, u32[]{:S(2)}, u32[]{:S(2)}) %collective-permute-start.5) | collective-permute-done | bytes 131104 | tf_op jit(solution)/shard_map/ppermute | solution.py:271
  15.1 1.5 %collective-permute-start.6 = (bf16[256,256]{1,0:T(8,128)(2,1)S(1)}, bf16[256,256]{1,0:T(8,128)(2,1)S(1)}, u32[]{:S(2)}, u32[]{:S(2)}) collective-permute-start(bf16[256,256]{1,0:T(8,128)(2,1)S(1)} %collective-permute-done.5.refs_3_), channel_id=1, source_target_pairs={{0,4},{8,0},{16,8},{24,16},{28,24},{20,28},{12,20},{4,12},{1,5},{9... | collective-permute-start | bytes 393224 | tf_op jit(solution)/shard_map/ppermute | solution.py:271
  17.1 2.9 %collective-permute-done.6.refs_5_ = bf16[256,256]{1,0:T(8,128)(2,1)S(1)} collective-permute-done((bf16[256,256]{1,0:T(8,128)(2,1)S(1)}, bf16[256,256]{1,0:T(8,128)(2,1)S(1)}, u32[]{:S(2)}, u32[]{:S(2)}) %collective-permute-start.6) | collective-permute-done | bytes 131104 | tf_op jit(solution)/shard_map/ppermute | solution.py:271
  20.0 1.5 %collective-permute-start.7 = (bf16[256,256]{1,0:T(8,128)(2,1)S(1)}, bf16[256,256]{1,0:T(8,128)(2,1)S(1)}, u32[]{:S(2)}, u32[]{:S(2)}) collective-permute-start(bf16[256,256]{1,0:T(8,128)(2,1)S(1)} %collective-permute-done.6.refs_5_), channel_id=1, source_target_pairs={{0,4},{8,0},{16,8},{24,16},{28,24},{20,28},{12,20},{4,12},{1,5},{9... | collective-permute-start | bytes 393224 | tf_op jit(solution)/shard_map/ppermute | solution.py:271
  22.1 5.0 %collective-permute-done.1.token_ref = bf16[128,4096]{1,0:T(8,128)(2,1)S(1)} collective-permute-done((bf16[128,4096]{1,0:T(8,128)(2,1)}, bf16[128,4096]{1,0:T(8,128)(2,1)S(1)}, u32[]{:S(2)}, u32[]{:S(2)}) %collective-permute-start.1) | collective-permute-done | bytes 1048608 | tf_op jit(solution)/shard_map/ppermute | solution.py:28
  27.1 1.2 %project_keys_values.2 = (bf16[128,256]{1,0:T(8,128)(2,1)S(1)}, bf16[128,4096]{1,0:T(8,128)(2,1)S(1)}) custom-call(bf16[128,4096]{1,0:T(8,128)(2,1)S(1)} %collective-permute-done.1.token_ref, f32[1,4096]{1,0:T(1,128)S(1)} %get-tuple-element.38.gain_ref, bf16[4096,128]{1,0:T(8,128)(2,1)S(1)} %get-tuple-element.39.wk_ref, ...), custom_call_target="tpu_custom_call" | custom-call | flops 268435456 | bytes 3145728 | tf_op jit(solution)/shard_map/project_keys_values/pallas_call | solution.py:147
  28.3 1.4 %collective-permute-done.8.token_ref = bf16[128,4096]{1,0:T(8,128)(2,1)S(1)} collective-permute-done((bf16[128,4096]{1,0:T(8,128)(2,1)S(1)}, bf16[128,4096]{1,0:T(8,128)(2,1)S(1)}, u32[]{:S(2)}, u32[]{:S(2)}) %collective-permute-start.8) | collective-permute-done | bytes 1048608 | tf_op jit(solution)/shard_map/ppermute | solution.py:28
  29.7 1.2 %project_keys_values.3 = (bf16[256,256]{1,0:T(8,128)(2,1)S(1)}, bf16[128,4096]{1,0:T(8,128)(2,1)S(1)}) custom-call(bf16[128,4096]{1,0:T(8,128)(2,1)S(1)} %collective-permute-done.8.token_ref, f32[1,4096]{1,0:T(1,128)S(1)} %get-tuple-element.38.gain_ref, bf16[4096,128]{1,0:T(8,128)(2,1)S(1)} %get-tuple-element.39.wk_ref, ...), custom_call_target="tpu_custom_call" | custom-call | flops 268435456 | bytes 3145728 | tf_op jit(solution)/shard_map/project_keys_values/pallas_call | solution.py:147
  31.0 1.9 %collective-permute-start.9 = (bf16[256,256]{1,0:T(8,128)(2,1)S(1)}, bf16[256,256]{1,0:T(8,128)(2,1)S(1)}, u32[]{:S(2)}, u32[]{:S(2)}) collective-permute-start(bf16[256,256]{1,0:T(8,128)(2,1)S(1)} %get-tuple-element.44.refs_1_), channel_id=1, source_target_pairs={{0,8},{8,16},{16,24},{24,28},{28,20},{20,12},{12,4},{4,0},{1,9},{9... | collective-permute-start | bytes 393224 | tf_op jit(solution)/shard_map/ppermute | solution.py:271
  33.0 1.9 %collective-permute-start.11 = (bf16[256,256]{1,0:T(8,128)(2,1)S(1)}, bf16[256,256]{1,0:T(8,128)(2,1)S(1)}, u32[]{:S(2)}, u32[]{:S(2)}) collective-permute-start(bf16[256,256]{1,0:T(8,128)(2,1)S(1)} %collective-permute-done.4.refs_6_), channel_id=1, source_target_pairs={{0,8},{8,16},{16,24},{24,28},{28,20},{20,12},{12,4},{4,0},{1,9},{9... | collective-permute-start | bytes 393224 | tf_op jit(solution)/shard_map/ppermute | solution.py:271
  34.9 1.4 %project_queries.1.refs_0_ = bf16[256,512]{1,0:T(8,128)(2,1)S(1)} custom-call(bf16[4096,512]{1,0:T(8,128)(2,1)S(1)} %get-tuple-element.33.wq_ref, f32[128,256]{1,0:T(8,128)S(1)} %pad_maximum_fusion.table_ref, bf16[128,4096]{1,0:T(8,128)(2,1)S(1)} %get-tuple-element.41.refs_0_, bf16[128,4096]{1,0:T(8,128)(2,1)S(1)} %get-tuple-element.45.refs_1_), custom_call_target="tpu_custom_call" | custom-call | flops 1073741824 | bytes 6291456 | tf_op jit(solution)/shard_map/project_queries/pallas_call | solution.py:147
  36.3 1.1 %collective-permute-done.9.refs_2_ = bf16[256,256]{1,0:T(8,128)(2,1)S(1)} collective-permute-done((bf16[256,256]{1,0:T(8,128)(2,1)S(1)}, bf16[256,256]{1,0:T(8,128)(2,1)S(1)}, u32[]{:S(2)}, u32[]{:S(2)}) %collective-permute-start.9) | collective-permute-done | bytes 131104 | tf_op jit(solution)/shard_map/ppermute | solution.py:271
  37.3 1.9 %collective-permute-start.13 = (bf16[256,256]{1,0:T(8,128)(2,1)S(1)}, bf16[256,256]{1,0:T(8,128)(2,1)S(1)}, u32[]{:S(2)}, u32[]{:S(2)}) collective-permute-start(bf16[256,256]{1,0:T(8,128)(2,1)S(1)} %collective-permute-done.9.refs_2_), channel_id=1, source_target_pairs={{0,8},{8,16},{16,24},{24,28},{28,20},{20,12},{12,4},{4,0},{1,9},{9... | collective-permute-start | bytes 393224 | tf_op jit(solution)/shard_map/ppermute | solution.py:271
  39.4 0.8 %collective-permute-done.11.refs_8_ = bf16[256,256]{1,0:T(8,128)(2,1)S(1)} collective-permute-done((bf16[256,256]{1,0:T(8,128)(2,1)S(1)}, bf16[256,256]{1,0:T(8,128)(2,1)S(1)}, u32[]{:S(2)}, u32[]{:S(2)}) %collective-permute-start.11) | collective-permute-done | bytes 131104 | tf_op jit(solution)/shard_map/ppermute | solution.py:271
  40.2 2.5 %attend.4 = (bf16[128,512]{1,0:T(8,128)(2,1)S(1)}, bf16[128,512]{1,0:T(8,128)(2,1)S(1)}) custom-call(s32[33]{0:T(128)S(1)} %plan.1.plan_ref, bf16[256,512]{1,0:T(8,128)(2,1)S(1)} %get-tuple-element.47.refs_0_, bf16[256,256]{1,0:T(8,128)(2,1)S(1)} %get-tuple-element.34.refs_1_, bf16[256,256]{1,0:T(8,128)(2,1)S(1)} %collective-permute-done.2.refs_2_, ...), custom_call_target="tpu_custom_call" | custom-call | flops 536870912 | bytes 1572864 | tf_op jit(solution)/shard_map/attend/pallas_call | solution.py:448
  42.6 1.9 %collective-permute-start.15 = (bf16[256,256]{1,0:T(8,128)(2,1)S(1)}, bf16[256,256]{1,0:T(8,128)(2,1)S(1)}, u32[]{:S(2)}, u32[]{:S(2)}) collective-permute-start(bf16[256,256]{1,0:T(8,128)(2,1)S(1)} %collective-permute-done.13.refs_4_), channel_id=1, source_target_pairs={{0,8},{8,16},{16,24},{24,28},{28,20},{20,12},{12,4},{4,0},{1,9},{9... | collective-permute-start | bytes 393224 | tf_op jit(solution)/shard_map/ppermute | solution.py:271
  44.7 2.9 %collective-permute-done.15.refs_6_ = bf16[256,256]{1,0:T(8,128)(2,1)S(1)} collective-permute-done((bf16[256,256]{1,0:T(8,128)(2,1)S(1)}, bf16[256,256]{1,0:T(8,128)(2,1)S(1)}, u32[]{:S(2)}, u32[]{:S(2)}) %collective-permute-start.15) | collective-permute-done | bytes 131104 | tf_op jit(solution)/shard_map/ppermute | solution.py:271
  47.7 1.9 %collective-permute-start.19 = (bf16[128,256]{1,0:T(8,128)(2,1)S(1)}, bf16[128,256]{1,0:T(8,128)(2,1)S(1)}, u32[]{:S(2)}, u32[]{:S(2)}) collective-permute-start(bf16[128,256]{1,0:T(8,128)(2,1)S(1)} %get-tuple-element.59), channel_id=1, source_target_pairs={{0,8},{8,16},{16,24},{24,28},{28,20},{20,12},{12,4},{4,0},{1,9},{9... | collective-permute-start | bytes 196616 | tf_op jit(solution)/shard_map/ppermute | solution.py:259
  49.6 1.6 %collective-permute-start.17 = (bf16[128,256]{1,0:T(8,128)(2,1)S(1)}, bf16[128,256]{1,0:T(8,128)(2,1)S(1)}, u32[]{:S(2)}, u32[]{:S(2)}) collective-permute-start(bf16[128,256]{1,0:T(8,128)(2,1)S(1)} %get-tuple-element.60), channel_id=1, source_target_pairs={{0,8},{8,16},{16,24},{24,28},{28,20},{20,12},{12,4},{4,0},{1,9},{9... | collective-permute-start | bytes 196616 | tf_op jit(solution)/shard_map/ppermute | solution.py:259
  51.2 1.5 %attend.6 = (f32[1,1,512]{2,1,0:T(1,128)S(1)}, f32[1,1,512]{2,1,0:T(1,128)S(1)}, f32[1,128,512]{2,1,0:T(8,128)S(1)}) custom-call(s32[33]{0:T(128)S(1)} %plan.1.plan_ref, bf16[256,512]{1,0:T(8,128)(2,1)S(1)} %project_queries.1.refs_0_, bf16[256,256]{1,0:T(8,128)(2,1)S(1)} %get-tuple-element.44.refs_1_, bf16[256,256]{1,0:T(8,128)(2,1)S(1)} %collective-permute-done.9.refs_2_, ...), custom_call_target="tpu_custom_call" | custom-call | flops 234881024 | bytes 1179648 | tf_op jit(solution)/shard_map/attend/pallas_call | solution.py:448
  52.7 1.0 %attend.7 = bf16[128,512]{1,0:T(8,128)(2,1)S(1)} custom-call(s32[33]{0:T(128)S(1)} %plan.1.plan_ref, bf16[256,512]{1,0:T(8,128)(2,1)S(1)} %project_queries.1.refs_0_, bf16[128,256]{1,0:T(8,128)(2,1)S(1)} %collective-permute-done.19.refs_1_, f32[1,1,512]{2,1,0:T(1,128)S(1)} %get-tuple-element.55.refs_2_, f32[1,1,512]{2,1,0:T(1,128)S(1)} %get-tuple-element.56.refs_3_, ...), custom_call_target="tpu_custom_call" | custom-call | flops 33554432 | bytes 327680 | tf_op jit(solution)/shard_map/attend/pallas_call | solution.py:448
  53.7 1.5 %collective-permute-start.20 = (bf16[128,512]{1,0:T(8,128)(2,1)S(1)}, bf16[128,512]{1,0:T(8,128)(2,1)S(1)}, u32[]{:S(2)}, u32[]{:S(2)}) collective-permute-start(bf16[128,512]{1,0:T(8,128)(2,1)S(1)} %attend.7), channel_id=1, source_target_pairs={{0,2},{1,3},{2,0},{3,1},{4,6},{5,7},{6,4},{7,5},{8,10},{9,11},{10,... | collective-permute-start | bytes 393224 | tf_op jit(solution)/shard_map/ppermute | solution.py:28
  55.2 1.6 %attend.5 = bf16[128,512]{1,0:T(8,128)(2,1)S(1)} custom-call(s32[33]{0:T(128)S(1)} %plan.1.plan_ref, bf16[256,512]{1,0:T(8,128)(2,1)S(1)} %project_queries.1.refs_0_, bf16[256,256]{1,0:T(8,128)(2,1)S(1)} %get-tuple-element.44.refs_1_, bf16[256,256]{1,0:T(8,128)(2,1)S(1)} %collective-permute-done.9.refs_2_, ...), custom_call_target="tpu_custom_call" | custom-call | flops 268435456 | bytes 1245184 | tf_op jit(solution)/shard_map/attend/pallas_call | solution.py:448
  56.9 1.3 %deliver.3.refs_1_ = bf16[1,128,2048]{2,1,0:T(8,128)(2,1)} custom-call(s32[3]{0:T(128)S(1)} %pad_add_fusion.info_ref, bf16[128,512]{1,0:T(8,128)(2,1)S(1)} %get-tuple-element.58.refs_0_, bf16[128,512]{1,0:T(8,128)(2,1)S(1)} %collective-permute-done.12.refs_1_), custom_call_target="tpu_custom_call" | custom-call | tf_op jit(solution)/shard_map/deliver/pallas_call | solution.py:480
  58.7 1.2 %deliver.4.refs_1_ = bf16[1,128,2048]{2,1,0:T(8,128)(2,1)} custom-call(s32[3]{0:T(128)S(1)} %pad_add_fusion.info_ref, bf16[128,512]{1,0:T(8,128)(2,1)S(1)} %collective-permute-done.20.refs_0_, bf16[1,128,2048]{2,1,0:T(8,128)(2,1)} %deliver.3.refs_1_), custom_call_target="tpu_custom_call", output_to_operand_aliasing={{}: (2, {})} | custom-call | tf_op jit(solution)/shard_map/deliver/pallas_call | solution.py:480
  59.9 1.9 %collective-permute-done.18.refs_0_ = bf16[128,512]{1,0:T(8,128)(2,1)S(1)} collective-permute-done((bf16[128,512]{1,0:T(8,128)(2,1)S(1)}, bf16[128,512]{1,0:T(8,128)(2,1)S(1)}, u32[]{:S(2)}, u32[]{:S(2)}) %collective-permute-start.18) | collective-permute-done | bytes 131104 | tf_op jit(solution)/shard_map/ppermute | solution.py:28
  61.8 1.2 %deliver.5 = bf16[1,128,2048]{2,1,0:T(8,128)(2,1)} custom-call(s32[3]{0:T(128)S(1)} %pad_add_fusion.info_ref, bf16[128,512]{1,0:T(8,128)(2,1)S(1)} %collective-permute-done.18.refs_0_, bf16[1,128,2048]{2,1,0:T(8,128)(2,1)} %deliver.4.refs_1_), custom_call_target="tpu_custom_call", output_to_operand_aliasing={{}: (2, {})} | custom-call | tf_op jit(solution)/shard_map/deliver/pallas_call | solution.py:480
  (33 shorter events, 4.2 us)
Async XLA Ops:
  0.1 4.7 %collective-permute-start = (bf16[128,4096]{1,0:T(8,128)(2,1)}, bf16[128,4096]{1,0:T(8,128)(2,1)S(1)}, u32[]{:S(2)}, u32[]{:S(2)}) collective-permute-start(bf16[128,4096]{1,0:T(8,128)(2,1)} %bitcast.6), channel_id=1, source_target_pairs={{0,1},{1,0},{2,3},{3,2},{4,5},{5,4},{6,7},{7,6},{8,9},{9,8},{10,11... | collective-permute-start | bytes 3145736 | tf_op jit(solution)/shard_map/ppermute | solution.py:28
  0.5 26.5 %collective-permute-start.1 = (bf16[128,4096]{1,0:T(8,128)(2,1)}, bf16[128,4096]{1,0:T(8,128)(2,1)S(1)}, u32[]{:S(2)}, u32[]{:S(2)}) collective-permute-start(bf16[128,4096]{1,0:T(8,128)(2,1)} %bitcast.7), channel_id=1, source_target_pairs={{0,2},{1,3},{2,0},{3,1},{4,6},{5,7},{6,4},{7,5},{8,10},{9,11},{10,... | collective-permute-start | bytes 3145736 | tf_op jit(solution)/shard_map/ppermute | solution.py:28
  4.8 6.7 %copy-start = (s32[4,4,4]{2,1,0:T(4,128)S(1)}, s32[4,4,4]{2,1,0:T(4,128)}, u32[]{:S(2)}) copy-start(s32[4,4,4]{2,1,0:T(4,128)} %vertical_ref.1) | copy-start | bytes 772
  4.8 6.7 %copy-start.1 = (s32[4,4,4]{2,1,0:T(4,128)S(1)}, s32[4,4,4]{2,1,0:T(4,128)}, u32[]{:S(2)}) copy-start(s32[4,4,4]{2,1,0:T(4,128)} %slash_ref.1) | copy-start | bytes 772
  9.4 5.6 %collective-permute-start.5 = (bf16[256,256]{1,0:T(8,128)(2,1)S(1)}, bf16[256,256]{1,0:T(8,128)(2,1)S(1)}, u32[]{:S(2)}, u32[]{:S(2)}) collective-permute-start(bf16[256,256]{1,0:T(8,128)(2,1)S(1)} %get-tuple-element.34.refs_1_), channel_id=1, source_target_pairs={{0,4},{8,0},{16,8},{24,16},{28,24},{20,28},{12,20},{4,12},{1,5},{9... | collective-permute-start | bytes 393224 | tf_op jit(solution)/shard_map/ppermute | solution.py:271
  11.0 5.6 %collective-permute-start.2 = (bf16[256,256]{1,0:T(8,128)(2,1)S(1)}, bf16[256,256]{1,0:T(8,128)(2,1)S(1)}, u32[]{:S(2)}, u32[]{:S(2)}) collective-permute-start(bf16[256,256]{1,0:T(8,128)(2,1)S(1)} %get-tuple-element.34.refs_1_), channel_id=1, source_target_pairs={{0,8},{8,16},{16,24},{24,28},{28,20},{20,12},{12,4},{4,0},{1,9},{9... | collective-permute-start | bytes 393224 | tf_op jit(solution)/shard_map/ppermute | solution.py:271
  15.1 5.0 %collective-permute-start.6 = (bf16[256,256]{1,0:T(8,128)(2,1)S(1)}, bf16[256,256]{1,0:T(8,128)(2,1)S(1)}, u32[]{:S(2)}, u32[]{:S(2)}) collective-permute-start(bf16[256,256]{1,0:T(8,128)(2,1)S(1)} %collective-permute-done.5.refs_3_), channel_id=1, source_target_pairs={{0,4},{8,0},{16,8},{24,16},{28,24},{20,28},{12,20},{4,12},{1,5},{9... | collective-permute-start | bytes 393224 | tf_op jit(solution)/shard_map/ppermute | solution.py:271
  16.6 5.0 %collective-permute-start.3 = (bf16[256,256]{1,0:T(8,128)(2,1)S(1)}, bf16[256,256]{1,0:T(8,128)(2,1)S(1)}, u32[]{:S(2)}, u32[]{:S(2)}) collective-permute-start(bf16[256,256]{1,0:T(8,128)(2,1)S(1)} %collective-permute-done.2.refs_2_), channel_id=1, source_target_pairs={{0,8},{8,16},{16,24},{24,28},{28,20},{20,12},{12,4},{4,0},{1,9},{9... | collective-permute-start | bytes 393224 | tf_op jit(solution)/shard_map/ppermute | solution.py:271
  20.0 7.0 %collective-permute-start.7 = (bf16[256,256]{1,0:T(8,128)(2,1)S(1)}, bf16[256,256]{1,0:T(8,128)(2,1)S(1)}, u32[]{:S(2)}, u32[]{:S(2)}) collective-permute-start(bf16[256,256]{1,0:T(8,128)(2,1)S(1)} %collective-permute-done.6.refs_5_), channel_id=1, source_target_pairs={{0,4},{8,0},{16,8},{24,16},{28,24},{20,28},{12,20},{4,12},{1,5},{9... | collective-permute-start | bytes 393224 | tf_op jit(solution)/shard_map/ppermute | solution.py:271
  21.5 5.5 %collective-permute-start.4 = (bf16[256,256]{1,0:T(8,128)(2,1)S(1)}, bf16[256,256]{1,0:T(8,128)(2,1)S(1)}, u32[]{:S(2)}, u32[]{:S(2)}) collective-permute-start(bf16[256,256]{1,0:T(8,128)(2,1)S(1)} %collective-permute-done.3.refs_4_), channel_id=1, source_target_pairs={{0,8},{8,16},{16,24},{24,28},{28,20},{20,12},{12,4},{4,0},{1,9},{9... | collective-permute-start | bytes 393224 | tf_op jit(solution)/shard_map/ppermute | solution.py:271
  27.1 2.7 %collective-permute-start.8 = (bf16[128,4096]{1,0:T(8,128)(2,1)S(1)}, bf16[128,4096]{1,0:T(8,128)(2,1)S(1)}, u32[]{:S(2)}, u32[]{:S(2)}) collective-permute-start(bf16[128,4096]{1,0:T(8,128)(2,1)S(1)} %collective-permute-done.1.token_ref), channel_id=1, source_target_pairs={{0,1},{1,0},{2,3},{3,2},{4,5},{5,4},{6,7},{7,6},{8,9},{9,8},{10,11... | collective-permute-start | bytes 3145736 | tf_op jit(solution)/shard_map/ppermute | solution.py:28
  31.0 6.4 %collective-permute-start.9 = (bf16[256,256]{1,0:T(8,128)(2,1)S(1)}, bf16[256,256]{1,0:T(8,128)(2,1)S(1)}, u32[]{:S(2)}, u32[]{:S(2)}) collective-permute-start(bf16[256,256]{1,0:T(8,128)(2,1)S(1)} %get-tuple-element.44.refs_1_), channel_id=1, source_target_pairs={{0,8},{8,16},{16,24},{24,28},{28,20},{20,12},{12,4},{4,0},{1,9},{9... | collective-permute-start | bytes 393224 | tf_op jit(solution)/shard_map/ppermute | solution.py:271
  32.9 6.3 %collective-permute-start.10 = (bf16[256,256]{1,0:T(8,128)(2,1)S(1)}, bf16[256,256]{1,0:T(8,128)(2,1)S(1)}, u32[]{:S(2)}, u32[]{:S(2)}) collective-permute-start(bf16[256,256]{1,0:T(8,128)(2,1)S(1)} %get-tuple-element.44.refs_1_), channel_id=1, source_target_pairs={{0,4},{8,0},{16,8},{24,16},{28,24},{20,28},{12,20},{4,12},{1,5},{9... | collective-permute-start | bytes 393224 | tf_op jit(solution)/shard_map/ppermute | solution.py:271
  33.0 7.1 %collective-permute-start.11 = (bf16[256,256]{1,0:T(8,128)(2,1)S(1)}, bf16[256,256]{1,0:T(8,128)(2,1)S(1)}, u32[]{:S(2)}, u32[]{:S(2)}) collective-permute-start(bf16[256,256]{1,0:T(8,128)(2,1)S(1)} %collective-permute-done.4.refs_6_), channel_id=1, source_target_pairs={{0,8},{8,16},{16,24},{24,28},{28,20},{20,12},{12,4},{4,0},{1,9},{9... | collective-permute-start | bytes 393224 | tf_op jit(solution)/shard_map/ppermute | solution.py:271
  37.3 5.3 %collective-permute-start.13 = (bf16[256,256]{1,0:T(8,128)(2,1)S(1)}, bf16[256,256]{1,0:T(8,128)(2,1)S(1)}, u32[]{:S(2)}, u32[]{:S(2)}) collective-permute-start(bf16[256,256]{1,0:T(8,128)(2,1)S(1)} %collective-permute-done.9.refs_2_), channel_id=1, source_target_pairs={{0,8},{8,16},{16,24},{24,28},{28,20},{20,12},{12,4},{4,0},{1,9},{9... | collective-permute-start | bytes 393224 | tf_op jit(solution)/shard_map/ppermute | solution.py:271
  39.2 5.4 %collective-permute-start.14 = (bf16[256,256]{1,0:T(8,128)(2,1)S(1)}, bf16[256,256]{1,0:T(8,128)(2,1)S(1)}, u32[]{:S(2)}, u32[]{:S(2)}) collective-permute-start(bf16[256,256]{1,0:T(8,128)(2,1)S(1)} %collective-permute-done.10.refs_3_), channel_id=1, source_target_pairs={{0,4},{8,0},{16,8},{24,16},{28,24},{20,28},{12,20},{4,12},{1,5},{9... | collective-permute-start | bytes 393224 | tf_op jit(solution)/shard_map/ppermute | solution.py:271
  42.6 5.0 %collective-permute-start.15 = (bf16[256,256]{1,0:T(8,128)(2,1)S(1)}, bf16[256,256]{1,0:T(8,128)(2,1)S(1)}, u32[]{:S(2)}, u32[]{:S(2)}) collective-permute-start(bf16[256,256]{1,0:T(8,128)(2,1)S(1)} %collective-permute-done.13.refs_4_), channel_id=1, source_target_pairs={{0,8},{8,16},{16,24},{24,28},{28,20},{20,12},{12,4},{4,0},{1,9},{9... | collective-permute-start | bytes 393224 | tf_op jit(solution)/shard_map/ppermute | solution.py:271
  44.6 6.6 %collective-permute-start.12 = (bf16[128,512]{1,0:T(8,128)(2,1)S(1)}, bf16[128,512]{1,0:T(8,128)(2,1)S(1)}, u32[]{:S(2)}, u32[]{:S(2)}) collective-permute-start(bf16[128,512]{1,0:T(8,128)(2,1)S(1)} %get-tuple-element.49), channel_id=1, source_target_pairs={{0,1},{1,0},{2,3},{3,2},{4,5},{5,4},{6,7},{7,6},{8,9},{9,8},{10,11... | collective-permute-start | bytes 393224 | tf_op jit(solution)/shard_map/ppermute | solution.py:28
  44.6 6.6 %collective-permute-start.16 = (bf16[256,256]{1,0:T(8,128)(2,1)S(1)}, bf16[256,256]{1,0:T(8,128)(2,1)S(1)}, u32[]{:S(2)}, u32[]{:S(2)}) collective-permute-start(bf16[256,256]{1,0:T(8,128)(2,1)S(1)} %collective-permute-done.14.refs_5_), channel_id=1, source_target_pairs={{0,4},{8,0},{16,8},{24,16},{28,24},{20,28},{12,20},{4,12},{1,5},{9... | collective-permute-start | bytes 393224 | tf_op jit(solution)/shard_map/ppermute | solution.py:271
  47.7 5.0 %collective-permute-start.19 = (bf16[128,256]{1,0:T(8,128)(2,1)S(1)}, bf16[128,256]{1,0:T(8,128)(2,1)S(1)}, u32[]{:S(2)}, u32[]{:S(2)}) collective-permute-start(bf16[128,256]{1,0:T(8,128)(2,1)S(1)} %get-tuple-element.59), channel_id=1, source_target_pairs={{0,8},{8,16},{16,24},{24,28},{28,20},{20,12},{12,4},{4,0},{1,9},{9... | collective-permute-start | bytes 196616 | tf_op jit(solution)/shard_map/ppermute | solution.py:259
  49.6 5.6 %collective-permute-start.17 = (bf16[128,256]{1,0:T(8,128)(2,1)S(1)}, bf16[128,256]{1,0:T(8,128)(2,1)S(1)}, u32[]{:S(2)}, u32[]{:S(2)}) collective-permute-start(bf16[128,256]{1,0:T(8,128)(2,1)S(1)} %get-tuple-element.60), channel_id=1, source_target_pairs={{0,8},{8,16},{16,24},{24,28},{28,20},{20,12},{12,4},{4,0},{1,9},{9... | collective-permute-start | bytes 196616 | tf_op jit(solution)/shard_map/ppermute | solution.py:259
  53.7 5.0 %collective-permute-start.20 = (bf16[128,512]{1,0:T(8,128)(2,1)S(1)}, bf16[128,512]{1,0:T(8,128)(2,1)S(1)}, u32[]{:S(2)}, u32[]{:S(2)}) collective-permute-start(bf16[128,512]{1,0:T(8,128)(2,1)S(1)} %attend.7), channel_id=1, source_target_pairs={{0,2},{1,3},{2,0},{3,1},{4,6},{5,7},{6,4},{7,5},{8,10},{9,11},{10,... | collective-permute-start | bytes 393224 | tf_op jit(solution)/shard_map/ppermute | solution.py:28
  56.9 5.0 %collective-permute-start.18 = (bf16[128,512]{1,0:T(8,128)(2,1)S(1)}, bf16[128,512]{1,0:T(8,128)(2,1)S(1)}, u32[]{:S(2)}, u32[]{:S(2)}) collective-permute-start(bf16[128,512]{1,0:T(8,128)(2,1)S(1)} %attend.5), channel_id=1, source_target_pairs={{0,3},{1,2},{2,1},{3,0},{4,7},{5,6},{6,5},{7,4},{8,11},{9,10},{10,... | collective-permute-start | bytes 393224 | tf_op jit(solution)/shard_map/ppermute | solution.py:28

commit v4 on v3

--- a/solution.py
+++ b/solution.py
@@ -462,31 +462,37 @@
     )(table, *queries, *arrays, *held)
 
 
-def deliver_kernel(masks, info_ref, *refs):
+def deliver_kernel(masks, *refs):
     pieces, (out_ref, sems) = refs[:len(masks)], refs[-2:]
-    cols = pieces[0].shape[1]
+    rows, cols = pieces[0].shape
+    me, strips = lax.axis_index("doc"), sems.shape[1]
     copies = []
     for at, (mask, piece) in enumerate(zip(masks, pieces)):
-        where = pl.ds(pl.multiple_of((info_ref[1] ^ mask) * cols, cols), cols)
-        copies.append(pltpu.make_async_copy(piece, out_ref.at[0, :, where], sems.at[at]))
-        copies[-1].start()
+        where = pl.ds(pl.multiple_of((me ^ mask) * cols, cols), cols)
+        for strip in range(strips):
+            band = pl.ds(strip * (rows // strips), rows // strips)
+            copies.append(
+                pltpu.make_async_copy(piece.at[band], out_ref.at[0, band, where], sems.at[at, strip])
+            )
+            copies[-1].start()
     for copy in copies:
         copy.wait()
 
 
-def deliver(info, masks, pieces, count, before=None):
+def deliver(masks, pieces, count, before=None):
     rows, cols = pieces[0].shape
     begun = () if before is None else (before,)
+    strips = 4 if rows % (4 * BAND) == 0 else 1
     return pl.pallas_call(
         functools.partial(deliver_kernel, masks),
-        in_specs=[SMEM] + [VMEM] * len(pieces) + [HBM] * len(begun),
+        in_specs=[VMEM] * len(pieces) + [HBM] * len(begun),
         out_specs=HBM,
         out_shape=jax.ShapeDtypeStruct((1, rows, count * cols), jnp.bfloat16),
-        input_output_aliases={1 + len(pieces): 0} if begun else {},
-        scratch_shapes=[pltpu.SemaphoreType.DMA((len(pieces),))],
+        input_output_aliases={len(pieces): 0} if begun else {},
+        scratch_shapes=[pltpu.SemaphoreType.DMA((len(pieces), strips))],
         compiler_params=pltpu.CompilerParams(vmem_limit_bytes=4 * MIB),
         name="deliver",
-    )(info, *pieces, *begun)
+    )(*pieces, *begun)
 
 
 def local(tokens, norm_gain, w_query, key_weight, value_weight, vertical_blocks, slash_offsets):
@@ -504,7 +510,7 @@
     table_of = plan(info, vertical_blocks, slash_offsets, not long, rows)
 
     twin = swap(own, "doc", 1)
-    across = swap(own, "doc", 2)
+    across = swap(tokens[0], "doc", 2)
     q_near, kv_near, gain_in, wq_in, wk_in, wv_in = project_near(
         own, twin, gain, w_query, key_weight, value_weight, table
     )
@@ -514,13 +520,13 @@
     near.advance()
 
     across = after(across, *near.latest)
+    near.advance()
     crossed = swap(across, "doc", 1)
     kv_across, across_in = project_keys_values(across, gain_in, wk_in, wv_in, table)
     kv_far, crossed_in = project_keys_values(crossed, gain_in, wk_in, wv_in, table, before=kv_across)
     far = ring(kv_far)
     far.advance()
-    near.advance(kv_far)
-    q_far = project_queries([across_in, after(crossed_in, kv_far)], wq_in, table)
+    q_far = project_queries([across_in, after(crossed_in, kv_far, *near.latest)], wq_in, table)
     mixed_own, mixed_twin = attend(
         table_of,
         [(0, (0, 0), 0, rows), (1, (0, rows), rows, rows)],
@@ -554,9 +560,9 @@
         )
         home.append(swap(mixed, "doc", 3))
     count = lax.axis_size("doc")
-    result = deliver(info, (0, 1), [mixed_own, out_twin], count)
-    result = deliver(info, (2,), home[:1], count, before=result)
-    return deliver(info, (3,), home[1:], count, before=result)
+    result = deliver((0, 1), [mixed_own, out_twin], count)
+    result = deliver((2,), home[:1], count, before=result)
+    return deliver((3,), home[1:], count, before=result)
 
 
 def solution(mesh):

time: 63.2 us -> 61.7 us (0.976)
  Pallas kernels: 20.5 us -> 18.9 us
    pallas_call x3, Pallas kernels: 3.68 us -> 2.13 us  [deliver(): pl.pallas_call(functools.partial(deliver_kernel, masks), in_specs=[VMEM]...]
    ppermute x13, waiting for transfers between devices: 9.47 us -> 10.2 us  [advance(): self.front[way] = lax.ppermute(value, 'seq', pairs)]
  transfers between devices with their start and end apart: 21 -> 21, of which waited for: 9 -> 8; matrix products, arithmetic and copies ran while one was open for 3% -> 3% of each run, Pallas kernels for 29% -> 30%
where the time goes in v4:
time: 61.7 us; the launch traced here: 61.6 us
  starting transfers between devices  22 us (36%)
  Pallas kernels  18.9 us (31%)
  waiting for transfers between devices  18.7 us (30%)
  other arithmetic  1.16 us (2%)
    ppermute x13, starting transfers between devices, advance(): self.front[way] = lax.ppermute(value, 'seq', pairs)  14.2 us
    ppermute x13, waiting for transfers between devices, advance(): self.front[way] = lax.ppermute(value, 'seq', pairs)  10.2 us
    ppermute x6, waiting for transfers between devices, swap(): lax.ppermute(value, axis, [(source, source ^ mask) for source in range(co...  8.42 us
    pallas_call x4, Pallas kernels, project_call(): pl.pallas_call(kernel, in_specs=kinds, out_specs=[VMEM] * len(shapes), ou...  8.41 us
    pallas_call x4, Pallas kernels, attend(): pl.pallas_call(kernel, in_specs=[SMEM] + [VMEM] * (len(queries) + len(arr...  6.6 us
    ppermute x6, starting transfers between devices, swap(): lax.ppermute(value, axis, [(source, source ^ mask) for source in range(co...  4.64 us
    ppermute x2, starting transfers between devices, last(): return lax.ppermute(array, 'seq', pairs)  3.21 us
    pallas_call x3, Pallas kernels, deliver(): pl.pallas_call(functools.partial(deliver_kernel, masks), in_specs=[VMEM]...  2.13 us
  transfers between devices with their start and end apart: 21, of which 8 were waited for; matrix products, arithmetic and copies ran while one was open for 3% of the time, Pallas kernels for 30%

profile of v4, /device:TPU:0, one launch (start us, length us, event | category | flops | bytes accessed | tf_op | source)
XLA Modules:
  0.0 61.6 jit_solution(11135150211770978748)
XLA Ops:
  0.5 2.6 %collective-permute-start.1 = (bf16[128,4096]{1,0:T(8,128)(2,1)}, bf16[128,4096]{1,0:T(8,128)(2,1)S(1)}, u32[]{:S(2)}, u32[]{:S(2)}) collective-permute-start(bf16[128,4096]{1,0:T(8,128)(2,1)} %bitcast.8), channel_id=1, source_target_pairs={{0,2},{1,3},{2,0},{3,1},{4,6},{5,7},{6,4},{7,5},{8,10},{9,11},{10,... | collective-permute-start | bytes 3145736 | tf_op jit(solution)/shard_map/ppermute | solution.py:28
  3.1 0.6 slice.9
  3.7 0.6 %add_convert_fusion = f32[128]{0:T(128)S(1)} fusion(s32[]{:T(128)} %bitcast.5), kind=kLoop, calls=%fused_computation.6 | loop fusion | flops 256 | bytes 516 | tf_op jit(solution)/shard_map/convert_element_type | solution.py:41
  4.8 4.6 %project_near.1 = (bf16[256,512]{1,0:T(8,128)(2,1)S(1)}, bf16[256,256]{1,0:T(8,128)(2,1)S(1)}, f32[1,4096]{1,0:T(1,128)S(1)}, bf16[4096,512]{1,0:T(8,128)(2,1)S(...) custom-call(bf16[128,4096]{1,0:T(8,128)(2,1)} %bitcast.9, ...), custom_call_target="tpu_custom_call" | custom-call | flops 1610612736 | bytes 8388608 | tf_op jit(solution)/shard_map/project_near/pallas_call | solution.py:147
  9.4 1.6 %collective-permute-start.2 = (bf16[256,256]{1,0:T(8,128)(2,1)S(1)}, bf16[256,256]{1,0:T(8,128)(2,1)S(1)}, u32[]{:S(2)}, u32[]{:S(2)}) collective-permute-start(bf16[256,256]{1,0:T(8,128)(2,1)S(1)} %get-tuple-element.33.refs_1_), channel_id=1, source_target_pairs={{0,8},{8,16},{16,24},{24,28},{28,20},{20,12},{12,4},{4,0},{1,9},{9... | collective-permute-start | bytes 393224 | tf_op jit(solution)/shard_map/ppermute | solution.py:271
  11.5 1.8 %plan.1.plan_ref = s32[33]{0:T(128)S(1)} custom-call(s32[3]{0:T(128)S(1)} %pad_add_fusion.info_ref, s32[4,4,4]{2,1,0:T(4,128)S(1)} %copy-done, s32[4,4,4]{2,1,0:T(4,128)S(1)} %copy-done.1), custom_call_target="tpu_custom_call" | custom-call | tf_op jit(solution)/shard_map/plan/pallas_call | solution.py:315
  13.3 1.7 %collective-permute-done.2.refs_2_ = bf16[256,256]{1,0:T(8,128)(2,1)S(1)} collective-permute-done((bf16[256,256]{1,0:T(8,128)(2,1)S(1)}, bf16[256,256]{1,0:T(8,128)(2,1)S(1)}, u32[]{:S(2)}, u32[]{:S(2)}) %collective-permute-start.2) | collective-permute-done | bytes 131104 | tf_op jit(solution)/shard_map/ppermute | solution.py:271
  15.1 1.6 %collective-permute-start.3 = (bf16[256,256]{1,0:T(8,128)(2,1)S(1)}, bf16[256,256]{1,0:T(8,128)(2,1)S(1)}, u32[]{:S(2)}, u32[]{:S(2)}) collective-permute-start(bf16[256,256]{1,0:T(8,128)(2,1)S(1)} %collective-permute-done.2.refs_2_), channel_id=1, source_target_pairs={{0,8},{8,16},{16,24},{24,28},{28,20},{20,12},{12,4},{4,0},{1,9},{9... | collective-permute-start | bytes 393224 | tf_op jit(solution)/shard_map/ppermute | solution.py:271
  17.1 2.9 %collective-permute-done.3.refs_4_ = bf16[256,256]{1,0:T(8,128)(2,1)S(1)} collective-permute-done((bf16[256,256]{1,0:T(8,128)(2,1)S(1)}, bf16[256,256]{1,0:T(8,128)(2,1)S(1)}, u32[]{:S(2)}, u32[]{:S(2)}) %collective-permute-start.3) | collective-permute-done | bytes 131104 | tf_op jit(solution)/shard_map/ppermute | solution.py:271
  20.0 1.6 %collective-permute-start.4 = (bf16[256,256]{1,0:T(8,128)(2,1)S(1)}, bf16[256,256]{1,0:T(8,128)(2,1)S(1)}, u32[]{:S(2)}, u32[]{:S(2)}) collective-permute-start(bf16[256,256]{1,0:T(8,128)(2,1)S(1)} %collective-permute-done.3.refs_4_), channel_id=1, source_target_pairs={{0,8},{8,16},{16,24},{24,28},{28,20},{20,12},{12,4},{4,0},{1,9},{9... | collective-permute-start | bytes 393224 | tf_op jit(solution)/shard_map/ppermute | solution.py:271
  22.1 5.0 %collective-permute-done.1.token_ref = bf16[128,4096]{1,0:T(8,128)(2,1)S(1)} collective-permute-done((bf16[128,4096]{1,0:T(8,128)(2,1)}, bf16[128,4096]{1,0:T(8,128)(2,1)S(1)}, u32[]{:S(2)}, u32[]{:S(2)}) %collective-permute-start.1) | collective-permute-done | bytes 1048608 | tf_op jit(solution)/shard_map/ppermute | solution.py:28
  27.1 1.9 %collective-permute-start.9 = (bf16[256,256]{1,0:T(8,128)(2,1)S(1)}, bf16[256,256]{1,0:T(8,128)(2,1)S(1)}, u32[]{:S(2)}, u32[]{:S(2)}) collective-permute-start(bf16[256,256]{1,0:T(8,128)(2,1)S(1)} %collective-permute-done.4.refs_6_), channel_id=1, source_target_pairs={{0,8},{8,16},{16,24},{24,28},{28,20},{20,12},{12,4},{4,0},{1,9},{9... | collective-permute-start | bytes 393224 | tf_op jit(solution)/shard_map/ppermute | solution.py:271
  29.0 1.2 %project_keys_values.2 = (bf16[128,256]{1,0:T(8,128)(2,1)S(1)}, bf16[128,4096]{1,0:T(8,128)(2,1)S(1)}) custom-call(bf16[128,4096]{1,0:T(8,128)(2,1)S(1)} %collective-permute-done.1.token_ref, f32[1,4096]{1,0:T(1,128)S(1)} %get-tuple-element.37.gain_ref, bf16[4096,128]{1,0:T(8,128)(2,1)S(1)} %get-tuple-element.38.wk_ref, ...), custom_call_target="tpu_custom_call" | custom-call | flops 268435456 | bytes 3145728 | tf_op jit(solution)/shard_map/project_keys_values/pallas_call | solution.py:147
  30.2 1.2 %project_keys_values.3 = (bf16[256,256]{1,0:T(8,128)(2,1)S(1)}, bf16[128,4096]{1,0:T(8,128)(2,1)S(1)}) custom-call(bf16[128,4096]{1,0:T(8,128)(2,1)S(1)} %collective-permute-done.8.token_ref, f32[1,4096]{1,0:T(1,128)S(1)} %get-tuple-element.37.gain_ref, bf16[4096,128]{1,0:T(8,128)(2,1)S(1)} %get-tuple-element.38.wk_ref, ...), custom_call_target="tpu_custom_call" | custom-call | flops 268435456 | bytes 3145728 | tf_op jit(solution)/shard_map/project_keys_values/pallas_call | solution.py:147
  31.4 1.6 %collective-permute-start.10 = (bf16[256,256]{1,0:T(8,128)(2,1)S(1)}, bf16[256,256]{1,0:T(8,128)(2,1)S(1)}, u32[]{:S(2)}, u32[]{:S(2)}) collective-permute-start(bf16[256,256]{1,0:T(8,128)(2,1)S(1)} %get-tuple-element.43.refs_1_), channel_id=1, source_target_pairs={{0,8},{8,16},{16,24},{24,28},{28,20},{20,12},{12,4},{4,0},{1,9},{9... | collective-permute-start | bytes 393224 | tf_op jit(solution)/shard_map/ppermute | solution.py:271
  33.5 1.4 %project_queries.1.refs_0_ = bf16[256,512]{1,0:T(8,128)(2,1)S(1)} custom-call(bf16[4096,512]{1,0:T(8,128)(2,1)S(1)} %get-tuple-element.32.wq_ref, f32[128,256]{1,0:T(8,128)S(1)} %pad_maximum_fusion.table_ref, bf16[128,4096]{1,0:T(8,128)(2,1)S(1)} %get-tuple-element.40.refs_0_, bf16[128,4096]{1,0:T(8,128)(2,1)S(1)} %get-tuple-element.44.refs_1_), custom_call_target="tpu_custom_call" | custom-call | flops 1073741824 | bytes 6291456 | tf_op jit(solution)/shard_map/project_queries/pallas_call | solution.py:147
  34.9 2.2 %collective-permute-done.10.refs_2_ = bf16[256,256]{1,0:T(8,128)(2,1)S(1)} collective-permute-done((bf16[256,256]{1,0:T(8,128)(2,1)S(1)}, bf16[256,256]{1,0:T(8,128)(2,1)S(1)}, u32[]{:S(2)}, u32[]{:S(2)}) %collective-permute-start.10) | collective-permute-done | bytes 131104 | tf_op jit(solution)/shard_map/ppermute | solution.py:271
  37.1 1.6 %collective-permute-start.13 = (bf16[256,256]{1,0:T(8,128)(2,1)S(1)}, bf16[256,256]{1,0:T(8,128)(2,1)S(1)}, u32[]{:S(2)}, u32[]{:S(2)}) collective-permute-start(bf16[256,256]{1,0:T(8,128)(2,1)S(1)} %collective-permute-done.10.refs_2_), channel_id=1, source_target_pairs={{0,8},{8,16},{16,24},{24,28},{28,20},{20,12},{12,4},{4,0},{1,9},{9... | collective-permute-start | bytes 393224 | tf_op jit(solution)/shard_map/ppermute | solution.py:271
  39.1 2.5 %attend.4 = (bf16[128,512]{1,0:T(8,128)(2,1)S(1)}, bf16[128,512]{1,0:T(8,128)(2,1)S(1)}) custom-call(s32[33]{0:T(128)S(1)} %plan.1.plan_ref, bf16[256,512]{1,0:T(8,128)(2,1)S(1)} %get-tuple-element.46.refs_0_, bf16[256,256]{1,0:T(8,128)(2,1)S(1)} %get-tuple-element.33.refs_1_, bf16[256,256]{1,0:T(8,128)(2,1)S(1)} %collective-permute-done.2.refs_2_, ...), custom_call_target="tpu_custom_call" | custom-call | flops 536870912 | bytes 1572864 | tf_op jit(solution)/shard_map/attend/pallas_call | solution.py:448
  42.0 1.6 %collective-permute-start.15 = (bf16[256,256]{1,0:T(8,128)(2,1)S(1)}, bf16[256,256]{1,0:T(8,128)(2,1)S(1)}, u32[]{:S(2)}, u32[]{:S(2)}) collective-permute-start(bf16[256,256]{1,0:T(8,128)(2,1)S(1)} %collective-permute-done.13.refs_4_), channel_id=1, source_target_pairs={{0,8},{8,16},{16,24},{24,28},{28,20},{20,12},{12,4},{4,0},{1,9},{9... | collective-permute-start | bytes 393224 | tf_op jit(solution)/shard_map/ppermute | solution.py:271
  44.1 2.9 %collective-permute-done.15.refs_6_ = bf16[256,256]{1,0:T(8,128)(2,1)S(1)} collective-permute-done((bf16[256,256]{1,0:T(8,128)(2,1)S(1)}, bf16[256,256]{1,0:T(8,128)(2,1)S(1)}, u32[]{:S(2)}, u32[]{:S(2)}) %collective-permute-start.15) | collective-permute-done | bytes 131104 | tf_op jit(solution)/shard_map/ppermute | solution.py:271
  47.0 1.6 %collective-permute-start.19 = (bf16[128,256]{1,0:T(8,128)(2,1)S(1)}, bf16[128,256]{1,0:T(8,128)(2,1)S(1)}, u32[]{:S(2)}, u32[]{:S(2)}) collective-permute-start(bf16[128,256]{1,0:T(8,128)(2,1)S(1)} %get-tuple-element.57), channel_id=1, source_target_pairs={{0,8},{8,16},{16,24},{24,28},{28,20},{20,12},{12,4},{4,0},{1,9},{9... | collective-permute-start | bytes 196616 | tf_op jit(solution)/shard_map/ppermute | solution.py:259
  48.7 1.6 %collective-permute-start.17 = (bf16[128,256]{1,0:T(8,128)(2,1)S(1)}, bf16[128,256]{1,0:T(8,128)(2,1)S(1)}, u32[]{:S(2)}, u32[]{:S(2)}) collective-permute-start(bf16[128,256]{1,0:T(8,128)(2,1)S(1)} %get-tuple-element.58), channel_id=1, source_target_pairs={{0,8},{8,16},{16,24},{24,28},{28,20},{20,12},{12,4},{4,0},{1,9},{9... | collective-permute-start | bytes 196616 | tf_op jit(solution)/shard_map/ppermute | solution.py:259
  50.2 1.5 %attend.6 = (f32[1,1,512]{2,1,0:T(1,128)S(1)}, f32[1,1,512]{2,1,0:T(1,128)S(1)}, f32[1,128,512]{2,1,0:T(8,128)S(1)}) custom-call(s32[33]{0:T(128)S(1)} %plan.1.plan_ref, bf16[256,512]{1,0:T(8,128)(2,1)S(1)} %project_queries.1.refs_0_, bf16[256,256]{1,0:T(8,128)(2,1)S(1)} %get-tuple-element.43.refs_1_, bf16[256,256]{1,0:T(8,128)(2,1)S(1)} %collective-permute-done.10.refs_2_, ...), custom_call_target="tpu_custom_call" | custom-call | flops 234881024 | bytes 1179648 | tf_op jit(solution)/shard_map/attend/pallas_call | solution.py:448
  51.7 1.0 %attend.7 = bf16[128,512]{1,0:T(8,128)(2,1)S(1)} custom-call(s32[33]{0:T(128)S(1)} %plan.1.plan_ref, bf16[256,512]{1,0:T(8,128)(2,1)S(1)} %project_queries.1.refs_0_, bf16[128,256]{1,0:T(8,128)(2,1)S(1)} %collective-permute-done.19.refs_1_, f32[1,1,512]{2,1,0:T(1,128)S(1)} %get-tuple-element.53.refs_2_, f32[1,1,512]{2,1,0:T(1,128)S(1)} %get-tuple-element.54.refs_3_, ...), custom_call_target="tpu_custom_call" | custom-call | flops 33554432 | bytes 327680 | tf_op jit(solution)/shard_map/attend/pallas_call | solution.py:448
  52.8 1.5 %collective-permute-start.20 = (bf16[128,512]{1,0:T(8,128)(2,1)S(1)}, bf16[128,512]{1,0:T(8,128)(2,1)S(1)}, u32[]{:S(2)}, u32[]{:S(2)}) collective-permute-start(bf16[128,512]{1,0:T(8,128)(2,1)S(1)} %attend.7), channel_id=1, source_target_pairs={{0,2},{1,3},{2,0},{3,1},{4,6},{5,7},{6,4},{7,5},{8,10},{9,11},{10,... | collective-permute-start | bytes 393224 | tf_op jit(solution)/shard_map/ppermute | solution.py:28
  54.3 1.6 %attend.5 = bf16[128,512]{1,0:T(8,128)(2,1)S(1)} custom-call(s32[33]{0:T(128)S(1)} %plan.1.plan_ref, bf16[256,512]{1,0:T(8,128)(2,1)S(1)} %project_queries.1.refs_0_, bf16[256,256]{1,0:T(8,128)(2,1)S(1)} %get-tuple-element.43.refs_1_, bf16[256,256]{1,0:T(8,128)(2,1)S(1)} %collective-permute-done.10.refs_2_, ...), custom_call_target="tpu_custom_call" | custom-call | flops 268435456 | bytes 1245184 | tf_op jit(solution)/shard_map/attend/pallas_call | solution.py:448
  56.0 0.8 %deliver.3.refs_1_ = bf16[1,128,2048]{2,1,0:T(8,128)(2,1)} custom-call(bf16[128,512]{1,0:T(8,128)(2,1)S(1)} %get-tuple-element.56.refs_0_, bf16[128,512]{1,0:T(8,128)(2,1)S(1)} %collective-permute-done.12.refs_1_), custom_call_target="tpu_custom_call" | custom-call | tf_op jit(solution)/shard_map/deliver/pallas_call | solution.py:486
  56.8 1.0 %collective-permute-done.20.refs_0_ = bf16[128,512]{1,0:T(8,128)(2,1)S(1)} collective-permute-done((bf16[128,512]{1,0:T(8,128)(2,1)S(1)}, bf16[128,512]{1,0:T(8,128)(2,1)S(1)}, u32[]{:S(2)}, u32[]{:S(2)}) %collective-permute-start.20) | collective-permute-done | bytes 131104 | tf_op jit(solution)/shard_map/ppermute | solution.py:28
  57.8 0.7 %deliver.4.refs_1_ = bf16[1,128,2048]{2,1,0:T(8,128)(2,1)} custom-call(bf16[128,512]{1,0:T(8,128)(2,1)S(1)} %collective-permute-done.20.refs_0_, bf16[1,128,2048]{2,1,0:T(8,128)(2,1)} %deliver.3.refs_1_), custom_call_target="tpu_custom_call", output_to_operand_aliasing={{}: (1, {})} | custom-call | tf_op jit(solution)/shard_map/deliver/pallas_call | solution.py:486
  58.5 2.4 %collective-permute-done.18.refs_0_ = bf16[128,512]{1,0:T(8,128)(2,1)S(1)} collective-permute-done((bf16[128,512]{1,0:T(8,128)(2,1)S(1)}, bf16[128,512]{1,0:T(8,128)(2,1)S(1)}, u32[]{:S(2)}, u32[]{:S(2)}) %collective-permute-start.18) | collective-permute-done | bytes 131104 | tf_op jit(solution)/shard_map/ppermute | solution.py:28
  60.9 0.7 %deliver.5 = bf16[1,128,2048]{2,1,0:T(8,128)(2,1)} custom-call(bf16[128,512]{1,0:T(8,128)(2,1)S(1)} %collective-permute-done.18.refs_0_, bf16[1,128,2048]{2,1,0:T(8,128)(2,1)} %deliver.4.refs_1_), custom_call_target="tpu_custom_call", output_to_operand_aliasing={{}: (1, {})} | custom-call | tf_op jit(solution)/shard_map/deliver/pallas_call | solution.py:486
  (33 shorter events, 4.2 us)
Async XLA Ops:
  0.1 4.7 %collective-permute-start = (bf16[128,4096]{1,0:T(8,128)(2,1)}, bf16[128,4096]{1,0:T(8,128)(2,1)S(1)}, u32[]{:S(2)}, u32[]{:S(2)}) collective-permute-start(bf16[128,4096]{1,0:T(8,128)(2,1)} %bitcast.7), channel_id=1, source_target_pairs={{0,1},{1,0},{2,3},{3,2},{4,5},{5,4},{6,7},{7,6},{8,9},{9,8},{10,11... | collective-permute-start | bytes 3145736 | tf_op jit(solution)/shard_map/ppermute | solution.py:28
  0.5 26.5 %collective-permute-start.1 = (bf16[128,4096]{1,0:T(8,128)(2,1)}, bf16[128,4096]{1,0:T(8,128)(2,1)S(1)}, u32[]{:S(2)}, u32[]{:S(2)}) collective-permute-start(bf16[128,4096]{1,0:T(8,128)(2,1)} %bitcast.8), channel_id=1, source_target_pairs={{0,2},{1,3},{2,0},{3,1},{4,6},{5,7},{6,4},{7,5},{8,10},{9,11},{10,... | collective-permute-start | bytes 3145736 | tf_op jit(solution)/shard_map/ppermute | solution.py:28
  4.8 6.7 %copy-start = (s32[4,4,4]{2,1,0:T(4,128)S(1)}, s32[4,4,4]{2,1,0:T(4,128)}, u32[]{:S(2)}) copy-start(s32[4,4,4]{2,1,0:T(4,128)} %vertical_ref.1) | copy-start | bytes 772
  4.8 6.7 %copy-start.1 = (s32[4,4,4]{2,1,0:T(4,128)S(1)}, s32[4,4,4]{2,1,0:T(4,128)}, u32[]{:S(2)}) copy-start(s32[4,4,4]{2,1,0:T(4,128)} %slash_ref.1) | copy-start | bytes 772
  9.4 5.6 %collective-permute-start.2 = (bf16[256,256]{1,0:T(8,128)(2,1)S(1)}, bf16[256,256]{1,0:T(8,128)(2,1)S(1)}, u32[]{:S(2)}, u32[]{:S(2)}) collective-permute-start(bf16[256,256]{1,0:T(8,128)(2,1)S(1)} %get-tuple-element.33.refs_1_), channel_id=1, source_target_pairs={{0,8},{8,16},{16,24},{24,28},{28,20},{20,12},{12,4},{4,0},{1,9},{9... | collective-permute-start | bytes 393224 | tf_op jit(solution)/shard_map/ppermute | solution.py:271
  11.1 5.6 %collective-permute-start.5 = (bf16[256,256]{1,0:T(8,128)(2,1)S(1)}, bf16[256,256]{1,0:T(8,128)(2,1)S(1)}, u32[]{:S(2)}, u32[]{:S(2)}) collective-permute-start(bf16[256,256]{1,0:T(8,128)(2,1)S(1)} %get-tuple-element.33.refs_1_), channel_id=1, source_target_pairs={{0,4},{8,0},{16,8},{24,16},{28,24},{20,28},{12,20},{4,12},{1,5},{9... | collective-permute-start | bytes 393224 | tf_op jit(solution)/shard_map/ppermute | solution.py:271
  15.1 5.0 %collective-permute-start.3 = (bf16[256,256]{1,0:T(8,128)(2,1)S(1)}, bf16[256,256]{1,0:T(8,128)(2,1)S(1)}, u32[]{:S(2)}, u32[]{:S(2)}) collective-permute-start(bf16[256,256]{1,0:T(8,128)(2,1)S(1)} %collective-permute-done.2.refs_2_), channel_id=1, source_target_pairs={{0,8},{8,16},{16,24},{24,28},{28,20},{20,12},{12,4},{4,0},{1,9},{9... | collective-permute-start | bytes 393224 | tf_op jit(solution)/shard_map/ppermute | solution.py:271
  16.6 5.0 %collective-permute-start.6 = (bf16[256,256]{1,0:T(8,128)(2,1)S(1)}, bf16[256,256]{1,0:T(8,128)(2,1)S(1)}, u32[]{:S(2)}, u32[]{:S(2)}) collective-permute-start(bf16[256,256]{1,0:T(8,128)(2,1)S(1)} %collective-permute-done.5.refs_3_), channel_id=1, source_target_pairs={{0,4},{8,0},{16,8},{24,16},{28,24},{20,28},{12,20},{4,12},{1,5},{9... | collective-permute-start | bytes 393224 | tf_op jit(solution)/shard_map/ppermute | solution.py:271
  20.0 7.0 %collective-permute-start.4 = (bf16[256,256]{1,0:T(8,128)(2,1)S(1)}, bf16[256,256]{1,0:T(8,128)(2,1)S(1)}, u32[]{:S(2)}, u32[]{:S(2)}) collective-permute-start(bf16[256,256]{1,0:T(8,128)(2,1)S(1)} %collective-permute-done.3.refs_4_), channel_id=1, source_target_pairs={{0,8},{8,16},{16,24},{24,28},{28,20},{20,12},{12,4},{4,0},{1,9},{9... | collective-permute-start | bytes 393224 | tf_op jit(solution)/shard_map/ppermute | solution.py:271
  21.6 5.5 %collective-permute-start.7 = (bf16[256,256]{1,0:T(8,128)(2,1)S(1)}, bf16[256,256]{1,0:T(8,128)(2,1)S(1)}, u32[]{:S(2)}, u32[]{:S(2)}) collective-permute-start(bf16[256,256]{1,0:T(8,128)(2,1)S(1)} %collective-permute-done.6.refs_5_), channel_id=1, source_target_pairs={{0,4},{8,0},{16,8},{24,16},{28,24},{20,28},{12,20},{4,12},{1,5},{9... | collective-permute-start | bytes 393224 | tf_op jit(solution)/shard_map/ppermute | solution.py:271
  27.1 3.1 %collective-permute-start.8 = (bf16[128,4096]{1,0:T(8,128)(2,1)S(1)}, bf16[128,4096]{1,0:T(8,128)(2,1)S(1)}, u32[]{:S(2)}, u32[]{:S(2)}) collective-permute-start(bf16[128,4096]{1,0:T(8,128)(2,1)S(1)} %collective-permute-done.1.token_ref), channel_id=1, source_target_pairs={{0,1},{1,0},{2,3},{3,2},{4,5},{5,4},{6,7},{7,6},{8,9},{9,8},{10,11... | collective-permute-start | bytes 3145736 | tf_op jit(solution)/shard_map/ppermute | solution.py:28
  27.1 6.4 %collective-permute-start.9 = (bf16[256,256]{1,0:T(8,128)(2,1)S(1)}, bf16[256,256]{1,0:T(8,128)(2,1)S(1)}, u32[]{:S(2)}, u32[]{:S(2)}) collective-permute-start(bf16[256,256]{1,0:T(8,128)(2,1)S(1)} %collective-permute-done.4.refs_6_), channel_id=1, source_target_pairs={{0,8},{8,16},{16,24},{24,28},{28,20},{20,12},{12,4},{4,0},{1,9},{9... | collective-permute-start | bytes 393224 | tf_op jit(solution)/shard_map/ppermute | solution.py:271
  31.4 5.6 %collective-permute-start.10 = (bf16[256,256]{1,0:T(8,128)(2,1)S(1)}, bf16[256,256]{1,0:T(8,128)(2,1)S(1)}, u32[]{:S(2)}, u32[]{:S(2)}) collective-permute-start(bf16[256,256]{1,0:T(8,128)(2,1)S(1)} %get-tuple-element.43.refs_1_), channel_id=1, source_target_pairs={{0,8},{8,16},{16,24},{24,28},{28,20},{20,12},{12,4},{4,0},{1,9},{9... | collective-permute-start | bytes 393224 | tf_op jit(solution)/shard_map/ppermute | solution.py:271
  33.1 5.6 %collective-permute-start.11 = (bf16[256,256]{1,0:T(8,128)(2,1)S(1)}, bf16[256,256]{1,0:T(8,128)(2,1)S(1)}, u32[]{:S(2)}, u32[]{:S(2)}) collective-permute-start(bf16[256,256]{1,0:T(8,128)(2,1)S(1)} %get-tuple-element.43.refs_1_), channel_id=1, source_target_pairs={{0,4},{8,0},{16,8},{24,16},{28,24},{20,28},{12,20},{4,12},{1,5},{9... | collective-permute-start | bytes 393224 | tf_op jit(solution)/shard_map/ppermute | solution.py:271
  37.1 5.0 %collective-permute-start.13 = (bf16[256,256]{1,0:T(8,128)(2,1)S(1)}, bf16[256,256]{1,0:T(8,128)(2,1)S(1)}, u32[]{:S(2)}, u32[]{:S(2)}) collective-permute-start(bf16[256,256]{1,0:T(8,128)(2,1)S(1)} %collective-permute-done.10.refs_2_), channel_id=1, source_target_pairs={{0,8},{8,16},{16,24},{24,28},{28,20},{20,12},{12,4},{4,0},{1,9},{9... | collective-permute-start | bytes 393224 | tf_op jit(solution)/shard_map/ppermute | solution.py:271
  38.7 5.0 %collective-permute-start.14 = (bf16[256,256]{1,0:T(8,128)(2,1)S(1)}, bf16[256,256]{1,0:T(8,128)(2,1)S(1)}, u32[]{:S(2)}, u32[]{:S(2)}) collective-permute-start(bf16[256,256]{1,0:T(8,128)(2,1)S(1)} %collective-permute-done.11.refs_3_), channel_id=1, source_target_pairs={{0,4},{8,0},{16,8},{24,16},{28,24},{20,28},{12,20},{4,12},{1,5},{9... | collective-permute-start | bytes 393224 | tf_op jit(solution)/shard_map/ppermute | solution.py:271
  42.0 5.0 %collective-permute-start.15 = (bf16[256,256]{1,0:T(8,128)(2,1)S(1)}, bf16[256,256]{1,0:T(8,128)(2,1)S(1)}, u32[]{:S(2)}, u32[]{:S(2)}) collective-permute-start(bf16[256,256]{1,0:T(8,128)(2,1)S(1)} %collective-permute-done.13.refs_4_), channel_id=1, source_target_pairs={{0,8},{8,16},{16,24},{24,28},{28,20},{20,12},{12,4},{4,0},{1,9},{9... | collective-permute-start | bytes 393224 | tf_op jit(solution)/shard_map/ppermute | solution.py:271
  43.6 6.6 %collective-permute-start.12 = (bf16[128,512]{1,0:T(8,128)(2,1)S(1)}, bf16[128,512]{1,0:T(8,128)(2,1)S(1)}, u32[]{:S(2)}, u32[]{:S(2)}) collective-permute-start(bf16[128,512]{1,0:T(8,128)(2,1)S(1)} %get-tuple-element.47), channel_id=1, source_target_pairs={{0,1},{1,0},{2,3},{3,2},{4,5},{5,4},{6,7},{7,6},{8,9},{9,8},{10,11... | collective-permute-start | bytes 393224 | tf_op jit(solution)/shard_map/ppermute | solution.py:28
  43.6 6.6 %collective-permute-start.16 = (bf16[256,256]{1,0:T(8,128)(2,1)S(1)}, bf16[256,256]{1,0:T(8,128)(2,1)S(1)}, u32[]{:S(2)}, u32[]{:S(2)}) collective-permute-start(bf16[256,256]{1,0:T(8,128)(2,1)S(1)} %collective-permute-done.14.refs_5_), channel_id=1, source_target_pairs={{0,4},{8,0},{16,8},{24,16},{28,24},{20,28},{12,20},{4,12},{1,5},{9... | collective-permute-start | bytes 393224 | tf_op jit(solution)/shard_map/ppermute | solution.py:271
  47.0 4.7 %collective-permute-start.19 = (bf16[128,256]{1,0:T(8,128)(2,1)S(1)}, bf16[128,256]{1,0:T(8,128)(2,1)S(1)}, u32[]{:S(2)}, u32[]{:S(2)}) collective-permute-start(bf16[128,256]{1,0:T(8,128)(2,1)S(1)} %get-tuple-element.57), channel_id=1, source_target_pairs={{0,8},{8,16},{16,24},{24,28},{28,20},{20,12},{12,4},{4,0},{1,9},{9... | collective-permute-start | bytes 196616 | tf_op jit(solution)/shard_map/ppermute | solution.py:259
  48.7 5.6 %collective-permute-start.17 = (bf16[128,256]{1,0:T(8,128)(2,1)S(1)}, bf16[128,256]{1,0:T(8,128)(2,1)S(1)}, u32[]{:S(2)}, u32[]{:S(2)}) collective-permute-start(bf16[128,256]{1,0:T(8,128)(2,1)S(1)} %get-tuple-element.58), channel_id=1, source_target_pairs={{0,8},{8,16},{16,24},{24,28},{28,20},{20,12},{12,4},{4,0},{1,9},{9... | collective-permute-start | bytes 196616 | tf_op jit(solution)/shard_map/ppermute | solution.py:259
  52.8 5.0 %collective-permute-start.20 = (bf16[128,512]{1,0:T(8,128)(2,1)S(1)}, bf16[128,512]{1,0:T(8,128)(2,1)S(1)}, u32[]{:S(2)}, u32[]{:S(2)}) collective-permute-start(bf16[128,512]{1,0:T(8,128)(2,1)S(1)} %attend.7), channel_id=1, source_target_pairs={{0,2},{1,3},{2,0},{3,1},{4,6},{5,7},{6,4},{7,5},{8,10},{9,11},{10,... | collective-permute-start | bytes 393224 | tf_op jit(solution)/shard_map/ppermute | solution.py:28
  55.9 5.0 %collective-permute-start.18 = (bf16[128,512]{1,0:T(8,128)(2,1)S(1)}, bf16[128,512]{1,0:T(8,128)(2,1)S(1)}, u32[]{:S(2)}, u32[]{:S(2)}) collective-permute-start(bf16[128,512]{1,0:T(8,128)(2,1)S(1)} %attend.5), channel_id=1, source_target_pairs={{0,3},{1,2},{2,1},{3,0},{4,7},{5,6},{6,5},{7,4},{8,11},{9,10},{10,... | collective-permute-start | bytes 393224 | tf_op jit(solution)/shard_map/ppermute | solution.py:28

commit v5 on v4

--- a/solution.py
+++ b/solution.py
@@ -52,7 +52,7 @@
         ).astype(jnp.bfloat16)
         return carry
 
-    lax.fori_loop(0, token_ref.shape[0] // BAND, norm_band, 0, unroll=2)
+    lax.fori_loop(0, token_ref.shape[0] // BAND, norm_band, 0, unroll=4)
 
 
 def rotate(value, table_ref):
@@ -276,7 +276,8 @@
 
 def plan_kernel(ring, lanes, heads, count, rows, info_ref, vertical_ref, slash_ref, plan_ref):
     place, me = info_ref[0], info_ref[1]
-    plan_ref[0] = place
+    row_at = lax.broadcasted_iota(jnp.int32, (1, rows), 1)
+    query_at = place * rows + jnp.concatenate([row_at] * QUERY_GROUP, axis=1)
 
     def enter(number, block):
         for lane in range(lanes):
@@ -288,8 +289,8 @@
                     found = found | (block == place - slash_ref[doc, group, s])
                 for s in range(vertical_ref.shape[2]):
                     found = found | ((block == vertical_ref[doc, group, s]) & (block < place - 1))
-                at = 1 + (lane * heads + head) * count + number
-                plan_ref[at] = jnp.where(found & (block >= 0), block * rows, OUT_OF_REACH)
+                shift = jnp.where(found & (block >= 0), block * rows, OUT_OF_REACH)
+                plan_ref[pl.ds((lane * heads + head) * count + number, 1), :] = query_at - shift
 
     if ring:
         order = ring_order(count)
@@ -311,12 +312,11 @@
 def plan(info, vertical, slash, ring, rows):
     count, lanes = lax.axis_size("seq"), lax.axis_size("doc")
     heads = vertical.shape[1] // lanes
-    length = 1 + lanes * heads * count
     return pl.pallas_call(
         functools.partial(plan_kernel, ring, lanes, heads, count, rows),
         in_specs=[SMEM] * 3,
-        out_specs=SMEM,
-        out_shape=jax.ShapeDtypeStruct((length,), jnp.int32),
+        out_specs=VMEM,
+        out_shape=jax.ShapeDtypeStruct((lanes * heads * count, QUERY_GROUP * rows), jnp.int32),
         compiler_params=pltpu.CompilerParams(vmem_limit_bytes=4 * MIB),
         name="plan",
     )(info, vertical, slash)
@@ -327,16 +327,13 @@
     state_refs = refs[:0 if begin else 3 * len(lanes)]
     out_refs = refs[len(state_refs):]
     heads = kv_refs[0].shape[1] // (2 * HEAD_WIDTH)
-    place = plan_ref[0]
     factor = HEAD_WIDTH ** (-0.5) * math.log2(math.e)
 
     for lane, (mask, q_at, kv_first, rows) in enumerate(lanes):
         rank = QUERY_GROUP * rows
-        row_at = place * rows + lax.broadcasted_iota(jnp.int32, (1, rows), 1)
-        query_at = jnp.concatenate([row_at] * QUERY_GROUP, axis=1)
         key_at = lax.broadcasted_iota(jnp.int32, (rows, rank), 0)
         for head in range(heads):
-            table = 1 + (mask * heads + head) * stride + slot_at
+            table = (mask * heads + head) * stride + slot_at
             queries = jnp.concatenate(
                 [
                     q_refs[q_at[0]][
@@ -368,10 +365,10 @@
                 )
                 parts = []
                 for j in range(len(slots)):
-                    shift = plan_ref[table + index * len(slots) + j]
+                    limit = plan_ref[pl.ds(table + index * len(slots) + j, 1), :]
                     parts.append(
                         jnp.where(
-                            key_at <= query_at - shift,
+                            key_at <= limit,
                             scores[j * rows:(j + 1) * rows],
                             -jnp.inf,
                         )
@@ -447,7 +444,7 @@
     )
     return pl.pallas_call(
         kernel,
-        in_specs=[SMEM] + [VMEM] * (len(queries) + len(arrays) + len(held)),
+        in_specs=[VMEM] * (1 + len(queries) + len(arrays) + len(held)),
         out_specs=[VMEM] * len(shapes),
         out_shape=shapes,
         compiler_params=pltpu.CompilerParams(
@@ -535,10 +532,9 @@
         near.slots,
         near.chunks,
     )
-    out_twin = swap(mixed_twin, "doc", 1)
     far.advance(q_far)
     far.advance(mixed_twin)
-    q_far = after(q_far, out_twin)
+    out_twin = swap(after(mixed_twin, *far.latest), "doc", 1)
     remote = [(2, (0, 0), 0, rows), (3, (0, rows), rows, rows)]
     if long:
         mixed = attend(table_of, remote, [q_far], far.arrays, far.slots, far.chunks)
@@ -551,14 +547,14 @@
             table_of, remote[:1], [q_far], ends[:1], [lambda index: (0, 0)], first=count, states=[state]
         )
         home = [swap(mixed, "doc", 2)]
-        (mixed,) = attend(
+        mixed = attend(
             table_of,
             remote[1:],
             [q_far],
             [*far.arrays, ends[1]],
             [*far.slots, lambda index: (count, -rows)],
         )
-        home.append(swap(mixed, "doc", 3))
+        home.append(swap(mixed[0], "doc", 3))
     count = lax.axis_size("doc")
     result = deliver((0, 1), [mixed_own, out_twin], count)
     result = deliver((2,), home[:1], count, before=result)

time: 61.7 us -> 61 us (0.989)
  Pallas kernels: 18.9 us -> 16 us
  waiting for transfers between devices: 18.7 us -> 20.7 us
    pallas_call x4, Pallas kernels: 6.6 us -> 4.63 us  [attend(): pl.pallas_call(kernel, in_specs=[VMEM] * (1 + len(queries) + len(arrays)...]
    ppermute x13, waiting for transfers between devices: 10.2 us -> 11.5 us  [advance(): self.front[way] = lax.ppermute(value, 'seq', pairs)]
  transfers between devices with their start and end apart: 21 -> 21, of which waited for: 8 -> 9; matrix products, arithmetic and copies ran while one was open for 3% -> 3% of each run, Pallas kernels for 30% -> 25%
where the time goes in v5:
time: 61 us; the launch traced here: 60.9 us
  starting transfers between devices  22.3 us (37%)
  waiting for transfers between devices  20.7 us (34%)
  Pallas kernels  16 us (26%)
  other arithmetic  1.16 us (2%)
  local copies, waits for them, and re-layouts  0.61 us (1%)
    ppermute x13, starting transfers between devices, advance(): self.front[way] = lax.ppermute(value, 'seq', pairs)  14.2 us
    ppermute x13, waiting for transfers between devices, advance(): self.front[way] = lax.ppermute(value, 'seq', pairs)  11.5 us
    ppermute x6, waiting for transfers between devices, swap(): lax.ppermute(value, axis, [(source, source ^ mask) for source in range(co...  9.03 us
    pallas_call x4, Pallas kernels, project_call(): pl.pallas_call(kernel, in_specs=kinds, out_specs=[VMEM] * len(shapes), ou...  7.98 us
    ppermute x6, starting transfers between devices, swap(): lax.ppermute(value, axis, [(source, source ^ mask) for source in range(co...  4.93 us
    pallas_call x4, Pallas kernels, attend(): pl.pallas_call(kernel, in_specs=[VMEM] * (1 + len(queries) + len(arrays)...  4.63 us
    ppermute x2, starting transfers between devices, last(): return lax.ppermute(array, 'seq', pairs)  3.21 us
    pallas_call x3, Pallas kernels, deliver(): pl.pallas_call(functools.partial(deliver_kernel, masks), in_specs=[VMEM]...  2.12 us
  transfers between devices with their start and end apart: 21, of which 9 were waited for; matrix products, arithmetic and copies ran while one was open for 3% of the time, Pallas kernels for 25%

profile of v5, /device:TPU:0, one launch (start us, length us, event | category | flops | bytes accessed | tf_op | source)
XLA Modules:
  0.0 60.9 jit_solution(13704887978340273863)
XLA Ops:
  0.5 2.6 %collective-permute-start.1 = (bf16[128,4096]{1,0:T(8,128)(2,1)}, bf16[128,4096]{1,0:T(8,128)(2,1)S(1)}, u32[]{:S(2)}, u32[]{:S(2)}) collective-permute-start(bf16[128,4096]{1,0:T(8,128)(2,1)} %bitcast.8), channel_id=1, source_target_pairs={{0,2},{1,3},{2,0},{3,1},{4,6},{5,7},{6,4},{7,5},{8,10},{9,11},{10,... | collective-permute-start | bytes 3145736 | tf_op jit(solution)/shard_map/ppermute | solution.py:28
  3.1 0.6 slice.9
  3.7 0.6 %add_convert_fusion = f32[128]{0:T(128)S(1)} fusion(s32[]{:T(128)} %bitcast.5), kind=kLoop, calls=%fused_computation.6 | loop fusion | flops 256 | bytes 516 | tf_op jit(solution)/shard_map/convert_element_type | solution.py:41
  4.8 4.6 %project_near.1 = (bf16[256,512]{1,0:T(8,128)(2,1)S(1)}, bf16[256,256]{1,0:T(8,128)(2,1)S(1)}, f32[1,4096]{1,0:T(1,128)S(1)}, bf16[4096,512]{1,0:T(8,128)(2,1)S(...) custom-call(bf16[128,4096]{1,0:T(8,128)(2,1)} %bitcast.9, ...), custom_call_target="tpu_custom_call" | custom-call | flops 1610612736 | bytes 8388608 | tf_op jit(solution)/shard_map/project_near/pallas_call | solution.py:147
  9.4 1.6 %collective-permute-start.2 = (bf16[256,256]{1,0:T(8,128)(2,1)S(1)}, bf16[256,256]{1,0:T(8,128)(2,1)S(1)}, u32[]{:S(2)}, u32[]{:S(2)}) collective-permute-start(bf16[256,256]{1,0:T(8,128)(2,1)S(1)} %get-tuple-element.33.refs_1_), channel_id=1, source_target_pairs={{0,8},{8,16},{16,24},{24,28},{28,20},{20,12},{12,4},{4,0},{1,9},{9... | collective-permute-start | bytes 393224 | tf_op jit(solution)/shard_map/ppermute | solution.py:271
  11.5 1.2 %plan.1.plan_ref = s32[32,512]{1,0:T(8,128)S(1)} custom-call(s32[3]{0:T(128)S(1)} %pad_add_fusion.info_ref, s32[4,4,4]{2,1,0:T(4,128)S(1)} %copy-done, s32[4,4,4]{2,1,0:T(4,128)S(1)} %copy-done.1), custom_call_target="tpu_custom_call" | custom-call | tf_op jit(solution)/shard_map/plan/pallas_call | solution.py:315
  12.8 2.3 %collective-permute-done.2.refs_2_ = bf16[256,256]{1,0:T(8,128)(2,1)S(1)} collective-permute-done((bf16[256,256]{1,0:T(8,128)(2,1)S(1)}, bf16[256,256]{1,0:T(8,128)(2,1)S(1)}, u32[]{:S(2)}, u32[]{:S(2)}) %collective-permute-start.2) | collective-permute-done | bytes 131104 | tf_op jit(solution)/shard_map/ppermute | solution.py:271
  15.1 1.6 %collective-permute-start.3 = (bf16[256,256]{1,0:T(8,128)(2,1)S(1)}, bf16[256,256]{1,0:T(8,128)(2,1)S(1)}, u32[]{:S(2)}, u32[]{:S(2)}) collective-permute-start(bf16[256,256]{1,0:T(8,128)(2,1)S(1)} %collective-permute-done.2.refs_2_), channel_id=1, source_target_pairs={{0,8},{8,16},{16,24},{24,28},{28,20},{20,12},{12,4},{4,0},{1,9},{9... | collective-permute-start | bytes 393224 | tf_op jit(solution)/shard_map/ppermute | solution.py:271
  17.1 2.9 %collective-permute-done.3.refs_4_ = bf16[256,256]{1,0:T(8,128)(2,1)S(1)} collective-permute-done((bf16[256,256]{1,0:T(8,128)(2,1)S(1)}, bf16[256,256]{1,0:T(8,128)(2,1)S(1)}, u32[]{:S(2)}, u32[]{:S(2)}) %collective-permute-start.3) | collective-permute-done | bytes 131104 | tf_op jit(solution)/shard_map/ppermute | solution.py:271
  20.0 1.6 %collective-permute-start.4 = (bf16[256,256]{1,0:T(8,128)(2,1)S(1)}, bf16[256,256]{1,0:T(8,128)(2,1)S(1)}, u32[]{:S(2)}, u32[]{:S(2)}) collective-permute-start(bf16[256,256]{1,0:T(8,128)(2,1)S(1)} %collective-permute-done.3.refs_4_), channel_id=1, source_target_pairs={{0,8},{8,16},{16,24},{24,28},{28,20},{20,12},{12,4},{4,0},{1,9},{9... | collective-permute-start | bytes 393224 | tf_op jit(solution)/shard_map/ppermute | solution.py:271
  22.1 5.0 %collective-permute-done.1.token_ref = bf16[128,4096]{1,0:T(8,128)(2,1)S(1)} collective-permute-done((bf16[128,4096]{1,0:T(8,128)(2,1)}, bf16[128,4096]{1,0:T(8,128)(2,1)S(1)}, u32[]{:S(2)}, u32[]{:S(2)}) %collective-permute-start.1) | collective-permute-done | bytes 1048608 | tf_op jit(solution)/shard_map/ppermute | solution.py:28
  27.1 1.9 %collective-permute-start.9 = (bf16[256,256]{1,0:T(8,128)(2,1)S(1)}, bf16[256,256]{1,0:T(8,128)(2,1)S(1)}, u32[]{:S(2)}, u32[]{:S(2)}) collective-permute-start(bf16[256,256]{1,0:T(8,128)(2,1)S(1)} %collective-permute-done.4.refs_6_), channel_id=1, source_target_pairs={{0,8},{8,16},{16,24},{24,28},{28,20},{20,12},{12,4},{4,0},{1,9},{9... | collective-permute-start | bytes 393224 | tf_op jit(solution)/shard_map/ppermute | solution.py:271
  29.0 1.0 %project_keys_values.2 = (bf16[128,256]{1,0:T(8,128)(2,1)S(1)}, bf16[128,4096]{1,0:T(8,128)(2,1)S(1)}) custom-call(bf16[128,4096]{1,0:T(8,128)(2,1)S(1)} %collective-permute-done.1.token_ref, f32[1,4096]{1,0:T(1,128)S(1)} %get-tuple-element.37.gain_ref, bf16[4096,128]{1,0:T(8,128)(2,1)S(1)} %get-tuple-element.38.wk_ref, ...), custom_call_target="tpu_custom_call" | custom-call | flops 268435456 | bytes 3145728 | tf_op jit(solution)/shard_map/project_keys_values/pallas_call | solution.py:147
  30.0 1.0 %project_keys_values.3 = (bf16[256,256]{1,0:T(8,128)(2,1)S(1)}, bf16[128,4096]{1,0:T(8,128)(2,1)S(1)}) custom-call(bf16[128,4096]{1,0:T(8,128)(2,1)S(1)} %collective-permute-done.8.token_ref, f32[1,4096]{1,0:T(1,128)S(1)} %get-tuple-element.37.gain_ref, bf16[4096,128]{1,0:T(8,128)(2,1)S(1)} %get-tuple-element.38.wk_ref, ...), custom_call_target="tpu_custom_call" | custom-call | flops 268435456 | bytes 3145728 | tf_op jit(solution)/shard_map/project_keys_values/pallas_call | solution.py:147
  31.0 1.6 %collective-permute-start.10 = (bf16[256,256]{1,0:T(8,128)(2,1)S(1)}, bf16[256,256]{1,0:T(8,128)(2,1)S(1)}, u32[]{:S(2)}, u32[]{:S(2)}) collective-permute-start(bf16[256,256]{1,0:T(8,128)(2,1)S(1)} %get-tuple-element.43.refs_1_), channel_id=1, source_target_pairs={{0,8},{8,16},{16,24},{24,28},{28,20},{20,12},{12,4},{4,0},{1,9},{9... | collective-permute-start | bytes 393224 | tf_op jit(solution)/shard_map/ppermute | solution.py:271
  33.1 1.4 %project_queries.1.refs_0_ = bf16[256,512]{1,0:T(8,128)(2,1)S(1)} custom-call(bf16[4096,512]{1,0:T(8,128)(2,1)S(1)} %get-tuple-element.32.wq_ref, f32[128,256]{1,0:T(8,128)S(1)} %pad_maximum_fusion.table_ref, bf16[128,4096]{1,0:T(8,128)(2,1)S(1)} %get-tuple-element.40.refs_0_, bf16[128,4096]{1,0:T(8,128)(2,1)S(1)} %get-tuple-element.44.refs_1_), custom_call_target="tpu_custom_call" | custom-call | flops 1073741824 | bytes 6291456 | tf_op jit(solution)/shard_map/project_queries/pallas_call | solution.py:147
  34.5 2.2 %collective-permute-done.10.refs_2_ = bf16[256,256]{1,0:T(8,128)(2,1)S(1)} collective-permute-done((bf16[256,256]{1,0:T(8,128)(2,1)S(1)}, bf16[256,256]{1,0:T(8,128)(2,1)S(1)}, u32[]{:S(2)}, u32[]{:S(2)}) %collective-permute-start.10) | collective-permute-done | bytes 131104 | tf_op jit(solution)/shard_map/ppermute | solution.py:271
  36.6 1.6 %collective-permute-start.12 = (bf16[256,256]{1,0:T(8,128)(2,1)S(1)}, bf16[256,256]{1,0:T(8,128)(2,1)S(1)}, u32[]{:S(2)}, u32[]{:S(2)}) collective-permute-start(bf16[256,256]{1,0:T(8,128)(2,1)S(1)} %collective-permute-done.10.refs_2_), channel_id=1, source_target_pairs={{0,8},{8,16},{16,24},{24,28},{28,20},{20,12},{12,4},{4,0},{1,9},{9... | collective-permute-start | bytes 393224 | tf_op jit(solution)/shard_map/ppermute | solution.py:271
  38.7 2.0 %attend.4 = (bf16[128,512]{1,0:T(8,128)(2,1)S(1)}, bf16[128,512]{1,0:T(8,128)(2,1)S(1)}) custom-call(s32[32,512]{1,0:T(8,128)S(1)} %plan.1.plan_ref, bf16[256,512]{1,0:T(8,128)(2,1)S(1)} %get-tuple-element.48.refs_0_, bf16[256,256]{1,0:T(8,128)(2,1)S(1)} %get-tuple-element.33.refs_1_, bf16[256,256]{1,0:T(8,128)(2,1)S(1)} %collective-permute-done.2.refs_2_, ...), custom_call_target="tpu_custom_call" | custom-call | flops 536870912 | bytes 1572864 | tf_op jit(solution)/shard_map/attend/pallas_call | solution.py:445
  40.7 0.9 %collective-permute-done.12.refs_4_ = bf16[256,256]{1,0:T(8,128)(2,1)S(1)} collective-permute-done((bf16[256,256]{1,0:T(8,128)(2,1)S(1)}, bf16[256,256]{1,0:T(8,128)(2,1)S(1)}, u32[]{:S(2)}, u32[]{:S(2)}) %collective-permute-start.12) | collective-permute-done | bytes 131104 | tf_op jit(solution)/shard_map/ppermute | solution.py:271
  41.6 1.6 %collective-permute-start.14 = (bf16[256,256]{1,0:T(8,128)(2,1)S(1)}, bf16[256,256]{1,0:T(8,128)(2,1)S(1)}, u32[]{:S(2)}, u32[]{:S(2)}) collective-permute-start(bf16[256,256]{1,0:T(8,128)(2,1)S(1)} %collective-permute-done.12.refs_4_), channel_id=1, source_target_pairs={{0,8},{8,16},{16,24},{24,28},{28,20},{20,12},{12,4},{4,0},{1,9},{9... | collective-permute-start | bytes 393224 | tf_op jit(solution)/shard_map/ppermute | solution.py:271
  43.6 3.2 %collective-permute-done.14.refs_6_ = bf16[256,256]{1,0:T(8,128)(2,1)S(1)} collective-permute-done((bf16[256,256]{1,0:T(8,128)(2,1)S(1)}, bf16[256,256]{1,0:T(8,128)(2,1)S(1)}, u32[]{:S(2)}, u32[]{:S(2)}) %collective-permute-start.14) | collective-permute-done | bytes 131104 | tf_op jit(solution)/shard_map/ppermute | solution.py:271
  46.9 1.6 %collective-permute-start.18 = (bf16[128,256]{1,0:T(8,128)(2,1)S(1)}, bf16[128,256]{1,0:T(8,128)(2,1)S(1)}, u32[]{:S(2)}, u32[]{:S(2)}) collective-permute-start(bf16[128,256]{1,0:T(8,128)(2,1)S(1)} %get-tuple-element.57), channel_id=1, source_target_pairs={{0,8},{8,16},{16,24},{24,28},{28,20},{20,12},{12,4},{4,0},{1,9},{9... | collective-permute-start | bytes 196616 | tf_op jit(solution)/shard_map/ppermute | solution.py:259
  48.5 1.6 %collective-permute-start.16 = (bf16[128,256]{1,0:T(8,128)(2,1)S(1)}, bf16[128,256]{1,0:T(8,128)(2,1)S(1)}, u32[]{:S(2)}, u32[]{:S(2)}) collective-permute-start(bf16[128,256]{1,0:T(8,128)(2,1)S(1)} %get-tuple-element.58), channel_id=1, source_target_pairs={{0,8},{8,16},{16,24},{24,28},{28,20},{20,12},{12,4},{4,0},{1,9},{9... | collective-permute-start | bytes 196616 | tf_op jit(solution)/shard_map/ppermute | solution.py:259
  50.1 1.0 %attend.6 = (f32[1,1,512]{2,1,0:T(1,128)S(1)}, f32[1,1,512]{2,1,0:T(1,128)S(1)}, f32[1,128,512]{2,1,0:T(8,128)S(1)}) custom-call(s32[32,512]{1,0:T(8,128)S(1)} %plan.1.plan_ref, bf16[256,512]{1,0:T(8,128)(2,1)S(1)} %project_queries.1.refs_0_, bf16[256,256]{1,0:T(8,128)(2,1)S(1)} %get-tuple-element.43.refs_1_, ...), custom_call_target="tpu_custom_call" | custom-call | flops 234881024 | bytes 1179648 | tf_op jit(solution)/shard_map/attend/pallas_call | solution.py:445
  51.7 1.6 %collective-permute-start.19 = (bf16[128,512]{1,0:T(8,128)(2,1)S(1)}, bf16[128,512]{1,0:T(8,128)(2,1)S(1)}, u32[]{:S(2)}, u32[]{:S(2)}) collective-permute-start(bf16[128,512]{1,0:T(8,128)(2,1)S(1)} %attend.7), channel_id=1, source_target_pairs={{0,2},{1,3},{2,0},{3,1},{4,6},{5,7},{6,4},{7,5},{8,10},{9,11},{10,... | collective-permute-start | bytes 393224 | tf_op jit(solution)/shard_map/ppermute | solution.py:28
  53.3 1.1 %attend.5 = bf16[128,512]{1,0:T(8,128)(2,1)S(1)} custom-call(s32[32,512]{1,0:T(8,128)S(1)} %plan.1.plan_ref, bf16[256,512]{1,0:T(8,128)(2,1)S(1)} %project_queries.1.refs_0_, bf16[256,256]{1,0:T(8,128)(2,1)S(1)} %get-tuple-element.43.refs_1_, bf16[256,256]{1,0:T(8,128)(2,1)S(1)} %collective-permute-done.10.refs_2_, ...), custom_call_target="tpu_custom_call" | custom-call | flops 268435456 | bytes 1245184 | tf_op jit(solution)/shard_map/attend/pallas_call | solution.py:445
  54.7 0.8 %deliver.3.refs_1_ = bf16[1,128,2048]{2,1,0:T(8,128)(2,1)} custom-call(bf16[128,512]{1,0:T(8,128)(2,1)S(1)} %get-tuple-element.55.refs_0_, bf16[128,512]{1,0:T(8,128)(2,1)S(1)} %collective-permute-done.20.refs_1_), custom_call_target="tpu_custom_call" | custom-call | tf_op jit(solution)/shard_map/deliver/pallas_call | solution.py:483
  55.5 2.1 %collective-permute-done.19.refs_0_ = bf16[128,512]{1,0:T(8,128)(2,1)S(1)} collective-permute-done((bf16[128,512]{1,0:T(8,128)(2,1)S(1)}, bf16[128,512]{1,0:T(8,128)(2,1)S(1)}, u32[]{:S(2)}, u32[]{:S(2)}) %collective-permute-start.19) | collective-permute-done | bytes 131104 | tf_op jit(solution)/shard_map/ppermute | solution.py:28
  57.6 0.7 %deliver.4.refs_1_ = bf16[1,128,2048]{2,1,0:T(8,128)(2,1)} custom-call(bf16[128,512]{1,0:T(8,128)(2,1)S(1)} %collective-permute-done.19.refs_0_, bf16[1,128,2048]{2,1,0:T(8,128)(2,1)} %deliver.3.refs_1_), custom_call_target="tpu_custom_call", output_to_operand_aliasing={{}: (1, {})} | custom-call | tf_op jit(solution)/shard_map/deliver/pallas_call | solution.py:483
  58.3 1.9 %collective-permute-done.17.refs_0_ = bf16[128,512]{1,0:T(8,128)(2,1)S(1)} collective-permute-done((bf16[128,512]{1,0:T(8,128)(2,1)S(1)}, bf16[128,512]{1,0:T(8,128)(2,1)S(1)}, u32[]{:S(2)}, u32[]{:S(2)}) %collective-permute-start.17) | collective-permute-done | bytes 131104 | tf_op jit(solution)/shard_map/ppermute | solution.py:28
  60.2 0.7 %deliver.5 = bf16[1,128,2048]{2,1,0:T(8,128)(2,1)} custom-call(bf16[128,512]{1,0:T(8,128)(2,1)S(1)} %collective-permute-done.17.refs_0_, bf16[1,128,2048]{2,1,0:T(8,128)(2,1)} %deliver.4.refs_1_), custom_call_target="tpu_custom_call", output_to_operand_aliasing={{}: (1, {})} | custom-call | tf_op jit(solution)/shard_map/deliver/pallas_call | solution.py:483
  (33 shorter events, 4.6 us)
Async XLA Ops:
  0.1 4.7 %collective-permute-start = (bf16[128,4096]{1,0:T(8,128)(2,1)}, bf16[128,4096]{1,0:T(8,128)(2,1)S(1)}, u32[]{:S(2)}, u32[]{:S(2)}) collective-permute-start(bf16[128,4096]{1,0:T(8,128)(2,1)} %bitcast.7), channel_id=1, source_target_pairs={{0,1},{1,0},{2,3},{3,2},{4,5},{5,4},{6,7},{7,6},{8,9},{9,8},{10,11... | collective-permute-start | bytes 3145736 | tf_op jit(solution)/shard_map/ppermute | solution.py:28
  0.5 26.5 %collective-permute-start.1 = (bf16[128,4096]{1,0:T(8,128)(2,1)}, bf16[128,4096]{1,0:T(8,128)(2,1)S(1)}, u32[]{:S(2)}, u32[]{:S(2)}) collective-permute-start(bf16[128,4096]{1,0:T(8,128)(2,1)} %bitcast.8), channel_id=1, source_target_pairs={{0,2},{1,3},{2,0},{3,1},{4,6},{5,7},{6,4},{7,5},{8,10},{9,11},{10,... | collective-permute-start | bytes 3145736 | tf_op jit(solution)/shard_map/ppermute | solution.py:28
  4.8 6.7 %copy-start = (s32[4,4,4]{2,1,0:T(4,128)S(1)}, s32[4,4,4]{2,1,0:T(4,128)}, u32[]{:S(2)}) copy-start(s32[4,4,4]{2,1,0:T(4,128)} %vertical_ref.1) | copy-start | bytes 772
  4.8 6.7 %copy-start.1 = (s32[4,4,4]{2,1,0:T(4,128)S(1)}, s32[4,4,4]{2,1,0:T(4,128)}, u32[]{:S(2)}) copy-start(s32[4,4,4]{2,1,0:T(4,128)} %slash_ref.1) | copy-start | bytes 772
  9.4 5.6 %collective-permute-start.2 = (bf16[256,256]{1,0:T(8,128)(2,1)S(1)}, bf16[256,256]{1,0:T(8,128)(2,1)S(1)}, u32[]{:S(2)}, u32[]{:S(2)}) collective-permute-start(bf16[256,256]{1,0:T(8,128)(2,1)S(1)} %get-tuple-element.33.refs_1_), channel_id=1, source_target_pairs={{0,8},{8,16},{16,24},{24,28},{28,20},{20,12},{12,4},{4,0},{1,9},{9... | collective-permute-start | bytes 393224 | tf_op jit(solution)/shard_map/ppermute | solution.py:271
  11.1 5.6 %collective-permute-start.5 = (bf16[256,256]{1,0:T(8,128)(2,1)S(1)}, bf16[256,256]{1,0:T(8,128)(2,1)S(1)}, u32[]{:S(2)}, u32[]{:S(2)}) collective-permute-start(bf16[256,256]{1,0:T(8,128)(2,1)S(1)} %get-tuple-element.33.refs_1_), channel_id=1, source_target_pairs={{0,4},{8,0},{16,8},{24,16},{28,24},{20,28},{12,20},{4,12},{1,5},{9... | collective-permute-start | bytes 393224 | tf_op jit(solution)/shard_map/ppermute | solution.py:271
  15.1 5.0 %collective-permute-start.3 = (bf16[256,256]{1,0:T(8,128)(2,1)S(1)}, bf16[256,256]{1,0:T(8,128)(2,1)S(1)}, u32[]{:S(2)}, u32[]{:S(2)}) collective-permute-start(bf16[256,256]{1,0:T(8,128)(2,1)S(1)} %collective-permute-done.2.refs_2_), channel_id=1, source_target_pairs={{0,8},{8,16},{16,24},{24,28},{28,20},{20,12},{12,4},{4,0},{1,9},{9... | collective-permute-start | bytes 393224 | tf_op jit(solution)/shard_map/ppermute | solution.py:271
  16.6 5.0 %collective-permute-start.6 = (bf16[256,256]{1,0:T(8,128)(2,1)S(1)}, bf16[256,256]{1,0:T(8,128)(2,1)S(1)}, u32[]{:S(2)}, u32[]{:S(2)}) collective-permute-start(bf16[256,256]{1,0:T(8,128)(2,1)S(1)} %collective-permute-done.5.refs_3_), channel_id=1, source_target_pairs={{0,4},{8,0},{16,8},{24,16},{28,24},{20,28},{12,20},{4,12},{1,5},{9... | collective-permute-start | bytes 393224 | tf_op jit(solution)/shard_map/ppermute | solution.py:271
  20.0 7.0 %collective-permute-start.4 = (bf16[256,256]{1,0:T(8,128)(2,1)S(1)}, bf16[256,256]{1,0:T(8,128)(2,1)S(1)}, u32[]{:S(2)}, u32[]{:S(2)}) collective-permute-start(bf16[256,256]{1,0:T(8,128)(2,1)S(1)} %collective-permute-done.3.refs_4_), channel_id=1, source_target_pairs={{0,8},{8,16},{16,24},{24,28},{28,20},{20,12},{12,4},{4,0},{1,9},{9... | collective-permute-start | bytes 393224 | tf_op jit(solution)/shard_map/ppermute | solution.py:271
  21.6 5.5 %collective-permute-start.7 = (bf16[256,256]{1,0:T(8,128)(2,1)S(1)}, bf16[256,256]{1,0:T(8,128)(2,1)S(1)}, u32[]{:S(2)}, u32[]{:S(2)}) collective-permute-start(bf16[256,256]{1,0:T(8,128)(2,1)S(1)} %collective-permute-done.6.refs_5_), channel_id=1, source_target_pairs={{0,4},{8,0},{16,8},{24,16},{28,24},{20,28},{12,20},{4,12},{1,5},{9... | collective-permute-start | bytes 393224 | tf_op jit(solution)/shard_map/ppermute | solution.py:271
  27.1 2.9 %collective-permute-start.8 = (bf16[128,4096]{1,0:T(8,128)(2,1)S(1)}, bf16[128,4096]{1,0:T(8,128)(2,1)S(1)}, u32[]{:S(2)}, u32[]{:S(2)}) collective-permute-start(bf16[128,4096]{1,0:T(8,128)(2,1)S(1)} %collective-permute-done.1.token_ref), channel_id=1, source_target_pairs={{0,1},{1,0},{2,3},{3,2},{4,5},{5,4},{6,7},{7,6},{8,9},{9,8},{10,11... | collective-permute-start | bytes 3145736 | tf_op jit(solution)/shard_map/ppermute | solution.py:28
  27.1 6.0 %collective-permute-start.9 = (bf16[256,256]{1,0:T(8,128)(2,1)S(1)}, bf16[256,256]{1,0:T(8,128)(2,1)S(1)}, u32[]{:S(2)}, u32[]{:S(2)}) collective-permute-start(bf16[256,256]{1,0:T(8,128)(2,1)S(1)} %collective-permute-done.4.refs_6_), channel_id=1, source_target_pairs={{0,8},{8,16},{16,24},{24,28},{28,20},{20,12},{12,4},{4,0},{1,9},{9... | collective-permute-start | bytes 393224 | tf_op jit(solution)/shard_map/ppermute | solution.py:271
  31.0 5.6 %collective-permute-start.10 = (bf16[256,256]{1,0:T(8,128)(2,1)S(1)}, bf16[256,256]{1,0:T(8,128)(2,1)S(1)}, u32[]{:S(2)}, u32[]{:S(2)}) collective-permute-start(bf16[256,256]{1,0:T(8,128)(2,1)S(1)} %get-tuple-element.43.refs_1_), channel_id=1, source_target_pairs={{0,8},{8,16},{16,24},{24,28},{28,20},{20,12},{12,4},{4,0},{1,9},{9... | collective-permute-start | bytes 393224 | tf_op jit(solution)/shard_map/ppermute | solution.py:271
  32.6 5.6 %collective-permute-start.11 = (bf16[256,256]{1,0:T(8,128)(2,1)S(1)}, bf16[256,256]{1,0:T(8,128)(2,1)S(1)}, u32[]{:S(2)}, u32[]{:S(2)}) collective-permute-start(bf16[256,256]{1,0:T(8,128)(2,1)S(1)} %get-tuple-element.43.refs_1_), channel_id=1, source_target_pairs={{0,4},{8,0},{16,8},{24,16},{28,24},{20,28},{12,20},{4,12},{1,5},{9... | collective-permute-start | bytes 393224 | tf_op jit(solution)/shard_map/ppermute | solution.py:271
  36.6 5.0 %collective-permute-start.12 = (bf16[256,256]{1,0:T(8,128)(2,1)S(1)}, bf16[256,256]{1,0:T(8,128)(2,1)S(1)}, u32[]{:S(2)}, u32[]{:S(2)}) collective-permute-start(bf16[256,256]{1,0:T(8,128)(2,1)S(1)} %collective-permute-done.10.refs_2_), channel_id=1, source_target_pairs={{0,8},{8,16},{16,24},{24,28},{28,20},{20,12},{12,4},{4,0},{1,9},{9... | collective-permute-start | bytes 393224 | tf_op jit(solution)/shard_map/ppermute | solution.py:271
  38.2 5.0 %collective-permute-start.13 = (bf16[256,256]{1,0:T(8,128)(2,1)S(1)}, bf16[256,256]{1,0:T(8,128)(2,1)S(1)}, u32[]{:S(2)}, u32[]{:S(2)}) collective-permute-start(bf16[256,256]{1,0:T(8,128)(2,1)S(1)} %collective-permute-done.11.refs_3_), channel_id=1, source_target_pairs={{0,4},{8,0},{16,8},{24,16},{28,24},{20,28},{12,20},{4,12},{1,5},{9... | collective-permute-start | bytes 393224 | tf_op jit(solution)/shard_map/ppermute | solution.py:271
  41.6 5.2 %collective-permute-start.14 = (bf16[256,256]{1,0:T(8,128)(2,1)S(1)}, bf16[256,256]{1,0:T(8,128)(2,1)S(1)}, u32[]{:S(2)}, u32[]{:S(2)}) collective-permute-start(bf16[256,256]{1,0:T(8,128)(2,1)S(1)} %collective-permute-done.12.refs_4_), channel_id=1, source_target_pairs={{0,8},{8,16},{16,24},{24,28},{28,20},{20,12},{12,4},{4,0},{1,9},{9... | collective-permute-start | bytes 393224 | tf_op jit(solution)/shard_map/ppermute | solution.py:271
  43.2 6.9 %collective-permute-start.15 = (bf16[256,256]{1,0:T(8,128)(2,1)S(1)}, bf16[256,256]{1,0:T(8,128)(2,1)S(1)}, u32[]{:S(2)}, u32[]{:S(2)}) collective-permute-start(bf16[256,256]{1,0:T(8,128)(2,1)S(1)} %collective-permute-done.13.refs_5_), channel_id=1, source_target_pairs={{0,4},{8,0},{16,8},{24,16},{28,24},{20,28},{12,20},{4,12},{1,5},{9... | collective-permute-start | bytes 393224 | tf_op jit(solution)/shard_map/ppermute | solution.py:271
  46.9 4.3 %collective-permute-start.18 = (bf16[128,256]{1,0:T(8,128)(2,1)S(1)}, bf16[128,256]{1,0:T(8,128)(2,1)S(1)}, u32[]{:S(2)}, u32[]{:S(2)}) collective-permute-start(bf16[128,256]{1,0:T(8,128)(2,1)S(1)} %get-tuple-element.57), channel_id=1, source_target_pairs={{0,8},{8,16},{16,24},{24,28},{28,20},{20,12},{12,4},{4,0},{1,9},{9... | collective-permute-start | bytes 196616 | tf_op jit(solution)/shard_map/ppermute | solution.py:259
  48.5 4.8 %collective-permute-start.16 = (bf16[128,256]{1,0:T(8,128)(2,1)S(1)}, bf16[128,256]{1,0:T(8,128)(2,1)S(1)}, u32[]{:S(2)}, u32[]{:S(2)}) collective-permute-start(bf16[128,256]{1,0:T(8,128)(2,1)S(1)} %get-tuple-element.58), channel_id=1, source_target_pairs={{0,8},{8,16},{16,24},{24,28},{28,20},{20,12},{12,4},{4,0},{1,9},{9... | collective-permute-start | bytes 196616 | tf_op jit(solution)/shard_map/ppermute | solution.py:259
  50.1 4.6 %collective-permute-start.20 = (bf16[128,512]{1,0:T(8,128)(2,1)S(1)}, bf16[128,512]{1,0:T(8,128)(2,1)S(1)}, u32[]{:S(2)}, u32[]{:S(2)}) collective-permute-start(bf16[128,512]{1,0:T(8,128)(2,1)S(1)} %get-tuple-element.56), channel_id=1, source_target_pairs={{0,1},{1,0},{2,3},{3,2},{4,5},{5,4},{6,7},{7,6},{8,9},{9,8},{10,11... | collective-permute-start | bytes 393224 | tf_op jit(solution)/shard_map/ppermute | solution.py:28
  51.7 5.9 %collective-permute-start.19 = (bf16[128,512]{1,0:T(8,128)(2,1)S(1)}, bf16[128,512]{1,0:T(8,128)(2,1)S(1)}, u32[]{:S(2)}, u32[]{:S(2)}) collective-permute-start(bf16[128,512]{1,0:T(8,128)(2,1)S(1)} %attend.7), channel_id=1, source_target_pairs={{0,2},{1,3},{2,0},{3,1},{4,6},{5,7},{6,4},{7,5},{8,10},{9,11},{10,... | collective-permute-start | bytes 393224 | tf_op jit(solution)/shard_map/ppermute | solution.py:28
  54.4 5.8 %collective-permute-start.17 = (bf16[128,512]{1,0:T(8,128)(2,1)S(1)}, bf16[128,512]{1,0:T(8,128)(2,1)S(1)}, u32[]{:S(2)}, u32[]{:S(2)}) collective-permute-start(bf16[128,512]{1,0:T(8,128)(2,1)S(1)} %attend.5), channel_id=1, source_target_pairs={{0,3},{1,2},{2,1},{3,0},{4,7},{5,6},{6,5},{7,4},{8,11},{9,10},{10,... | collective-permute-start | bytes 393224 | tf_op jit(solution)/shard_map/ppermute | solution.py:28

commit v6 on v5

--- a/solution.py
+++ b/solution.py
@@ -77,7 +77,7 @@
     return total
 
 
-def write_keys_values(normed_ref, wk_ref, wv_ref, table_ref, kv_ref, ahead):
+def write_keys_values(normed_ref, wk_ref, wv_ref, table_ref, kv_ref):
     rows = table_ref.shape[0]
     for head in range(wk_ref.shape[1] // HEAD_WIDTH):
         at = slice(head * HEAD_WIDTH, (head + 1) * HEAD_WIDTH)
@@ -87,19 +87,19 @@
         out = 2 * head * HEAD_WIDTH
         for first in range(0, normed_ref.shape[0], rows):
             mine = both[first:first + rows]
-            band = slice(ahead + first, ahead + first + rows)
+            band = slice(first, first + rows)
             kv_ref[band, out:out + HEAD_WIDTH] = rotate(mine[:, :HEAD_WIDTH], table_ref)
             kv_ref[band, out + HEAD_WIDTH:out + 2 * HEAD_WIDTH] = mine[:, HEAD_WIDTH:].astype(
                 jnp.bfloat16
             )
 
 
-def write_queries(normed_ref, wq_ref, table_ref, q_ref, ahead):
+def write_queries(normed_ref, wq_ref, table_ref, q_ref):
     rows, pair = table_ref.shape[0], 2 * HEAD_WIDTH
     for start in range(0, wq_ref.shape[1], pair):
         both = multiply(normed_ref, lambda k: wq_ref[k, start:start + pair])
         for first in range(0, normed_ref.shape[0], rows):
-            band = slice(ahead + first, ahead + first + rows)
+            band = slice(first, first + rows)
             for at in (0, HEAD_WIDTH):
                 q_ref[band, start + at:start + at + HEAD_WIDTH] = rotate(
                     both[first:first + rows, at:at + HEAD_WIDTH], table_ref
@@ -122,24 +122,19 @@
     normalize(own_ref, gain_ref, normed_ref, 0)
     copies[2].wait()
     copies[3].wait()
-    write_keys_values(normed_ref, wk_ref, wv_ref, table_ref, kv_ref, 0)
+    write_keys_values(normed_ref, wk_ref, wv_ref, table_ref, kv_ref)
     copies[4].wait()
-    write_queries(normed_ref, wq_ref, table_ref, q_ref, 0)
-
-
-def keys_values_kernel(before, token_ref, gain_ref, wk_ref, wv_ref, table_ref, *refs):
-    kv_ref, normed_ref = refs[-2:]
-    ahead = 0
-    if before:
-        ahead = refs[0].shape[0]
-        kv_ref[:ahead, :] = refs[0][...]
+    write_queries(normed_ref, wq_ref, table_ref, q_ref)
+
+
+def keys_values_kernel(token_ref, gain_ref, wk_ref, wv_ref, table_ref, kv_ref, normed_ref):
     normalize(token_ref, gain_ref, normed_ref, 0)
-    write_keys_values(normed_ref, wk_ref, wv_ref, table_ref, kv_ref, ahead)
+    write_keys_values(normed_ref, wk_ref, wv_ref, table_ref, kv_ref)
 
 
 def queries_kernel(pieces, wq_ref, table_ref, *refs):
-    for at, normed_ref in enumerate(refs[:pieces]):
-        write_queries(normed_ref, wq_ref, table_ref, refs[pieces], at * normed_ref.shape[0])
+    for normed_ref, q_ref in zip(refs[:pieces], refs[pieces:]):
+        write_queries(normed_ref, wq_ref, table_ref, q_ref)
 
 
 def project_call(kernel, name, operands, kinds, shapes, scratch, rows, columns):
@@ -182,17 +177,15 @@
     )
 
 
-def project_keys_values(tokens, gain, key_weight, value_weight, table, before=None):
-    held = () if before is None else (before,)
+def project_keys_values(tokens, gain, key_weight, value_weight, table):
     rows, cols = tokens.shape[0], 2 * key_weight.shape[1]
-    total = rows + sum(array.shape[0] for array in held)
-    operands = (tokens, gain, key_weight, value_weight, table, *held)
+    operands = (tokens, gain, key_weight, value_weight, table)
     return project_call(
-        functools.partial(keys_values_kernel, len(held)),
+        keys_values_kernel,
         "project_keys_values",
         operands,
         [VMEM] * len(operands),
-        [((total, cols), jnp.bfloat16), (tokens.shape, jnp.bfloat16)],
+        [((rows, cols), jnp.bfloat16), (tokens.shape, jnp.bfloat16)],
         [],
         rows,
         cols,
@@ -201,18 +194,17 @@
 
 def project_queries(normed, w_query, table):
     operands = (w_query, table, *normed)
-    rows = sum(array.shape[0] for array in normed)
-    (queries,) = project_call(
+    q_cols = w_query.shape[1]
+    return project_call(
         functools.partial(queries_kernel, len(normed)),
         "project_queries",
         operands,
         [VMEM] * len(operands),
-        [((rows, w_query.shape[1]), jnp.bfloat16)],
+        [((array.shape[0], q_cols), jnp.bfloat16) for array in normed],
         [],
-        rows,
-        w_query.shape[1],
-    )
-    return queries
+        sum(array.shape[0] for array in normed),
+        q_cols,
+    )
 
 
 def ring_order(count):
@@ -253,10 +245,6 @@
     def hold(self, array):
         self.slots.append(lambda index, r=len(self.arrays): (r, 0))
         self.arrays.append(array)
-
-    def last(self, array):
-        pairs = [(s, self.order[(at + 1) % self.count]) for at, s in enumerate(self.order)]
-        return lax.ppermute(array, "seq", pairs)
 
     def advance(self, *others):
         if self.stage >= self.count // 2:
@@ -281,9 +269,9 @@
 
     def enter(number, block):
         for lane in range(lanes):
-            doc = me ^ lane
+            doc, holder = (me ^ lane, me) if lane < 2 else (me, me ^ lane)
             for head in range(heads):
-                group = me * heads + head
+                group = holder * heads + head
                 found = (block == place) | (block == place - 1)
                 for s in range(slash_ref.shape[2]):
                     found = found | (block == place - slash_ref[doc, group, s])
@@ -520,10 +508,17 @@
     near.advance()
     crossed = swap(across, "doc", 1)
     kv_across, across_in = project_keys_values(across, gain_in, wk_in, wv_in, table)
-    kv_far, crossed_in = project_keys_values(crossed, gain_in, wk_in, wv_in, table, before=kv_across)
-    far = ring(kv_far)
+    home_across = swap(kv_across, "doc", 2)
+    kv_crossed, crossed_in = project_keys_values(crossed, gain_in, wk_in, wv_in, table)
+    home_crossed = swap(kv_crossed, "doc", 3)
+    q_across, q_crossed = project_queries(
+        [across_in, after(crossed_in, kv_crossed)], wq_in, table
+    )
+
+    arrived = after((home_across, home_crossed), q_crossed, *near.latest)
+    far = ring(jnp.concatenate(arrived, axis=0))
     far.advance()
-    q_far = project_queries([across_in, after(crossed_in, kv_far, *near.latest)], wq_in, table)
+    queries = [swap(after(q_across, home_crossed), "doc", 2), swap(q_crossed, "doc", 3)]
     mixed_own, mixed_twin = attend(
         table_of,
         [(0, (0, 0), 0, rows), (1, (0, rows), rows, rows)],
@@ -532,33 +527,29 @@
         near.slots,
         near.chunks,
     )
-    far.advance(q_far)
-    far.advance(mixed_twin)
-    out_twin = swap(after(mixed_twin, *far.latest), "doc", 1)
-    remote = [(2, (0, 0), 0, rows), (3, (0, rows), rows, rows)]
+    far.advance()
+    far.advance(mixed_twin, *queries)
+    remote = [(2, (0, 0), 0, rows), (3, (1, 0), rows, rows)]
     if long:
-        mixed = attend(table_of, remote, [q_far], far.arrays, far.slots, far.chunks)
-        home = [swap(value, "doc", 2 + at) for at, value in enumerate(mixed)]
+        out_twin = swap(mixed_twin, "doc", 1)
+        mixed = attend(table_of, remote, queries, far.arrays, far.slots, far.chunks)
     else:
-        ends = [far.last(far.front[1][at * rows:(at + 1) * rows]) for at in range(2)]
-        count = len(far.slots)
-        state = attend(table_of, remote[:1], [q_far], far.arrays, far.slots, end=False)
-        (mixed,) = attend(
-            table_of, remote[:1], [q_far], ends[:1], [lambda index: (0, 0)], first=count, states=[state]
-        )
-        home = [swap(mixed, "doc", 2)]
+        far.advance()
+        last = len(far.slots) - 1
+        states = attend(table_of, remote, queries, far.arrays[:last], far.slots[:last], end=False)
+        out_twin = swap(after(mixed_twin, states[0]), "doc", 1)
         mixed = attend(
             table_of,
-            remote[1:],
-            [q_far],
-            [*far.arrays, ends[1]],
-            [*far.slots, lambda index: (count, -rows)],
+            remote,
+            queries,
+            far.arrays[last:],
+            far.slots[:1],
+            first=last,
+            states=[states[:3], states[3:]],
         )
-        home.append(swap(mixed[0], "doc", 3))
     count = lax.axis_size("doc")
     result = deliver((0, 1), [mixed_own, out_twin], count)
-    result = deliver((2,), home[:1], count, before=result)
-    return deliver((3,), home[1:], count, before=result)
+    return deliver((2, 3), mixed, count, before=result)
 
 
 def solution(mesh):

time: 61 us -> 62.5 us (1.025)
  waiting for transfers between devices: 20.7 us -> 23.4 us
  Pallas kernels: 16 us -> 15.3 us
    ppermute x13 -> x14, waiting for transfers between devices: 11.5 us -> 15 us  [advance(): self.front[way] = lax.ppermute(value, 'seq', pairs)]
    ppermute x2 -> x0, starting transfers between devices: 3.21 us -> none  [last(): return lax.ppermute(array, 'seq', pairs)]
    ppermute x13 -> x14, starting transfers between devices: 14.2 us -> 15.8 us  [advance(): self.front[way] = lax.ppermute(value, 'seq', pairs)]
    ppermute x6 -> x8, starting transfers between devices: 4.93 us -> 5.94 us  [swap(): lax.ppermute(value, axis, [(source, source ^ mask) for source in range(co...]
    ppermute x6 -> x8, waiting for transfers between devices: 9.03 us -> 8.41 us  [swap(): lax.ppermute(value, axis, [(source, source ^ mask) for source in range(co...]
    pallas_call x3 -> x2, Pallas kernels: 2.12 us -> 1.53 us  [deliver(): pl.pallas_call(functools.partial(deliver_kernel, masks), in_specs=[VMEM]...]
    pallas_call x4 -> x3, Pallas kernels: 4.63 us -> 4.6 us  [attend(): pl.pallas_call(kernel, in_specs=[VMEM] * (1 + len(queries) + len(arrays)...]
  transfers between devices with their start and end apart: 21 -> 22, of which waited for: 9 -> 11; matrix products, arithmetic and copies ran while one was open for 3% -> 3% of each run, Pallas kernels for 25% -> 19%
where the time goes in v6:
time: 62.5 us; the launch traced here: 62.4 us
  waiting for transfers between devices  23.4 us (37%)
  starting transfers between devices  21.7 us (35%)
  Pallas kernels  15.3 us (24%)
  other arithmetic  1.16 us (2%)
    ppermute x14, starting transfers between devices, advance(): self.front[way] = lax.ppermute(value, 'seq', pairs)  15.8 us
    ppermute x14, waiting for transfers between devices, advance(): self.front[way] = lax.ppermute(value, 'seq', pairs)  15 us
    ppermute x8, waiting for transfers between devices, swap(): lax.ppermute(value, axis, [(source, source ^ mask) for source in range(co...  8.41 us
    pallas_call x4, Pallas kernels, project_call(): pl.pallas_call(kernel, in_specs=kinds, out_specs=[VMEM] * len(shapes), ou...  7.98 us
    ppermute x8, starting transfers between devices, swap(): lax.ppermute(value, axis, [(source, source ^ mask) for source in range(co...  5.94 us
    pallas_call x3, Pallas kernels, attend(): pl.pallas_call(kernel, in_specs=[VMEM] * (1 + len(queries) + len(arrays)...  4.6 us
    pallas_call x2, Pallas kernels, deliver(): pl.pallas_call(functools.partial(deliver_kernel, masks), in_specs=[VMEM]...  1.53 us
  transfers between devices with their start and end apart: 22, of which 11 were waited for; matrix products, arithmetic and copies ran while one was open for 3% of the time, Pallas kernels for 19%

profile of v6, /device:TPU:0, one launch (start us, length us, event | category | flops | bytes accessed | tf_op | source)
XLA Modules:
  0.0 62.4 jit_solution(7377001635253612043)
XLA Ops:
  0.5 2.6 %collective-permute-start.1 = (bf16[128,4096]{1,0:T(8,128)(2,1)}, bf16[128,4096]{1,0:T(8,128)(2,1)S(1)}, u32[]{:S(2)}, u32[]{:S(2)}) collective-permute-start(bf16[128,4096]{1,0:T(8,128)(2,1)} %bitcast.8), channel_id=1, source_target_pairs={{0,2},{1,3},{2,0},{3,1},{4,6},{5,7},{6,4},{7,5},{8,10},{9,11},{10,... | collective-permute-start | bytes 3145736 | tf_op jit(solution)/shard_map/ppermute | solution.py:28
  3.1 0.6 slice.3
  3.7 0.6 %add_convert_fusion = f32[128]{0:T(128)S(1)} fusion(s32[]{:T(128)} %bitcast.5), kind=kLoop, calls=%fused_computation.8 | loop fusion | flops 256 | bytes 516 | tf_op jit(solution)/shard_map/convert_element_type | solution.py:41
  4.8 4.6 %project_near.1 = (bf16[256,512]{1,0:T(8,128)(2,1)S(1)}, bf16[256,256]{1,0:T(8,128)(2,1)S(1)}, f32[1,4096]{1,0:T(1,128)S(1)}, bf16[4096,512]{1,0:T(8,128)(2,1)S(...) custom-call(bf16[128,4096]{1,0:T(8,128)(2,1)} %bitcast.9, ...), custom_call_target="tpu_custom_call" | custom-call | flops 1610612736 | bytes 8388608 | tf_op jit(solution)/shard_map/project_near/pallas_call | solution.py:142
  9.4 1.6 %collective-permute-start.2 = (bf16[256,256]{1,0:T(8,128)(2,1)S(1)}, bf16[256,256]{1,0:T(8,128)(2,1)S(1)}, u32[]{:S(2)}, u32[]{:S(2)}) collective-permute-start(bf16[256,256]{1,0:T(8,128)(2,1)S(1)} %get-tuple-element.41.refs_1_), channel_id=1, source_target_pairs={{0,8},{8,16},{16,24},{24,28},{28,20},{20,12},{12,4},{4,0},{1,9},{9... | collective-permute-start | bytes 393224 | tf_op jit(solution)/shard_map/ppermute | solution.py:259
  11.5 1.2 %plan.1.plan_ref = s32[32,512]{1,0:T(8,128)S(1)} custom-call(s32[3]{0:T(128)S(1)} %pad_add_fusion.info_ref, s32[4,4,4]{2,1,0:T(4,128)S(1)} %copy-done, s32[4,4,4]{2,1,0:T(4,128)S(1)} %copy-done.1), custom_call_target="tpu_custom_call" | custom-call | tf_op jit(solution)/shard_map/plan/pallas_call | solution.py:303
  12.8 2.3 %collective-permute-done.2.refs_2_ = bf16[256,256]{1,0:T(8,128)(2,1)S(1)} collective-permute-done((bf16[256,256]{1,0:T(8,128)(2,1)S(1)}, bf16[256,256]{1,0:T(8,128)(2,1)S(1)}, u32[]{:S(2)}, u32[]{:S(2)}) %collective-permute-start.2) | collective-permute-done | bytes 131104 | tf_op jit(solution)/shard_map/ppermute | solution.py:259
  15.1 1.6 %collective-permute-start.3 = (bf16[256,256]{1,0:T(8,128)(2,1)S(1)}, bf16[256,256]{1,0:T(8,128)(2,1)S(1)}, u32[]{:S(2)}, u32[]{:S(2)}) collective-permute-start(bf16[256,256]{1,0:T(8,128)(2,1)S(1)} %collective-permute-done.2.refs_2_), channel_id=1, source_target_pairs={{0,8},{8,16},{16,24},{24,28},{28,20},{20,12},{12,4},{4,0},{1,9},{9... | collective-permute-start | bytes 393224 | tf_op jit(solution)/shard_map/ppermute | solution.py:259
  17.1 2.9 %collective-permute-done.3.refs_4_ = bf16[256,256]{1,0:T(8,128)(2,1)S(1)} collective-permute-done((bf16[256,256]{1,0:T(8,128)(2,1)S(1)}, bf16[256,256]{1,0:T(8,128)(2,1)S(1)}, u32[]{:S(2)}, u32[]{:S(2)}) %collective-permute-start.3) | collective-permute-done | bytes 131104 | tf_op jit(solution)/shard_map/ppermute | solution.py:259
  20.0 1.6 %collective-permute-start.4 = (bf16[256,256]{1,0:T(8,128)(2,1)S(1)}, bf16[256,256]{1,0:T(8,128)(2,1)S(1)}, u32[]{:S(2)}, u32[]{:S(2)}) collective-permute-start(bf16[256,256]{1,0:T(8,128)(2,1)S(1)} %collective-permute-done.3.refs_4_), channel_id=1, source_target_pairs={{0,8},{8,16},{16,24},{24,28},{28,20},{20,12},{12,4},{4,0},{1,9},{9... | collective-permute-start | bytes 393224 | tf_op jit(solution)/shard_map/ppermute | solution.py:259
  22.1 5.0 %collective-permute-done.1.token_ref = bf16[128,4096]{1,0:T(8,128)(2,1)S(1)} collective-permute-done((bf16[128,4096]{1,0:T(8,128)(2,1)}, bf16[128,4096]{1,0:T(8,128)(2,1)S(1)}, u32[]{:S(2)}, u32[]{:S(2)}) %collective-permute-start.1) | collective-permute-done | bytes 1048608 | tf_op jit(solution)/shard_map/ppermute | solution.py:28
  27.1 1.9 %collective-permute-start.13 = (bf16[256,256]{1,0:T(8,128)(2,1)S(1)}, bf16[256,256]{1,0:T(8,128)(2,1)S(1)}, u32[]{:S(2)}, u32[]{:S(2)}) collective-permute-start(bf16[256,256]{1,0:T(8,128)(2,1)S(1)} %collective-permute-done.4.refs_6_), channel_id=1, source_target_pairs={{0,8},{8,16},{16,24},{24,28},{28,20},{20,12},{12,4},{4,0},{1,9},{9... | collective-permute-start | bytes 393224 | tf_op jit(solution)/shard_map/ppermute | solution.py:259
  29.0 1.0 %project_keys_values.2 = (bf16[128,256]{1,0:T(8,128)(2,1)S(1)}, bf16[128,4096]{1,0:T(8,128)(2,1)S(1)}) custom-call(bf16[128,4096]{1,0:T(8,128)(2,1)S(1)} %collective-permute-done.1.token_ref, f32[1,4096]{1,0:T(1,128)S(1)} %get-tuple-element.45.gain_ref, bf16[4096,128]{1,0:T(8,128)(2,1)S(1)} %get-tuple-element.46.wk_ref, ...), custom_call_target="tpu_custom_call" | custom-call | flops 268435456 | bytes 3145728 | tf_op jit(solution)/shard_map/project_keys_values/pallas_call | solution.py:142
  30.0 1.6 %collective-permute-start.12 = (bf16[128,256]{1,0:T(8,128)(2,1)S(1)}, bf16[128,256]{1,0:T(8,128)(2,1)S(1)}, u32[]{:S(2)}, u32[]{:S(2)}) collective-permute-start(bf16[128,256]{1,0:T(8,128)(2,1)S(1)} %get-tuple-element.55), channel_id=1, source_target_pairs={{0,2},{1,3},{2,0},{3,1},{4,6},{5,7},{6,4},{7,5},{8,10},{9,11},{10,... | collective-permute-start | bytes 196616 | tf_op jit(solution)/shard_map/ppermute | solution.py:28
  31.5 1.0 %project_keys_values.3 = (bf16[128,256]{1,0:T(8,128)(2,1)S(1)}, bf16[128,4096]{1,0:T(8,128)(2,1)S(1)}) custom-call(bf16[128,4096]{1,0:T(8,128)(2,1)S(1)} %collective-permute-done.8.token_ref, f32[1,4096]{1,0:T(1,128)S(1)} %get-tuple-element.45.gain_ref, bf16[4096,128]{1,0:T(8,128)(2,1)S(1)} %get-tuple-element.46.wk_ref, ...), custom_call_target="tpu_custom_call" | custom-call | flops 268435456 | bytes 3145728 | tf_op jit(solution)/shard_map/project_keys_values/pallas_call | solution.py:142
  32.6 1.4 %project_queries.1 = (bf16[128,512]{1,0:T(8,128)(2,1)S(1)}, bf16[128,512]{1,0:T(8,128)(2,1)S(1)}) custom-call(bf16[4096,512]{1,0:T(8,128)(2,1)S(1)} %get-tuple-element.40.wq_ref, f32[128,256]{1,0:T(8,128)S(1)} %pad_maximum_fusion.table_ref, bf16[128,4096]{1,0:T(8,128)(2,1)S(1)} %get-tuple-element.48.refs_0_, bf16[128,4096]{1,0:T(8,128)(2,1)S(1)} %get-tuple-element.51.refs_1_), custom_call_target="tpu_custom_call" | custom-call | flops 1073741824 | bytes 6291456 | tf_op jit(solution)/shard_map/project_queries/pallas_call | solution.py:142
  34.3 2.6 %collective-permute-done.9 = bf16[128,256]{1,0:T(8,128)(2,1)S(1)} collective-permute-done((bf16[128,256]{1,0:T(8,128)(2,1)S(1)}, bf16[128,256]{1,0:T(8,128)(2,1)S(1)}, u32[]{:S(2)}, u32[]{:S(2)}) %collective-permute-start.9) | collective-permute-done | bytes 65568 | tf_op jit(solution)/shard_map/ppermute | solution.py:28
  37.0 0.5 collective-permute-start.16
  37.5 1.6 %collective-permute-start.14 = (bf16[256,256]{1,0:T(8,128)(2,1)S(1)}, bf16[256,256]{1,0:T(8,128)(2,1)S(1)}, u32[]{:S(2)}, u32[]{:S(2)}) collective-permute-start(bf16[256,256]{1,0:T(8,128)(2,1)S(1)} %constant_dynamic-update-slice_fusion.refs_2_), channel_id=1, source_target_pairs={{0,8},{8,16},{16,24},{24,28},{28,20},{20,12},{12,4},{4,0},{1,9},{9... | collective-permute-start | bytes 393224 | tf_op jit(solution)/shard_map/ppermute | solution.py:259
  39.0 1.2 %collective-permute-start.10 = (bf16[128,512]{1,0:T(8,128)(2,1)S(1)}, bf16[128,512]{1,0:T(8,128)(2,1)S(1)}, u32[]{:S(2)}, u32[]{:S(2)}) collective-permute-start(bf16[128,512]{1,0:T(8,128)(2,1)S(1)} %get-tuple-element.53), channel_id=1, source_target_pairs={{0,2},{1,3},{2,0},{3,1},{4,6},{5,7},{6,4},{7,5},{8,10},{9,11},{10,... | collective-permute-start | bytes 393224 | tf_op jit(solution)/shard_map/ppermute | solution.py:28
  40.2 2.3 %collective-permute-done.16.refs_4_ = bf16[256,256]{1,0:T(8,128)(2,1)S(1)} collective-permute-done((bf16[256,256]{1,0:T(8,128)(2,1)S(1)}, bf16[256,256]{1,0:T(8,128)(2,1)S(1)}, u32[]{:S(2)}, u32[]{:S(2)}) %collective-permute-start.16) | collective-permute-done | bytes 131104 | tf_op jit(solution)/shard_map/ppermute | solution.py:259
  43.0 1.6 %collective-permute-start.15 = (bf16[256,256]{1,0:T(8,128)(2,1)S(1)}, bf16[256,256]{1,0:T(8,128)(2,1)S(1)}, u32[]{:S(2)}, u32[]{:S(2)}) collective-permute-start(bf16[256,256]{1,0:T(8,128)(2,1)S(1)} %collective-permute-done.14.refs_3_), channel_id=1, source_target_pairs={{0,8},{8,16},{16,24},{24,28},{28,20},{20,12},{12,4},{4,0},{1,9},{9... | collective-permute-start | bytes 393224 | tf_op jit(solution)/shard_map/ppermute | solution.py:259
  44.6 2.0 %attend.3 = (bf16[128,512]{1,0:T(8,128)(2,1)S(1)}, bf16[128,512]{1,0:T(8,128)(2,1)S(1)}) custom-call(s32[32,512]{1,0:T(8,128)S(1)} %plan.1.plan_ref, bf16[256,512]{1,0:T(8,128)(2,1)S(1)} %get-tuple-element.59.refs_0_, bf16[256,256]{1,0:T(8,128)(2,1)S(1)} %get-tuple-element.41.refs_1_, bf16[256,256]{1,0:T(8,128)(2,1)S(1)} %collective-permute-done.2.refs_2_, ...), custom_call_target="tpu_custom_call" | custom-call | flops 536870912 | bytes 1572864 | tf_op jit(solution)/shard_map/attend/pallas_call | solution.py:433
  46.6 0.5 collective-permute-done.10.refs_0_
  47.9 1.6 %collective-permute-start.17 = (bf16[256,256]{1,0:T(8,128)(2,1)S(1)}, bf16[256,256]{1,0:T(8,128)(2,1)S(1)}, u32[]{:S(2)}, u32[]{:S(2)}) collective-permute-start(bf16[256,256]{1,0:T(8,128)(2,1)S(1)} %collective-permute-done.15.refs_5_), channel_id=1, source_target_pairs={{0,8},{8,16},{16,24},{24,28},{28,20},{20,12},{12,4},{4,0},{1,9},{9... | collective-permute-start | bytes 393224 | tf_op jit(solution)/shard_map/ppermute | solution.py:259
  49.5 3.4 %collective-permute-done.20.refs_8_ = bf16[256,256]{1,0:T(8,128)(2,1)S(1)} collective-permute-done((bf16[256,256]{1,0:T(8,128)(2,1)S(1)}, bf16[256,256]{1,0:T(8,128)(2,1)S(1)}, u32[]{:S(2)}, u32[]{:S(2)}) %collective-permute-start.20) | collective-permute-done | bytes 131104 | tf_op jit(solution)/shard_map/ppermute | solution.py:259
  53.1 1.8 %attend.4 = (f32[1,1,512]{2,1,0:T(1,128)S(1)}, f32[1,1,512]{2,1,0:T(1,128)S(1)}, f32[1,128,512]{2,1,0:T(8,128)S(1)}, f32[1,1,512]{2,1,0:T(1,128)S(1)}, f32[1,1,5...) custom-call(s32[32,512]{1,0:T(8,128)S(1)} %plan.1.plan_ref, bf16[128,512]{1,0:T(8,128)(2,1)S(1)} %collective-permute-done.10.refs_0_, ...), custom_call_target="tpu_custom_call" | custom-call | flops 469762048 | bytes 1441792 | tf_op jit(solution)/shard_map/attend/pallas_call | solution.py:433
  55.0 1.6 %collective-permute-start.18 = (bf16[256,256]{1,0:T(8,128)(2,1)S(1)}, bf16[256,256]{1,0:T(8,128)(2,1)S(1)}, u32[]{:S(2)}, u32[]{:S(2)}) collective-permute-start(bf16[256,256]{1,0:T(8,128)(2,1)S(1)} %collective-permute-done.17.refs_7_), channel_id=1, source_target_pairs={{0,8},{8,16},{16,24},{24,28},{28,20},{20,12},{12,4},{4,0},{1,9},{9... | collective-permute-start | bytes 393224 | tf_op jit(solution)/shard_map/ppermute | solution.py:259
  56.6 0.8 %deliver.2.refs_2_ = bf16[1,128,2048]{2,1,0:T(8,128)(2,1)} custom-call(bf16[128,512]{1,0:T(8,128)(2,1)S(1)} %get-tuple-element.71.refs_0_, bf16[128,512]{1,0:T(8,128)(2,1)S(1)} %collective-permute-done.21.refs_1_), custom_call_target="tpu_custom_call" | custom-call | tf_op jit(solution)/shard_map/deliver/pallas_call | solution.py:471
  57.4 3.5 %collective-permute-done.18.refs_2_ = bf16[256,256]{1,0:T(8,128)(2,1)S(1)} collective-permute-done((bf16[256,256]{1,0:T(8,128)(2,1)S(1)}, bf16[256,256]{1,0:T(8,128)(2,1)S(1)}, u32[]{:S(2)}, u32[]{:S(2)}) %collective-permute-start.18) | collective-permute-done | bytes 131104 | tf_op jit(solution)/shard_map/ppermute | solution.py:259
  60.9 0.7 %attend.5 = (bf16[128,512]{1,0:T(8,128)(2,1)S(1)}, bf16[128,512]{1,0:T(8,128)(2,1)S(1)}) custom-call(s32[32,512]{1,0:T(8,128)S(1)} %plan.1.plan_ref, bf16[128,512]{1,0:T(8,128)(2,1)S(1)} %collective-permute-done.10.refs_0_, bf16[128,512]{1,0:T(8,128)(2,1)S(1)} %collective-permute-done.11.refs_1_, bf16[256,256]{1,0:T(8,128)(2,1)S(1)} %collective-permute-done.18.refs_2_, ...), custom_call_target="tpu_custom_call" | custom-call | flops 67108864 | bytes 655360 | tf_op jit(solution)/shard_map/attend/pallas_call | solution.py:433
  61.6 0.8 %deliver.3 = bf16[1,128,2048]{2,1,0:T(8,128)(2,1)} custom-call(bf16[128,512]{1,0:T(8,128)(2,1)S(1)} %get-tuple-element.69.refs_0_, bf16[128,512]{1,0:T(8,128)(2,1)S(1)} %get-tuple-element.70.refs_1_, bf16[1,128,2048]{2,1,0:T(8,128)(2,1)} %deliver.2.refs_2_), custom_call_target="tpu_custom_call", output_to_operand_aliasing={{}: (2, {})} | custom-call | tf_op jit(solution)/shard_map/deliver/pallas_call | solution.py:471
  (34 shorter events, 4.3 us)
Async XLA Ops:
  0.1 4.7 %collective-permute-start = (bf16[128,4096]{1,0:T(8,128)(2,1)}, bf16[128,4096]{1,0:T(8,128)(2,1)S(1)}, u32[]{:S(2)}, u32[]{:S(2)}) collective-permute-start(bf16[128,4096]{1,0:T(8,128)(2,1)} %bitcast.7), channel_id=1, source_target_pairs={{0,1},{1,0},{2,3},{3,2},{4,5},{5,4},{6,7},{7,6},{8,9},{9,8},{10,11... | collective-permute-start | bytes 3145736 | tf_op jit(solution)/shard_map/ppermute | solution.py:28
  0.5 26.5 %collective-permute-start.1 = (bf16[128,4096]{1,0:T(8,128)(2,1)}, bf16[128,4096]{1,0:T(8,128)(2,1)S(1)}, u32[]{:S(2)}, u32[]{:S(2)}) collective-permute-start(bf16[128,4096]{1,0:T(8,128)(2,1)} %bitcast.8), channel_id=1, source_target_pairs={{0,2},{1,3},{2,0},{3,1},{4,6},{5,7},{6,4},{7,5},{8,10},{9,11},{10,... | collective-permute-start | bytes 3145736 | tf_op jit(solution)/shard_map/ppermute | solution.py:28
  4.8 6.7 %copy-start = (s32[4,4,4]{2,1,0:T(4,128)S(1)}, s32[4,4,4]{2,1,0:T(4,128)}, u32[]{:S(2)}) copy-start(s32[4,4,4]{2,1,0:T(4,128)} %vertical_ref.1) | copy-start | bytes 772
  4.8 6.7 %copy-start.1 = (s32[4,4,4]{2,1,0:T(4,128)S(1)}, s32[4,4,4]{2,1,0:T(4,128)}, u32[]{:S(2)}) copy-start(s32[4,4,4]{2,1,0:T(4,128)} %slash_ref.1) | copy-start | bytes 772
  9.4 5.6 %collective-permute-start.2 = (bf16[256,256]{1,0:T(8,128)(2,1)S(1)}, bf16[256,256]{1,0:T(8,128)(2,1)S(1)}, u32[]{:S(2)}, u32[]{:S(2)}) collective-permute-start(bf16[256,256]{1,0:T(8,128)(2,1)S(1)} %get-tuple-element.41.refs_1_), channel_id=1, source_target_pairs={{0,8},{8,16},{16,24},{24,28},{28,20},{20,12},{12,4},{4,0},{1,9},{9... | collective-permute-start | bytes 393224 | tf_op jit(solution)/shard_map/ppermute | solution.py:259
  11.1 5.6 %collective-permute-start.5 = (bf16[256,256]{1,0:T(8,128)(2,1)S(1)}, bf16[256,256]{1,0:T(8,128)(2,1)S(1)}, u32[]{:S(2)}, u32[]{:S(2)}) collective-permute-start(bf16[256,256]{1,0:T(8,128)(2,1)S(1)} %get-tuple-element.41.refs_1_), channel_id=1, source_target_pairs={{0,4},{8,0},{16,8},{24,16},{28,24},{20,28},{12,20},{4,12},{1,5},{9... | collective-permute-start | bytes 393224 | tf_op jit(solution)/shard_map/ppermute | solution.py:259
  15.1 5.0 %collective-permute-start.3 = (bf16[256,256]{1,0:T(8,128)(2,1)S(1)}, bf16[256,256]{1,0:T(8,128)(2,1)S(1)}, u32[]{:S(2)}, u32[]{:S(2)}) collective-permute-start(bf16[256,256]{1,0:T(8,128)(2,1)S(1)} %collective-permute-done.2.refs_2_), channel_id=1, source_target_pairs={{0,8},{8,16},{16,24},{24,28},{28,20},{20,12},{12,4},{4,0},{1,9},{9... | collective-permute-start | bytes 393224 | tf_op jit(solution)/shard_map/ppermute | solution.py:259
  16.6 5.0 %collective-permute-start.6 = (bf16[256,256]{1,0:T(8,128)(2,1)S(1)}, bf16[256,256]{1,0:T(8,128)(2,1)S(1)}, u32[]{:S(2)}, u32[]{:S(2)}) collective-permute-start(bf16[256,256]{1,0:T(8,128)(2,1)S(1)} %collective-permute-done.5.refs_3_), channel_id=1, source_target_pairs={{0,4},{8,0},{16,8},{24,16},{28,24},{20,28},{12,20},{4,12},{1,5},{9... | collective-permute-start | bytes 393224 | tf_op jit(solution)/shard_map/ppermute | solution.py:259
  20.0 7.0 %collective-permute-start.4 = (bf16[256,256]{1,0:T(8,128)(2,1)S(1)}, bf16[256,256]{1,0:T(8,128)(2,1)S(1)}, u32[]{:S(2)}, u32[]{:S(2)}) collective-permute-start(bf16[256,256]{1,0:T(8,128)(2,1)S(1)} %collective-permute-done.3.refs_4_), channel_id=1, source_target_pairs={{0,8},{8,16},{16,24},{24,28},{28,20},{20,12},{12,4},{4,0},{1,9},{9... | collective-permute-start | bytes 393224 | tf_op jit(solution)/shard_map/ppermute | solution.py:259
  21.6 5.5 %collective-permute-start.7 = (bf16[256,256]{1,0:T(8,128)(2,1)S(1)}, bf16[256,256]{1,0:T(8,128)(2,1)S(1)}, u32[]{:S(2)}, u32[]{:S(2)}) collective-permute-start(bf16[256,256]{1,0:T(8,128)(2,1)S(1)} %collective-permute-done.6.refs_5_), channel_id=1, source_target_pairs={{0,4},{8,0},{16,8},{24,16},{28,24},{20,28},{12,20},{4,12},{1,5},{9... | collective-permute-start | bytes 393224 | tf_op jit(solution)/shard_map/ppermute | solution.py:259
  27.1 4.5 %collective-permute-start.8 = (bf16[128,4096]{1,0:T(8,128)(2,1)S(1)}, bf16[128,4096]{1,0:T(8,128)(2,1)S(1)}, u32[]{:S(2)}, u32[]{:S(2)}) collective-permute-start(bf16[128,4096]{1,0:T(8,128)(2,1)S(1)} %collective-permute-done.1.token_ref), channel_id=1, source_target_pairs={{0,1},{1,0},{2,3},{3,2},{4,5},{5,4},{6,7},{7,6},{8,9},{9,8},{10,11... | collective-permute-start | bytes 3145736 | tf_op jit(solution)/shard_map/ppermute | solution.py:28
  27.1 7.2 %collective-permute-start.13 = (bf16[256,256]{1,0:T(8,128)(2,1)S(1)}, bf16[256,256]{1,0:T(8,128)(2,1)S(1)}, u32[]{:S(2)}, u32[]{:S(2)}) collective-permute-start(bf16[256,256]{1,0:T(8,128)(2,1)S(1)} %collective-permute-done.4.refs_6_), channel_id=1, source_target_pairs={{0,8},{8,16},{16,24},{24,28},{28,20},{20,12},{12,4},{4,0},{1,9},{9... | collective-permute-start | bytes 393224 | tf_op jit(solution)/shard_map/ppermute | solution.py:259
  30.0 4.3 %collective-permute-start.12 = (bf16[128,256]{1,0:T(8,128)(2,1)S(1)}, bf16[128,256]{1,0:T(8,128)(2,1)S(1)}, u32[]{:S(2)}, u32[]{:S(2)}) collective-permute-start(bf16[128,256]{1,0:T(8,128)(2,1)S(1)} %get-tuple-element.55), channel_id=1, source_target_pairs={{0,2},{1,3},{2,0},{3,1},{4,6},{5,7},{6,4},{7,5},{8,10},{9,11},{10,... | collective-permute-start | bytes 196616 | tf_op jit(solution)/shard_map/ppermute | solution.py:28
  32.5 4.4 %collective-permute-start.9 = (bf16[128,256]{1,0:T(8,128)(2,1)S(1)}, bf16[128,256]{1,0:T(8,128)(2,1)S(1)}, u32[]{:S(2)}, u32[]{:S(2)}) collective-permute-start(bf16[128,256]{1,0:T(8,128)(2,1)S(1)} %get-tuple-element.50), channel_id=1, source_target_pairs={{0,3},{1,2},{2,1},{3,0},{4,7},{5,6},{6,5},{7,4},{8,11},{9,10},{10,... | collective-permute-start | bytes 196616 | tf_op jit(solution)/shard_map/ppermute | solution.py:28
  37.0 5.6 %collective-permute-start.16 = (bf16[256,256]{1,0:T(8,128)(2,1)S(1)}, bf16[256,256]{1,0:T(8,128)(2,1)S(1)}, u32[]{:S(2)}, u32[]{:S(2)}) collective-permute-start(bf16[256,256]{1,0:T(8,128)(2,1)S(1)} %constant_dynamic-update-slice_fusion.refs_2_), channel_id=1, source_target_pairs={{0,4},{8,0},{16,8},{24,16},{28,24},{20,28},{12,20},{4,12},{1,5},{9... | collective-permute-start | bytes 393224 | tf_op jit(solution)/shard_map/ppermute | solution.py:259
  37.5 5.5 %collective-permute-start.14 = (bf16[256,256]{1,0:T(8,128)(2,1)S(1)}, bf16[256,256]{1,0:T(8,128)(2,1)S(1)}, u32[]{:S(2)}, u32[]{:S(2)}) collective-permute-start(bf16[256,256]{1,0:T(8,128)(2,1)S(1)} %constant_dynamic-update-slice_fusion.refs_2_), channel_id=1, source_target_pairs={{0,8},{8,16},{16,24},{24,28},{28,20},{20,12},{12,4},{4,0},{1,9},{9... | collective-permute-start | bytes 393224 | tf_op jit(solution)/shard_map/ppermute | solution.py:259
  39.0 7.6 %collective-permute-start.11 = (bf16[128,512]{1,0:T(8,128)(2,1)S(1)}, bf16[128,512]{1,0:T(8,128)(2,1)S(1)}, u32[]{:S(2)}, u32[]{:S(2)}) collective-permute-start(bf16[128,512]{1,0:T(8,128)(2,1)S(1)} %get-tuple-element.54), channel_id=1, source_target_pairs={{0,3},{1,2},{2,1},{3,0},{4,7},{5,6},{6,5},{7,4},{8,11},{9,10},{10,... | collective-permute-start | bytes 393224 | tf_op jit(solution)/shard_map/ppermute | solution.py:28
  39.0 8.1 %collective-permute-start.10 = (bf16[128,512]{1,0:T(8,128)(2,1)S(1)}, bf16[128,512]{1,0:T(8,128)(2,1)S(1)}, u32[]{:S(2)}, u32[]{:S(2)}) collective-permute-start(bf16[128,512]{1,0:T(8,128)(2,1)S(1)} %get-tuple-element.53), channel_id=1, source_target_pairs={{0,2},{1,3},{2,0},{3,1},{4,6},{5,7},{6,4},{7,5},{8,10},{9,11},{10,... | collective-permute-start | bytes 393224 | tf_op jit(solution)/shard_map/ppermute | solution.py:28
  42.5 5.0 %collective-permute-start.19 = (bf16[256,256]{1,0:T(8,128)(2,1)S(1)}, bf16[256,256]{1,0:T(8,128)(2,1)S(1)}, u32[]{:S(2)}, u32[]{:S(2)}) collective-permute-start(bf16[256,256]{1,0:T(8,128)(2,1)S(1)} %collective-permute-done.16.refs_4_), channel_id=1, source_target_pairs={{0,4},{8,0},{16,8},{24,16},{28,24},{20,28},{12,20},{4,12},{1,5},{9... | collective-permute-start | bytes 393224 | tf_op jit(solution)/shard_map/ppermute | solution.py:259
  43.0 5.0 %collective-permute-start.15 = (bf16[256,256]{1,0:T(8,128)(2,1)S(1)}, bf16[256,256]{1,0:T(8,128)(2,1)S(1)}, u32[]{:S(2)}, u32[]{:S(2)}) collective-permute-start(bf16[256,256]{1,0:T(8,128)(2,1)S(1)} %collective-permute-done.14.refs_3_), channel_id=1, source_target_pairs={{0,8},{8,16},{16,24},{24,28},{28,20},{20,12},{12,4},{4,0},{1,9},{9... | collective-permute-start | bytes 393224 | tf_op jit(solution)/shard_map/ppermute | solution.py:259
  47.5 5.4 %collective-permute-start.20 = (bf16[256,256]{1,0:T(8,128)(2,1)S(1)}, bf16[256,256]{1,0:T(8,128)(2,1)S(1)}, u32[]{:S(2)}, u32[]{:S(2)}) collective-permute-start(bf16[256,256]{1,0:T(8,128)(2,1)S(1)} %collective-permute-done.19.refs_6_), channel_id=1, source_target_pairs={{0,4},{8,0},{16,8},{24,16},{28,24},{20,28},{12,20},{4,12},{1,5},{9... | collective-permute-start | bytes 393224 | tf_op jit(solution)/shard_map/ppermute | solution.py:259
  47.9 5.1 %collective-permute-start.17 = (bf16[256,256]{1,0:T(8,128)(2,1)S(1)}, bf16[256,256]{1,0:T(8,128)(2,1)S(1)}, u32[]{:S(2)}, u32[]{:S(2)}) collective-permute-start(bf16[256,256]{1,0:T(8,128)(2,1)S(1)} %collective-permute-done.15.refs_5_), channel_id=1, source_target_pairs={{0,8},{8,16},{16,24},{24,28},{28,20},{20,12},{12,4},{4,0},{1,9},{9... | collective-permute-start | bytes 393224 | tf_op jit(solution)/shard_map/ppermute | solution.py:259
  54.9 1.7 %collective-permute-start.21 = (bf16[128,512]{1,0:T(8,128)(2,1)S(1)}, bf16[128,512]{1,0:T(8,128)(2,1)S(1)}, u32[]{:S(2)}, u32[]{:S(2)}) collective-permute-start(bf16[128,512]{1,0:T(8,128)(2,1)S(1)} %get-tuple-element.72), channel_id=1, source_target_pairs={{0,1},{1,0},{2,3},{3,2},{4,5},{5,4},{6,7},{7,6},{8,9},{9,8},{10,11... | collective-permute-start | bytes 393224 | tf_op jit(solution)/shard_map/ppermute | solution.py:28
  55.0 5.9 %collective-permute-start.18 = (bf16[256,256]{1,0:T(8,128)(2,1)S(1)}, bf16[256,256]{1,0:T(8,128)(2,1)S(1)}, u32[]{:S(2)}, u32[]{:S(2)}) collective-permute-start(bf16[256,256]{1,0:T(8,128)(2,1)S(1)} %collective-permute-done.17.refs_7_), channel_id=1, source_target_pairs={{0,8},{8,16},{16,24},{24,28},{28,20},{20,12},{12,4},{4,0},{1,9},{9... | collective-permute-start | bytes 393224 | tf_op jit(solution)/shard_map/ppermute | solution.py:259

commit v7 on v6

--- a/solution.py
+++ b/solution.py
@@ -529,15 +529,14 @@
     )
     far.advance()
     far.advance(mixed_twin, *queries)
+    out_twin = swap(after(mixed_twin, *far.latest), "doc", 1)
     remote = [(2, (0, 0), 0, rows), (3, (1, 0), rows, rows)]
     if long:
-        out_twin = swap(mixed_twin, "doc", 1)
         mixed = attend(table_of, remote, queries, far.arrays, far.slots, far.chunks)
     else:
         far.advance()
         last = len(far.slots) - 1
         states = attend(table_of, remote, queries, far.arrays[:last], far.slots[:last], end=False)
-        out_twin = swap(after(mixed_twin, states[0]), "doc", 1)
         mixed = attend(
             table_of,
             remote,

time: 62.5 us -> 60.7 us (0.971)
  waiting for transfers between devices: 23.4 us -> 21.6 us
    ppermute x14, waiting for transfers between devices: 15 us -> 13.2 us  [advance(): self.front[way] = lax.ppermute(value, 'seq', pairs)]
  transfers between devices with their start and end apart: 22 -> 22, of which waited for: 11 -> 11; matrix products, arithmetic and copies ran while one was open for 3% -> 3% of each run, Pallas kernels for 19% -> 23%
where the time goes in v7:
time: 60.7 us; the launch traced here: 60.5 us
  starting transfers between devices  21.6 us (36%)
  waiting for transfers between devices  21.6 us (36%)
  Pallas kernels  15.4 us (25%)
  other arithmetic  1.16 us (2%)
  local copies, waits for them, and re-layouts  0.61 us (1%)
    ppermute x14, starting transfers between devices, advance(): self.front[way] = lax.ppermute(value, 'seq', pairs)  15.7 us
    ppermute x14, waiting for transfers between devices, advance(): self.front[way] = lax.ppermute(value, 'seq', pairs)  13.2 us
    ppermute x8, waiting for transfers between devices, swap(): lax.ppermute(value, axis, [(source, source ^ mask) for source in range(co...  8.41 us
    pallas_call x4, Pallas kernels, project_call(): pl.pallas_call(kernel, in_specs=kinds, out_specs=[VMEM] * len(shapes), ou...  7.98 us
    ppermute x8, starting transfers between devices, swap(): lax.ppermute(value, axis, [(source, source ^ mask) for source in range(co...  5.87 us
    pallas_call x3, Pallas kernels, attend(): pl.pallas_call(kernel, in_specs=[VMEM] * (1 + len(queries) + len(arrays)...  4.61 us
    pallas_call x2, Pallas kernels, deliver(): pl.pallas_call(functools.partial(deliver_kernel, masks), in_specs=[VMEM]...  1.54 us
    pallas_call x1, Pallas kernels, plan(): pl.pallas_call(functools.partial(plan_kernel, ring, lanes, heads, count,...  1.23 us
  transfers between devices with their start and end apart: 22, of which 11 were waited for; matrix products, arithmetic and copies ran while one was open for 3% of the time, Pallas kernels for 23%

profile of v7, /device:TPU:0, one launch (start us, length us, event | category | flops | bytes accessed | tf_op | source)
XLA Modules:
  0.0 60.5 jit_solution(13452724407468657461)
XLA Ops:
  0.5 2.6 %collective-permute-start.1 = (bf16[128,4096]{1,0:T(8,128)(2,1)}, bf16[128,4096]{1,0:T(8,128)(2,1)S(1)}, u32[]{:S(2)}, u32[]{:S(2)}) collective-permute-start(bf16[128,4096]{1,0:T(8,128)(2,1)} %bitcast.8), channel_id=1, source_target_pairs={{0,2},{1,3},{2,0},{3,1},{4,6},{5,7},{6,4},{7,5},{8,10},{9,11},{10,... | collective-permute-start | bytes 3145736 | tf_op jit(solution)/shard_map/ppermute | solution.py:28
  3.1 0.6 slice.3
  3.7 0.6 %add_convert_fusion = f32[128]{0:T(128)S(1)} fusion(s32[]{:T(128)} %bitcast.5), kind=kLoop, calls=%fused_computation.8 | loop fusion | flops 256 | bytes 516 | tf_op jit(solution)/shard_map/convert_element_type | solution.py:41
  4.8 4.6 %project_near.1 = (bf16[256,512]{1,0:T(8,128)(2,1)S(1)}, bf16[256,256]{1,0:T(8,128)(2,1)S(1)}, f32[1,4096]{1,0:T(1,128)S(1)}, bf16[4096,512]{1,0:T(8,128)(2,1)S(...) custom-call(bf16[128,4096]{1,0:T(8,128)(2,1)} %bitcast.9, ...), custom_call_target="tpu_custom_call" | custom-call | flops 1610612736 | bytes 8388608 | tf_op jit(solution)/shard_map/project_near/pallas_call | solution.py:142
  9.4 1.6 %collective-permute-start.2 = (bf16[256,256]{1,0:T(8,128)(2,1)S(1)}, bf16[256,256]{1,0:T(8,128)(2,1)S(1)}, u32[]{:S(2)}, u32[]{:S(2)}) collective-permute-start(bf16[256,256]{1,0:T(8,128)(2,1)S(1)} %get-tuple-element.41.refs_1_), channel_id=1, source_target_pairs={{0,8},{8,16},{16,24},{24,28},{28,20},{20,12},{12,4},{4,0},{1,9},{9... | collective-permute-start | bytes 393224 | tf_op jit(solution)/shard_map/ppermute | solution.py:259
  11.5 1.2 %plan.1.plan_ref = s32[32,512]{1,0:T(8,128)S(1)} custom-call(s32[3]{0:T(128)S(1)} %pad_add_fusion.info_ref, s32[4,4,4]{2,1,0:T(4,128)S(1)} %copy-done, s32[4,4,4]{2,1,0:T(4,128)S(1)} %copy-done.1), custom_call_target="tpu_custom_call" | custom-call | tf_op jit(solution)/shard_map/plan/pallas_call | solution.py:303
  12.8 2.3 %collective-permute-done.2.refs_2_ = bf16[256,256]{1,0:T(8,128)(2,1)S(1)} collective-permute-done((bf16[256,256]{1,0:T(8,128)(2,1)S(1)}, bf16[256,256]{1,0:T(8,128)(2,1)S(1)}, u32[]{:S(2)}, u32[]{:S(2)}) %collective-permute-start.2) | collective-permute-done | bytes 131104 | tf_op jit(solution)/shard_map/ppermute | solution.py:259
  15.1 1.6 %collective-permute-start.3 = (bf16[256,256]{1,0:T(8,128)(2,1)S(1)}, bf16[256,256]{1,0:T(8,128)(2,1)S(1)}, u32[]{:S(2)}, u32[]{:S(2)}) collective-permute-start(bf16[256,256]{1,0:T(8,128)(2,1)S(1)} %collective-permute-done.2.refs_2_), channel_id=1, source_target_pairs={{0,8},{8,16},{16,24},{24,28},{28,20},{20,12},{12,4},{4,0},{1,9},{9... | collective-permute-start | bytes 393224 | tf_op jit(solution)/shard_map/ppermute | solution.py:259
  17.1 2.9 %collective-permute-done.3.refs_4_ = bf16[256,256]{1,0:T(8,128)(2,1)S(1)} collective-permute-done((bf16[256,256]{1,0:T(8,128)(2,1)S(1)}, bf16[256,256]{1,0:T(8,128)(2,1)S(1)}, u32[]{:S(2)}, u32[]{:S(2)}) %collective-permute-start.3) | collective-permute-done | bytes 131104 | tf_op jit(solution)/shard_map/ppermute | solution.py:259
  20.0 1.6 %collective-permute-start.4 = (bf16[256,256]{1,0:T(8,128)(2,1)S(1)}, bf16[256,256]{1,0:T(8,128)(2,1)S(1)}, u32[]{:S(2)}, u32[]{:S(2)}) collective-permute-start(bf16[256,256]{1,0:T(8,128)(2,1)S(1)} %collective-permute-done.3.refs_4_), channel_id=1, source_target_pairs={{0,8},{8,16},{16,24},{24,28},{28,20},{20,12},{12,4},{4,0},{1,9},{9... | collective-permute-start | bytes 393224 | tf_op jit(solution)/shard_map/ppermute | solution.py:259
  22.1 5.0 %collective-permute-done.1.token_ref = bf16[128,4096]{1,0:T(8,128)(2,1)S(1)} collective-permute-done((bf16[128,4096]{1,0:T(8,128)(2,1)}, bf16[128,4096]{1,0:T(8,128)(2,1)S(1)}, u32[]{:S(2)}, u32[]{:S(2)}) %collective-permute-start.1) | collective-permute-done | bytes 1048608 | tf_op jit(solution)/shard_map/ppermute | solution.py:28
  27.1 1.9 %collective-permute-start.13 = (bf16[256,256]{1,0:T(8,128)(2,1)S(1)}, bf16[256,256]{1,0:T(8,128)(2,1)S(1)}, u32[]{:S(2)}, u32[]{:S(2)}) collective-permute-start(bf16[256,256]{1,0:T(8,128)(2,1)S(1)} %collective-permute-done.4.refs_6_), channel_id=1, source_target_pairs={{0,8},{8,16},{16,24},{24,28},{28,20},{20,12},{12,4},{4,0},{1,9},{9... | collective-permute-start | bytes 393224 | tf_op jit(solution)/shard_map/ppermute | solution.py:259
  29.0 1.0 %project_keys_values.2 = (bf16[128,256]{1,0:T(8,128)(2,1)S(1)}, bf16[128,4096]{1,0:T(8,128)(2,1)S(1)}) custom-call(bf16[128,4096]{1,0:T(8,128)(2,1)S(1)} %collective-permute-done.1.token_ref, f32[1,4096]{1,0:T(1,128)S(1)} %get-tuple-element.45.gain_ref, bf16[4096,128]{1,0:T(8,128)(2,1)S(1)} %get-tuple-element.46.wk_ref, ...), custom_call_target="tpu_custom_call" | custom-call | flops 268435456 | bytes 3145728 | tf_op jit(solution)/shard_map/project_keys_values/pallas_call | solution.py:142
  30.0 1.6 %collective-permute-start.12 = (bf16[128,256]{1,0:T(8,128)(2,1)S(1)}, bf16[128,256]{1,0:T(8,128)(2,1)S(1)}, u32[]{:S(2)}, u32[]{:S(2)}) collective-permute-start(bf16[128,256]{1,0:T(8,128)(2,1)S(1)} %get-tuple-element.55), channel_id=1, source_target_pairs={{0,2},{1,3},{2,0},{3,1},{4,6},{5,7},{6,4},{7,5},{8,10},{9,11},{10,... | collective-permute-start | bytes 196616 | tf_op jit(solution)/shard_map/ppermute | solution.py:28
  31.5 1.0 %project_keys_values.3 = (bf16[128,256]{1,0:T(8,128)(2,1)S(1)}, bf16[128,4096]{1,0:T(8,128)(2,1)S(1)}) custom-call(bf16[128,4096]{1,0:T(8,128)(2,1)S(1)} %collective-permute-done.8.token_ref, f32[1,4096]{1,0:T(1,128)S(1)} %get-tuple-element.45.gain_ref, bf16[4096,128]{1,0:T(8,128)(2,1)S(1)} %get-tuple-element.46.wk_ref, ...), custom_call_target="tpu_custom_call" | custom-call | flops 268435456 | bytes 3145728 | tf_op jit(solution)/shard_map/project_keys_values/pallas_call | solution.py:142
  32.6 1.4 %project_queries.1 = (bf16[128,512]{1,0:T(8,128)(2,1)S(1)}, bf16[128,512]{1,0:T(8,128)(2,1)S(1)}) custom-call(bf16[4096,512]{1,0:T(8,128)(2,1)S(1)} %get-tuple-element.40.wq_ref, f32[128,256]{1,0:T(8,128)S(1)} %pad_maximum_fusion.table_ref, bf16[128,4096]{1,0:T(8,128)(2,1)S(1)} %get-tuple-element.48.refs_0_, bf16[128,4096]{1,0:T(8,128)(2,1)S(1)} %get-tuple-element.51.refs_1_), custom_call_target="tpu_custom_call" | custom-call | flops 1073741824 | bytes 6291456 | tf_op jit(solution)/shard_map/project_queries/pallas_call | solution.py:142
  34.3 2.6 %collective-permute-done.9 = bf16[128,256]{1,0:T(8,128)(2,1)S(1)} collective-permute-done((bf16[128,256]{1,0:T(8,128)(2,1)S(1)}, bf16[128,256]{1,0:T(8,128)(2,1)S(1)}, u32[]{:S(2)}, u32[]{:S(2)}) %collective-permute-start.9) | collective-permute-done | bytes 65568 | tf_op jit(solution)/shard_map/ppermute | solution.py:28
  37.0 0.5 collective-permute-start.16
  37.5 1.6 %collective-permute-start.14 = (bf16[256,256]{1,0:T(8,128)(2,1)S(1)}, bf16[256,256]{1,0:T(8,128)(2,1)S(1)}, u32[]{:S(2)}, u32[]{:S(2)}) collective-permute-start(bf16[256,256]{1,0:T(8,128)(2,1)S(1)} %constant_dynamic-update-slice_fusion.refs_2_), channel_id=1, source_target_pairs={{0,8},{8,16},{16,24},{24,28},{28,20},{20,12},{12,4},{4,0},{1,9},{9... | collective-permute-start | bytes 393224 | tf_op jit(solution)/shard_map/ppermute | solution.py:259
  39.0 1.2 %collective-permute-start.10 = (bf16[128,512]{1,0:T(8,128)(2,1)S(1)}, bf16[128,512]{1,0:T(8,128)(2,1)S(1)}, u32[]{:S(2)}, u32[]{:S(2)}) collective-permute-start(bf16[128,512]{1,0:T(8,128)(2,1)S(1)} %get-tuple-element.53), channel_id=1, source_target_pairs={{0,2},{1,3},{2,0},{3,1},{4,6},{5,7},{6,4},{7,5},{8,10},{9,11},{10,... | collective-permute-start | bytes 393224 | tf_op jit(solution)/shard_map/ppermute | solution.py:28
  40.2 2.3 %collective-permute-done.16.refs_4_ = bf16[256,256]{1,0:T(8,128)(2,1)S(1)} collective-permute-done((bf16[256,256]{1,0:T(8,128)(2,1)S(1)}, bf16[256,256]{1,0:T(8,128)(2,1)S(1)}, u32[]{:S(2)}, u32[]{:S(2)}) %collective-permute-start.16) | collective-permute-done | bytes 131104 | tf_op jit(solution)/shard_map/ppermute | solution.py:259
  43.0 1.6 %collective-permute-start.15 = (bf16[256,256]{1,0:T(8,128)(2,1)S(1)}, bf16[256,256]{1,0:T(8,128)(2,1)S(1)}, u32[]{:S(2)}, u32[]{:S(2)}) collective-permute-start(bf16[256,256]{1,0:T(8,128)(2,1)S(1)} %collective-permute-done.14.refs_3_), channel_id=1, source_target_pairs={{0,8},{8,16},{16,24},{24,28},{28,20},{20,12},{12,4},{4,0},{1,9},{9... | collective-permute-start | bytes 393224 | tf_op jit(solution)/shard_map/ppermute | solution.py:259
  44.6 2.0 %attend.3 = (bf16[128,512]{1,0:T(8,128)(2,1)S(1)}, bf16[128,512]{1,0:T(8,128)(2,1)S(1)}) custom-call(s32[32,512]{1,0:T(8,128)S(1)} %plan.1.plan_ref, bf16[256,512]{1,0:T(8,128)(2,1)S(1)} %get-tuple-element.59.refs_0_, bf16[256,256]{1,0:T(8,128)(2,1)S(1)} %get-tuple-element.41.refs_1_, bf16[256,256]{1,0:T(8,128)(2,1)S(1)} %collective-permute-done.2.refs_2_, ...), custom_call_target="tpu_custom_call" | custom-call | flops 536870912 | bytes 1572864 | tf_op jit(solution)/shard_map/attend/pallas_call | solution.py:433
  46.6 0.5 collective-permute-done.10.refs_0_
  47.9 1.6 %collective-permute-start.17 = (bf16[256,256]{1,0:T(8,128)(2,1)S(1)}, bf16[256,256]{1,0:T(8,128)(2,1)S(1)}, u32[]{:S(2)}, u32[]{:S(2)}) collective-permute-start(bf16[256,256]{1,0:T(8,128)(2,1)S(1)} %collective-permute-done.15.refs_5_), channel_id=1, source_target_pairs={{0,8},{8,16},{16,24},{24,28},{28,20},{20,12},{12,4},{4,0},{1,9},{9... | collective-permute-start | bytes 393224 | tf_op jit(solution)/shard_map/ppermute | solution.py:259
  49.5 3.4 %collective-permute-done.20.refs_8_ = bf16[256,256]{1,0:T(8,128)(2,1)S(1)} collective-permute-done((bf16[256,256]{1,0:T(8,128)(2,1)S(1)}, bf16[256,256]{1,0:T(8,128)(2,1)S(1)}, u32[]{:S(2)}, u32[]{:S(2)}) %collective-permute-start.20) | collective-permute-done | bytes 131104 | tf_op jit(solution)/shard_map/ppermute | solution.py:259
  53.1 1.6 %collective-permute-start.18 = (bf16[256,256]{1,0:T(8,128)(2,1)S(1)}, bf16[256,256]{1,0:T(8,128)(2,1)S(1)}, u32[]{:S(2)}, u32[]{:S(2)}) collective-permute-start(bf16[256,256]{1,0:T(8,128)(2,1)S(1)} %collective-permute-done.17.refs_7_), channel_id=1, source_target_pairs={{0,8},{8,16},{16,24},{24,28},{28,20},{20,12},{12,4},{4,0},{1,9},{9... | collective-permute-start | bytes 393224 | tf_op jit(solution)/shard_map/ppermute | solution.py:259
  54.6 1.8 %attend.4 = (f32[1,1,512]{2,1,0:T(1,128)S(1)}, f32[1,1,512]{2,1,0:T(1,128)S(1)}, f32[1,128,512]{2,1,0:T(8,128)S(1)}, f32[1,1,512]{2,1,0:T(1,128)S(1)}, f32[1,1,5...) custom-call(s32[32,512]{1,0:T(8,128)S(1)} %plan.1.plan_ref, bf16[128,512]{1,0:T(8,128)(2,1)S(1)} %collective-permute-done.10.refs_0_, ...), custom_call_target="tpu_custom_call" | custom-call | flops 469762048 | bytes 1441792 | tf_op jit(solution)/shard_map/attend/pallas_call | solution.py:433
  56.5 0.8 %deliver.2.refs_2_ = bf16[1,128,2048]{2,1,0:T(8,128)(2,1)} custom-call(bf16[128,512]{1,0:T(8,128)(2,1)S(1)} %get-tuple-element.71.refs_0_, bf16[128,512]{1,0:T(8,128)(2,1)S(1)} %collective-permute-done.21.refs_1_), custom_call_target="tpu_custom_call" | custom-call | tf_op jit(solution)/shard_map/deliver/pallas_call | solution.py:471
  57.3 1.7 %collective-permute-done.18.refs_2_ = bf16[256,256]{1,0:T(8,128)(2,1)S(1)} collective-permute-done((bf16[256,256]{1,0:T(8,128)(2,1)S(1)}, bf16[256,256]{1,0:T(8,128)(2,1)S(1)}, u32[]{:S(2)}, u32[]{:S(2)}) %collective-permute-start.18) | collective-permute-done | bytes 131104 | tf_op jit(solution)/shard_map/ppermute | solution.py:259
  59.0 0.7 %attend.5 = (bf16[128,512]{1,0:T(8,128)(2,1)S(1)}, bf16[128,512]{1,0:T(8,128)(2,1)S(1)}) custom-call(s32[32,512]{1,0:T(8,128)S(1)} %plan.1.plan_ref, bf16[128,512]{1,0:T(8,128)(2,1)S(1)} %collective-permute-done.10.refs_0_, bf16[128,512]{1,0:T(8,128)(2,1)S(1)} %collective-permute-done.11.refs_1_, bf16[256,256]{1,0:T(8,128)(2,1)S(1)} %collective-permute-done.18.refs_2_, ...), custom_call_target="tpu_custom_call" | custom-call | flops 67108864 | bytes 655360 | tf_op jit(solution)/shard_map/attend/pallas_call | solution.py:433
  59.7 0.8 %deliver.3 = bf16[1,128,2048]{2,1,0:T(8,128)(2,1)} custom-call(bf16[128,512]{1,0:T(8,128)(2,1)S(1)} %get-tuple-element.69.refs_0_, bf16[128,512]{1,0:T(8,128)(2,1)S(1)} %get-tuple-element.70.refs_1_, bf16[1,128,2048]{2,1,0:T(8,128)(2,1)} %deliver.2.refs_2_), custom_call_target="tpu_custom_call", output_to_operand_aliasing={{}: (2, {})} | custom-call | tf_op jit(solution)/shard_map/deliver/pallas_call | solution.py:471
  (34 shorter events, 4.2 us)
Async XLA Ops:
  0.1 4.7 %collective-permute-start = (bf16[128,4096]{1,0:T(8,128)(2,1)}, bf16[128,4096]{1,0:T(8,128)(2,1)S(1)}, u32[]{:S(2)}, u32[]{:S(2)}) collective-permute-start(bf16[128,4096]{1,0:T(8,128)(2,1)} %bitcast.7), channel_id=1, source_target_pairs={{0,1},{1,0},{2,3},{3,2},{4,5},{5,4},{6,7},{7,6},{8,9},{9,8},{10,11... | collective-permute-start | bytes 3145736 | tf_op jit(solution)/shard_map/ppermute | solution.py:28
  0.5 26.5 %collective-permute-start.1 = (bf16[128,4096]{1,0:T(8,128)(2,1)}, bf16[128,4096]{1,0:T(8,128)(2,1)S(1)}, u32[]{:S(2)}, u32[]{:S(2)}) collective-permute-start(bf16[128,4096]{1,0:T(8,128)(2,1)} %bitcast.8), channel_id=1, source_target_pairs={{0,2},{1,3},{2,0},{3,1},{4,6},{5,7},{6,4},{7,5},{8,10},{9,11},{10,... | collective-permute-start | bytes 3145736 | tf_op jit(solution)/shard_map/ppermute | solution.py:28
  4.8 6.7 %copy-start = (s32[4,4,4]{2,1,0:T(4,128)S(1)}, s32[4,4,4]{2,1,0:T(4,128)}, u32[]{:S(2)}) copy-start(s32[4,4,4]{2,1,0:T(4,128)} %vertical_ref.1) | copy-start | bytes 772
  4.8 6.7 %copy-start.1 = (s32[4,4,4]{2,1,0:T(4,128)S(1)}, s32[4,4,4]{2,1,0:T(4,128)}, u32[]{:S(2)}) copy-start(s32[4,4,4]{2,1,0:T(4,128)} %slash_ref.1) | copy-start | bytes 772
  9.4 5.6 %collective-permute-start.2 = (bf16[256,256]{1,0:T(8,128)(2,1)S(1)}, bf16[256,256]{1,0:T(8,128)(2,1)S(1)}, u32[]{:S(2)}, u32[]{:S(2)}) collective-permute-start(bf16[256,256]{1,0:T(8,128)(2,1)S(1)} %get-tuple-element.41.refs_1_), channel_id=1, source_target_pairs={{0,8},{8,16},{16,24},{24,28},{28,20},{20,12},{12,4},{4,0},{1,9},{9... | collective-permute-start | bytes 393224 | tf_op jit(solution)/shard_map/ppermute | solution.py:259
  11.1 5.6 %collective-permute-start.5 = (bf16[256,256]{1,0:T(8,128)(2,1)S(1)}, bf16[256,256]{1,0:T(8,128)(2,1)S(1)}, u32[]{:S(2)}, u32[]{:S(2)}) collective-permute-start(bf16[256,256]{1,0:T(8,128)(2,1)S(1)} %get-tuple-element.41.refs_1_), channel_id=1, source_target_pairs={{0,4},{8,0},{16,8},{24,16},{28,24},{20,28},{12,20},{4,12},{1,5},{9... | collective-permute-start | bytes 393224 | tf_op jit(solution)/shard_map/ppermute | solution.py:259
  15.1 5.0 %collective-permute-start.3 = (bf16[256,256]{1,0:T(8,128)(2,1)S(1)}, bf16[256,256]{1,0:T(8,128)(2,1)S(1)}, u32[]{:S(2)}, u32[]{:S(2)}) collective-permute-start(bf16[256,256]{1,0:T(8,128)(2,1)S(1)} %collective-permute-done.2.refs_2_), channel_id=1, source_target_pairs={{0,8},{8,16},{16,24},{24,28},{28,20},{20,12},{12,4},{4,0},{1,9},{9... | collective-permute-start | bytes 393224 | tf_op jit(solution)/shard_map/ppermute | solution.py:259
  16.6 5.0 %collective-permute-start.6 = (bf16[256,256]{1,0:T(8,128)(2,1)S(1)}, bf16[256,256]{1,0:T(8,128)(2,1)S(1)}, u32[]{:S(2)}, u32[]{:S(2)}) collective-permute-start(bf16[256,256]{1,0:T(8,128)(2,1)S(1)} %collective-permute-done.5.refs_3_), channel_id=1, source_target_pairs={{0,4},{8,0},{16,8},{24,16},{28,24},{20,28},{12,20},{4,12},{1,5},{9... | collective-permute-start | bytes 393224 | tf_op jit(solution)/shard_map/ppermute | solution.py:259
  20.0 7.0 %collective-permute-start.4 = (bf16[256,256]{1,0:T(8,128)(2,1)S(1)}, bf16[256,256]{1,0:T(8,128)(2,1)S(1)}, u32[]{:S(2)}, u32[]{:S(2)}) collective-permute-start(bf16[256,256]{1,0:T(8,128)(2,1)S(1)} %collective-permute-done.3.refs_4_), channel_id=1, source_target_pairs={{0,8},{8,16},{16,24},{24,28},{28,20},{20,12},{12,4},{4,0},{1,9},{9... | collective-permute-start | bytes 393224 | tf_op jit(solution)/shard_map/ppermute | solution.py:259
  21.6 5.5 %collective-permute-start.7 = (bf16[256,256]{1,0:T(8,128)(2,1)S(1)}, bf16[256,256]{1,0:T(8,128)(2,1)S(1)}, u32[]{:S(2)}, u32[]{:S(2)}) collective-permute-start(bf16[256,256]{1,0:T(8,128)(2,1)S(1)} %collective-permute-done.6.refs_5_), channel_id=1, source_target_pairs={{0,4},{8,0},{16,8},{24,16},{28,24},{20,28},{12,20},{4,12},{1,5},{9... | collective-permute-start | bytes 393224 | tf_op jit(solution)/shard_map/ppermute | solution.py:259
  27.1 4.5 %collective-permute-start.8 = (bf16[128,4096]{1,0:T(8,128)(2,1)S(1)}, bf16[128,4096]{1,0:T(8,128)(2,1)S(1)}, u32[]{:S(2)}, u32[]{:S(2)}) collective-permute-start(bf16[128,4096]{1,0:T(8,128)(2,1)S(1)} %collective-permute-done.1.token_ref), channel_id=1, source_target_pairs={{0,1},{1,0},{2,3},{3,2},{4,5},{5,4},{6,7},{7,6},{8,9},{9,8},{10,11... | collective-permute-start | bytes 3145736 | tf_op jit(solution)/shard_map/ppermute | solution.py:28
  27.1 7.2 %collective-permute-start.13 = (bf16[256,256]{1,0:T(8,128)(2,1)S(1)}, bf16[256,256]{1,0:T(8,128)(2,1)S(1)}, u32[]{:S(2)}, u32[]{:S(2)}) collective-permute-start(bf16[256,256]{1,0:T(8,128)(2,1)S(1)} %collective-permute-done.4.refs_6_), channel_id=1, source_target_pairs={{0,8},{8,16},{16,24},{24,28},{28,20},{20,12},{12,4},{4,0},{1,9},{9... | collective-permute-start | bytes 393224 | tf_op jit(solution)/shard_map/ppermute | solution.py:259
  30.0 4.3 %collective-permute-start.12 = (bf16[128,256]{1,0:T(8,128)(2,1)S(1)}, bf16[128,256]{1,0:T(8,128)(2,1)S(1)}, u32[]{:S(2)}, u32[]{:S(2)}) collective-permute-start(bf16[128,256]{1,0:T(8,128)(2,1)S(1)} %get-tuple-element.55), channel_id=1, source_target_pairs={{0,2},{1,3},{2,0},{3,1},{4,6},{5,7},{6,4},{7,5},{8,10},{9,11},{10,... | collective-permute-start | bytes 196616 | tf_op jit(solution)/shard_map/ppermute | solution.py:28
  32.5 4.4 %collective-permute-start.9 = (bf16[128,256]{1,0:T(8,128)(2,1)S(1)}, bf16[128,256]{1,0:T(8,128)(2,1)S(1)}, u32[]{:S(2)}, u32[]{:S(2)}) collective-permute-start(bf16[128,256]{1,0:T(8,128)(2,1)S(1)} %get-tuple-element.50), channel_id=1, source_target_pairs={{0,3},{1,2},{2,1},{3,0},{4,7},{5,6},{6,5},{7,4},{8,11},{9,10},{10,... | collective-permute-start | bytes 196616 | tf_op jit(solution)/shard_map/ppermute | solution.py:28
  37.0 5.6 %collective-permute-start.16 = (bf16[256,256]{1,0:T(8,128)(2,1)S(1)}, bf16[256,256]{1,0:T(8,128)(2,1)S(1)}, u32[]{:S(2)}, u32[]{:S(2)}) collective-permute-start(bf16[256,256]{1,0:T(8,128)(2,1)S(1)} %constant_dynamic-update-slice_fusion.refs_2_), channel_id=1, source_target_pairs={{0,4},{8,0},{16,8},{24,16},{28,24},{20,28},{12,20},{4,12},{1,5},{9... | collective-permute-start | bytes 393224 | tf_op jit(solution)/shard_map/ppermute | solution.py:259
  37.5 5.5 %collective-permute-start.14 = (bf16[256,256]{1,0:T(8,128)(2,1)S(1)}, bf16[256,256]{1,0:T(8,128)(2,1)S(1)}, u32[]{:S(2)}, u32[]{:S(2)}) collective-permute-start(bf16[256,256]{1,0:T(8,128)(2,1)S(1)} %constant_dynamic-update-slice_fusion.refs_2_), channel_id=1, source_target_pairs={{0,8},{8,16},{16,24},{24,28},{28,20},{20,12},{12,4},{4,0},{1,9},{9... | collective-permute-start | bytes 393224 | tf_op jit(solution)/shard_map/ppermute | solution.py:259
  39.0 7.6 %collective-permute-start.11 = (bf16[128,512]{1,0:T(8,128)(2,1)S(1)}, bf16[128,512]{1,0:T(8,128)(2,1)S(1)}, u32[]{:S(2)}, u32[]{:S(2)}) collective-permute-start(bf16[128,512]{1,0:T(8,128)(2,1)S(1)} %get-tuple-element.54), channel_id=1, source_target_pairs={{0,3},{1,2},{2,1},{3,0},{4,7},{5,6},{6,5},{7,4},{8,11},{9,10},{10,... | collective-permute-start | bytes 393224 | tf_op jit(solution)/shard_map/ppermute | solution.py:28
  39.0 8.1 %collective-permute-start.10 = (bf16[128,512]{1,0:T(8,128)(2,1)S(1)}, bf16[128,512]{1,0:T(8,128)(2,1)S(1)}, u32[]{:S(2)}, u32[]{:S(2)}) collective-permute-start(bf16[128,512]{1,0:T(8,128)(2,1)S(1)} %get-tuple-element.53), channel_id=1, source_target_pairs={{0,2},{1,3},{2,0},{3,1},{4,6},{5,7},{6,4},{7,5},{8,10},{9,11},{10,... | collective-permute-start | bytes 393224 | tf_op jit(solution)/shard_map/ppermute | solution.py:28
  42.5 5.0 %collective-permute-start.19 = (bf16[256,256]{1,0:T(8,128)(2,1)S(1)}, bf16[256,256]{1,0:T(8,128)(2,1)S(1)}, u32[]{:S(2)}, u32[]{:S(2)}) collective-permute-start(bf16[256,256]{1,0:T(8,128)(2,1)S(1)} %collective-permute-done.16.refs_4_), channel_id=1, source_target_pairs={{0,4},{8,0},{16,8},{24,16},{28,24},{20,28},{12,20},{4,12},{1,5},{9... | collective-permute-start | bytes 393224 | tf_op jit(solution)/shard_map/ppermute | solution.py:259
  43.0 5.0 %collective-permute-start.15 = (bf16[256,256]{1,0:T(8,128)(2,1)S(1)}, bf16[256,256]{1,0:T(8,128)(2,1)S(1)}, u32[]{:S(2)}, u32[]{:S(2)}) collective-permute-start(bf16[256,256]{1,0:T(8,128)(2,1)S(1)} %collective-permute-done.14.refs_3_), channel_id=1, source_target_pairs={{0,8},{8,16},{16,24},{24,28},{28,20},{20,12},{12,4},{4,0},{1,9},{9... | collective-permute-start | bytes 393224 | tf_op jit(solution)/shard_map/ppermute | solution.py:259
  47.5 5.4 %collective-permute-start.20 = (bf16[256,256]{1,0:T(8,128)(2,1)S(1)}, bf16[256,256]{1,0:T(8,128)(2,1)S(1)}, u32[]{:S(2)}, u32[]{:S(2)}) collective-permute-start(bf16[256,256]{1,0:T(8,128)(2,1)S(1)} %collective-permute-done.19.refs_6_), channel_id=1, source_target_pairs={{0,4},{8,0},{16,8},{24,16},{28,24},{20,28},{12,20},{4,12},{1,5},{9... | collective-permute-start | bytes 393224 | tf_op jit(solution)/shard_map/ppermute | solution.py:259
  47.9 5.1 %collective-permute-start.17 = (bf16[256,256]{1,0:T(8,128)(2,1)S(1)}, bf16[256,256]{1,0:T(8,128)(2,1)S(1)}, u32[]{:S(2)}, u32[]{:S(2)}) collective-permute-start(bf16[256,256]{1,0:T(8,128)(2,1)S(1)} %collective-permute-done.15.refs_5_), channel_id=1, source_target_pairs={{0,8},{8,16},{16,24},{24,28},{28,20},{20,12},{12,4},{4,0},{1,9},{9... | collective-permute-start | bytes 393224 | tf_op jit(solution)/shard_map/ppermute | solution.py:259
  53.1 3.4 %collective-permute-start.21 = (bf16[128,512]{1,0:T(8,128)(2,1)S(1)}, bf16[128,512]{1,0:T(8,128)(2,1)S(1)}, u32[]{:S(2)}, u32[]{:S(2)}) collective-permute-start(bf16[128,512]{1,0:T(8,128)(2,1)S(1)} %get-tuple-element.72), channel_id=1, source_target_pairs={{0,1},{1,0},{2,3},{3,2},{4,5},{5,4},{6,7},{7,6},{8,9},{9,8},{10,11... | collective-permute-start | bytes 393224 | tf_op jit(solution)/shard_map/ppermute | solution.py:28
  53.1 5.9 %collective-permute-start.18 = (bf16[256,256]{1,0:T(8,128)(2,1)S(1)}, bf16[256,256]{1,0:T(8,128)(2,1)S(1)}, u32[]{:S(2)}, u32[]{:S(2)}) collective-permute-start(bf16[256,256]{1,0:T(8,128)(2,1)S(1)} %collective-permute-done.17.refs_7_), channel_id=1, source_target_pairs={{0,8},{8,16},{16,24},{24,28},{28,20},{20,12},{12,4},{4,0},{1,9},{9... | collective-permute-start | bytes 393224 | tf_op jit(solution)/shard_map/ppermute | solution.py:259

commit v8 on v7

--- a/solution.py
+++ b/solution.py
@@ -52,7 +52,7 @@
         ).astype(jnp.bfloat16)
         return carry
 
-    lax.fori_loop(0, token_ref.shape[0] // BAND, norm_band, 0, unroll=4)
+    lax.fori_loop(0, token_ref.shape[0] // BAND, norm_band, 0, unroll=8)
 
 
 def rotate(value, table_ref):
@@ -505,12 +505,12 @@
     near.advance()
 
     across = after(across, *near.latest)
-    near.advance()
     crossed = swap(across, "doc", 1)
     kv_across, across_in = project_keys_values(across, gain_in, wk_in, wv_in, table)
     home_across = swap(kv_across, "doc", 2)
-    kv_crossed, crossed_in = project_keys_values(crossed, gain_in, wk_in, wv_in, table)
+    kv_crossed, crossed_in = project_keys_values(after(crossed, kv_across), gain_in, wk_in, wv_in, table)
     home_crossed = swap(kv_crossed, "doc", 3)
+    near.advance(kv_crossed)
     q_across, q_crossed = project_queries(
         [across_in, after(crossed_in, kv_crossed)], wq_in, table
     )

time: 60.7 us -> 63.1 us (1.040)
  waiting for transfers between devices: 21.6 us -> 24.8 us
    ppermute x8, waiting for transfers between devices: 8.41 us -> 10 us  [swap(): lax.ppermute(value, axis, [(source, source ^ mask) for source in range(co...]
    ppermute x14, waiting for transfers between devices: 13.2 us -> 14.8 us  [advance(): self.front[way] = lax.ppermute(value, 'seq', pairs)]
  transfers between devices with their start and end apart: 22 -> 22, of which waited for: 11 -> 13; matrix products, arithmetic and copies ran while one was open for 3% -> 3% of each run, Pallas kernels for 23% -> 20%
where the time goes in v8:
time: 63.1 us; the launch traced here: 62.9 us
  waiting for transfers between devices  24.8 us (39%)
  starting transfers between devices  21.2 us (34%)
  Pallas kernels  14.9 us (24%)
  other arithmetic  1.16 us (2%)
    ppermute x14, starting transfers between devices, advance(): self.front[way] = lax.ppermute(value, 'seq', pairs)  15.7 us
    ppermute x14, waiting for transfers between devices, advance(): self.front[way] = lax.ppermute(value, 'seq', pairs)  14.8 us
    ppermute x8, waiting for transfers between devices, swap(): lax.ppermute(value, axis, [(source, source ^ mask) for source in range(co...  10 us
    pallas_call x4, Pallas kernels, project_call(): pl.pallas_call(kernel, in_specs=kinds, out_specs=[VMEM] * len(shapes), ou...  7.58 us
    ppermute x8, starting transfers between devices, swap(): lax.ppermute(value, axis, [(source, source ^ mask) for source in range(co...  5.5 us
    pallas_call x3, Pallas kernels, attend(): pl.pallas_call(kernel, in_specs=[VMEM] * (1 + len(queries) + len(arrays)...  4.6 us
    pallas_call x2, Pallas kernels, deliver(): pl.pallas_call(functools.partial(deliver_kernel, masks), in_specs=[VMEM]...  1.54 us
  transfers between devices with their start and end apart: 22, of which 13 were waited for; matrix products, arithmetic and copies ran while one was open for 3% of the time, Pallas kernels for 20%

profile of v8, /device:TPU:0, one launch (start us, length us, event | category | flops | bytes accessed | tf_op | source)
XLA Modules:
  0.0 62.9 jit_solution(16216695049089821274)
XLA Ops:
  0.5 2.6 %collective-permute-start.1 = (bf16[128,4096]{1,0:T(8,128)(2,1)}, bf16[128,4096]{1,0:T(8,128)(2,1)S(1)}, u32[]{:S(2)}, u32[]{:S(2)}) collective-permute-start(bf16[128,4096]{1,0:T(8,128)(2,1)} %bitcast.8), channel_id=1, source_target_pairs={{0,2},{1,3},{2,0},{3,1},{4,6},{5,7},{6,4},{7,5},{8,10},{9,11},{10,... | collective-permute-start | bytes 3145736 | tf_op jit(solution)/shard_map/ppermute | solution.py:28
  3.7 0.6 %add_convert_fusion = f32[128]{0:T(128)S(1)} fusion(s32[]{:T(128)} %bitcast.5), kind=kLoop, calls=%fused_computation.8 | loop fusion | flops 256 | bytes 516 | tf_op jit(solution)/shard_map/convert_element_type | solution.py:41
  4.8 4.6 %project_near.1 = (bf16[256,512]{1,0:T(8,128)(2,1)S(1)}, bf16[256,256]{1,0:T(8,128)(2,1)S(1)}, f32[1,4096]{1,0:T(1,128)S(1)}, bf16[4096,512]{1,0:T(8,128)(2,1)S(...) custom-call(bf16[128,4096]{1,0:T(8,128)(2,1)} %bitcast.9, ...), custom_call_target="tpu_custom_call" | custom-call | flops 1610612736 | bytes 8388608 | tf_op jit(solution)/shard_map/project_near/pallas_call | solution.py:142
  9.4 1.6 %collective-permute-start.5 = (bf16[256,256]{1,0:T(8,128)(2,1)S(1)}, bf16[256,256]{1,0:T(8,128)(2,1)S(1)}, u32[]{:S(2)}, u32[]{:S(2)}) collective-permute-start(bf16[256,256]{1,0:T(8,128)(2,1)S(1)} %get-tuple-element.43.refs_1_), channel_id=1, source_target_pairs={{0,4},{8,0},{16,8},{24,16},{28,24},{20,28},{12,20},{4,12},{1,5},{9... | collective-permute-start | bytes 393224 | tf_op jit(solution)/shard_map/ppermute | solution.py:259
  11.5 1.2 %plan.1.plan_ref = s32[32,512]{1,0:T(8,128)S(1)} custom-call(s32[3]{0:T(128)S(1)} %pad_add_fusion.info_ref, s32[4,4,4]{2,1,0:T(4,128)S(1)} %copy-done, s32[4,4,4]{2,1,0:T(4,128)S(1)} %copy-done.1), custom_call_target="tpu_custom_call" | custom-call | tf_op jit(solution)/shard_map/plan/pallas_call | solution.py:303
  12.8 2.3 %collective-permute-done.5.refs_3_ = bf16[256,256]{1,0:T(8,128)(2,1)S(1)} collective-permute-done((bf16[256,256]{1,0:T(8,128)(2,1)S(1)}, bf16[256,256]{1,0:T(8,128)(2,1)S(1)}, u32[]{:S(2)}, u32[]{:S(2)}) %collective-permute-start.5) | collective-permute-done | bytes 131104 | tf_op jit(solution)/shard_map/ppermute | solution.py:259
  15.1 1.5 %collective-permute-start.6 = (bf16[256,256]{1,0:T(8,128)(2,1)S(1)}, bf16[256,256]{1,0:T(8,128)(2,1)S(1)}, u32[]{:S(2)}, u32[]{:S(2)}) collective-permute-start(bf16[256,256]{1,0:T(8,128)(2,1)S(1)} %collective-permute-done.5.refs_3_), channel_id=1, source_target_pairs={{0,4},{8,0},{16,8},{24,16},{28,24},{20,28},{12,20},{4,12},{1,5},{9... | collective-permute-start | bytes 393224 | tf_op jit(solution)/shard_map/ppermute | solution.py:259
  17.1 2.9 %collective-permute-done.6.refs_5_ = bf16[256,256]{1,0:T(8,128)(2,1)S(1)} collective-permute-done((bf16[256,256]{1,0:T(8,128)(2,1)S(1)}, bf16[256,256]{1,0:T(8,128)(2,1)S(1)}, u32[]{:S(2)}, u32[]{:S(2)}) %collective-permute-start.6) | collective-permute-done | bytes 131104 | tf_op jit(solution)/shard_map/ppermute | solution.py:259
  20.0 1.5 %collective-permute-start.7 = (bf16[256,256]{1,0:T(8,128)(2,1)S(1)}, bf16[256,256]{1,0:T(8,128)(2,1)S(1)}, u32[]{:S(2)}, u32[]{:S(2)}) collective-permute-start(bf16[256,256]{1,0:T(8,128)(2,1)S(1)} %collective-permute-done.6.refs_5_), channel_id=1, source_target_pairs={{0,4},{8,0},{16,8},{24,16},{28,24},{20,28},{12,20},{4,12},{1,5},{9... | collective-permute-start | bytes 393224 | tf_op jit(solution)/shard_map/ppermute | solution.py:259
  22.1 5.0 %collective-permute-done.1.token_ref = bf16[128,4096]{1,0:T(8,128)(2,1)S(1)} collective-permute-done((bf16[128,4096]{1,0:T(8,128)(2,1)}, bf16[128,4096]{1,0:T(8,128)(2,1)S(1)}, u32[]{:S(2)}, u32[]{:S(2)}) %collective-permute-start.1) | collective-permute-done | bytes 1048608 | tf_op jit(solution)/shard_map/ppermute | solution.py:28
  27.1 0.8 %project_keys_values.2 = (bf16[128,256]{1,0:T(8,128)(2,1)S(1)}, bf16[128,4096]{1,0:T(8,128)(2,1)S(1)}) custom-call(bf16[128,4096]{1,0:T(8,128)(2,1)S(1)} %collective-permute-done.1.token_ref, f32[1,4096]{1,0:T(1,128)S(1)} %get-tuple-element.47.gain_ref, bf16[4096,128]{1,0:T(8,128)(2,1)S(1)} %get-tuple-element.48.wk_ref, ...), custom_call_target="tpu_custom_call" | custom-call | flops 268435456 | bytes 3145728 | tf_op jit(solution)/shard_map/project_keys_values/pallas_call | solution.py:142
  27.9 1.8 %collective-permute-done.8.token_ref = bf16[128,4096]{1,0:T(8,128)(2,1)S(1)} collective-permute-done((bf16[128,4096]{1,0:T(8,128)(2,1)S(1)}, bf16[128,4096]{1,0:T(8,128)(2,1)S(1)}, u32[]{:S(2)}, u32[]{:S(2)}) %collective-permute-start.8) | collective-permute-done | bytes 1048608 | tf_op jit(solution)/shard_map/ppermute | solution.py:28
  29.7 0.8 %project_keys_values.3 = (bf16[128,256]{1,0:T(8,128)(2,1)S(1)}, bf16[128,4096]{1,0:T(8,128)(2,1)S(1)}) custom-call(bf16[128,4096]{1,0:T(8,128)(2,1)S(1)} %collective-permute-done.8.token_ref, f32[1,4096]{1,0:T(1,128)S(1)} %get-tuple-element.47.gain_ref, bf16[4096,128]{1,0:T(8,128)(2,1)S(1)} %get-tuple-element.48.wk_ref, ...), custom_call_target="tpu_custom_call" | custom-call | flops 268435456 | bytes 3145728 | tf_op jit(solution)/shard_map/project_keys_values/pallas_call | solution.py:142
  30.5 1.9 %collective-permute-start.13 = (bf16[256,256]{1,0:T(8,128)(2,1)S(1)}, bf16[256,256]{1,0:T(8,128)(2,1)S(1)}, u32[]{:S(2)}, u32[]{:S(2)}) collective-permute-start(bf16[256,256]{1,0:T(8,128)(2,1)S(1)} %collective-permute-done.4.refs_6_), channel_id=1, source_target_pairs={{0,8},{8,16},{16,24},{24,28},{28,20},{20,12},{12,4},{4,0},{1,9},{9... | collective-permute-start | bytes 393224 | tf_op jit(solution)/shard_map/ppermute | solution.py:259
  32.4 1.5 %collective-permute-start.12 = (bf16[128,256]{1,0:T(8,128)(2,1)S(1)}, bf16[128,256]{1,0:T(8,128)(2,1)S(1)}, u32[]{:S(2)}, u32[]{:S(2)}) collective-permute-start(bf16[128,256]{1,0:T(8,128)(2,1)S(1)} %get-tuple-element.51), channel_id=1, source_target_pairs={{0,2},{1,3},{2,0},{3,1},{4,6},{5,7},{6,4},{7,5},{8,10},{9,11},{10,... | collective-permute-start | bytes 196616 | tf_op jit(solution)/shard_map/ppermute | solution.py:28
  33.9 1.4 %project_queries.1 = (bf16[128,512]{1,0:T(8,128)(2,1)S(1)}, bf16[128,512]{1,0:T(8,128)(2,1)S(1)}) custom-call(bf16[4096,512]{1,0:T(8,128)(2,1)S(1)} %get-tuple-element.42.wq_ref, f32[128,256]{1,0:T(8,128)S(1)} %pad_maximum_fusion.table_ref, bf16[128,4096]{1,0:T(8,128)(2,1)S(1)} %get-tuple-element.50.refs_0_, bf16[128,4096]{1,0:T(8,128)(2,1)S(1)} %get-tuple-element.55.refs_1_), custom_call_target="tpu_custom_call" | custom-call | flops 1073741824 | bytes 6291456 | tf_op jit(solution)/shard_map/project_queries/pallas_call | solution.py:142
  35.3 1.4 %collective-permute-done.12 = bf16[128,256]{1,0:T(8,128)(2,1)S(1)} collective-permute-done((bf16[128,256]{1,0:T(8,128)(2,1)S(1)}, bf16[128,256]{1,0:T(8,128)(2,1)S(1)}, u32[]{:S(2)}, u32[]{:S(2)}) %collective-permute-start.12) | collective-permute-done | bytes 65568 | tf_op jit(solution)/shard_map/ppermute | solution.py:28
  36.7 1.4 %collective-permute-done.9 = bf16[128,256]{1,0:T(8,128)(2,1)S(1)} collective-permute-done((bf16[128,256]{1,0:T(8,128)(2,1)S(1)}, bf16[128,256]{1,0:T(8,128)(2,1)S(1)}, u32[]{:S(2)}, u32[]{:S(2)}) %collective-permute-start.9) | collective-permute-done | bytes 65568 | tf_op jit(solution)/shard_map/ppermute | solution.py:28
  38.6 1.6 %collective-permute-start.14 = (bf16[256,256]{1,0:T(8,128)(2,1)S(1)}, bf16[256,256]{1,0:T(8,128)(2,1)S(1)}, u32[]{:S(2)}, u32[]{:S(2)}) collective-permute-start(bf16[256,256]{1,0:T(8,128)(2,1)S(1)} %constant_dynamic-update-slice_fusion.refs_2_), channel_id=1, source_target_pairs={{0,8},{8,16},{16,24},{24,28},{28,20},{20,12},{12,4},{4,0},{1,9},{9... | collective-permute-start | bytes 393224 | tf_op jit(solution)/shard_map/ppermute | solution.py:259
  40.5 0.7 %collective-permute-start.10 = (bf16[128,512]{1,0:T(8,128)(2,1)S(1)}, bf16[128,512]{1,0:T(8,128)(2,1)S(1)}, u32[]{:S(2)}, u32[]{:S(2)}) collective-permute-start(bf16[128,512]{1,0:T(8,128)(2,1)S(1)} %get-tuple-element.57), channel_id=1, source_target_pairs={{0,2},{1,3},{2,0},{3,1},{4,6},{5,7},{6,4},{7,5},{8,10},{9,11},{10,... | collective-permute-start | bytes 393224 | tf_op jit(solution)/shard_map/ppermute | solution.py:28
  41.2 2.3 %collective-permute-done.16.refs_4_ = bf16[256,256]{1,0:T(8,128)(2,1)S(1)} collective-permute-done((bf16[256,256]{1,0:T(8,128)(2,1)S(1)}, bf16[256,256]{1,0:T(8,128)(2,1)S(1)}, u32[]{:S(2)}, u32[]{:S(2)}) %collective-permute-start.16) | collective-permute-done | bytes 131104 | tf_op jit(solution)/shard_map/ppermute | solution.py:259
  43.9 1.6 %collective-permute-start.15 = (bf16[256,256]{1,0:T(8,128)(2,1)S(1)}, bf16[256,256]{1,0:T(8,128)(2,1)S(1)}, u32[]{:S(2)}, u32[]{:S(2)}) collective-permute-start(bf16[256,256]{1,0:T(8,128)(2,1)S(1)} %collective-permute-done.14.refs_3_), channel_id=1, source_target_pairs={{0,8},{8,16},{16,24},{24,28},{28,20},{20,12},{12,4},{4,0},{1,9},{9... | collective-permute-start | bytes 393224 | tf_op jit(solution)/shard_map/ppermute | solution.py:259
  45.5 2.0 %attend.3 = (bf16[128,512]{1,0:T(8,128)(2,1)S(1)}, bf16[128,512]{1,0:T(8,128)(2,1)S(1)}) custom-call(s32[32,512]{1,0:T(8,128)S(1)} %plan.1.plan_ref, bf16[256,512]{1,0:T(8,128)(2,1)S(1)} %get-tuple-element.63.refs_0_, bf16[256,256]{1,0:T(8,128)(2,1)S(1)} %get-tuple-element.43.refs_1_, bf16[256,256]{1,0:T(8,128)(2,1)S(1)} %collective-permute-done.2.refs_2_, ...), custom_call_target="tpu_custom_call" | custom-call | flops 536870912 | bytes 1572864 | tf_op jit(solution)/shard_map/attend/pallas_call | solution.py:433
  48.8 1.6 %collective-permute-start.17 = (bf16[256,256]{1,0:T(8,128)(2,1)S(1)}, bf16[256,256]{1,0:T(8,128)(2,1)S(1)}, u32[]{:S(2)}, u32[]{:S(2)}) collective-permute-start(bf16[256,256]{1,0:T(8,128)(2,1)S(1)} %collective-permute-done.15.refs_5_), channel_id=1, source_target_pairs={{0,8},{8,16},{16,24},{24,28},{28,20},{20,12},{12,4},{4,0},{1,9},{9... | collective-permute-start | bytes 393224 | tf_op jit(solution)/shard_map/ppermute | solution.py:259
  50.9 3.0 %collective-permute-done.17.refs_7_ = bf16[256,256]{1,0:T(8,128)(2,1)S(1)} collective-permute-done((bf16[256,256]{1,0:T(8,128)(2,1)S(1)}, bf16[256,256]{1,0:T(8,128)(2,1)S(1)}, u32[]{:S(2)}, u32[]{:S(2)}) %collective-permute-start.17) | collective-permute-done | bytes 131104 | tf_op jit(solution)/shard_map/ppermute | solution.py:259
  53.9 1.6 %collective-permute-done.20.refs_8_ = bf16[256,256]{1,0:T(8,128)(2,1)S(1)} collective-permute-done((bf16[256,256]{1,0:T(8,128)(2,1)S(1)}, bf16[256,256]{1,0:T(8,128)(2,1)S(1)}, u32[]{:S(2)}, u32[]{:S(2)}) %collective-permute-start.20) | collective-permute-done | bytes 131104 | tf_op jit(solution)/shard_map/ppermute | solution.py:259
  55.5 1.6 %collective-permute-start.18 = (bf16[256,256]{1,0:T(8,128)(2,1)S(1)}, bf16[256,256]{1,0:T(8,128)(2,1)S(1)}, u32[]{:S(2)}, u32[]{:S(2)}) collective-permute-start(bf16[256,256]{1,0:T(8,128)(2,1)S(1)} %collective-permute-done.17.refs_7_), channel_id=1, source_target_pairs={{0,8},{8,16},{16,24},{24,28},{28,20},{20,12},{12,4},{4,0},{1,9},{9... | collective-permute-start | bytes 393224 | tf_op jit(solution)/shard_map/ppermute | solution.py:259
  57.1 1.8 %attend.4 = (f32[1,1,512]{2,1,0:T(1,128)S(1)}, f32[1,1,512]{2,1,0:T(1,128)S(1)}, f32[1,128,512]{2,1,0:T(8,128)S(1)}, f32[1,1,512]{2,1,0:T(1,128)S(1)}, f32[1,1,5...) custom-call(s32[32,512]{1,0:T(8,128)S(1)} %plan.1.plan_ref, bf16[128,512]{1,0:T(8,128)(2,1)S(1)} %collective-permute-done.10.refs_0_, ...), custom_call_target="tpu_custom_call" | custom-call | flops 469762048 | bytes 1441792 | tf_op jit(solution)/shard_map/attend/pallas_call | solution.py:433
  58.9 0.8 %deliver.2.refs_2_ = bf16[1,128,2048]{2,1,0:T(8,128)(2,1)} custom-call(bf16[128,512]{1,0:T(8,128)(2,1)S(1)} %get-tuple-element.75.refs_0_, bf16[128,512]{1,0:T(8,128)(2,1)S(1)} %collective-permute-done.21.refs_1_), custom_call_target="tpu_custom_call" | custom-call | tf_op jit(solution)/shard_map/deliver/pallas_call | solution.py:471
  59.6 1.7 %collective-permute-done.18.refs_2_ = bf16[256,256]{1,0:T(8,128)(2,1)S(1)} collective-permute-done((bf16[256,256]{1,0:T(8,128)(2,1)S(1)}, bf16[256,256]{1,0:T(8,128)(2,1)S(1)}, u32[]{:S(2)}, u32[]{:S(2)}) %collective-permute-start.18) | collective-permute-done | bytes 131104 | tf_op jit(solution)/shard_map/ppermute | solution.py:259
  61.4 0.7 %attend.5 = (bf16[128,512]{1,0:T(8,128)(2,1)S(1)}, bf16[128,512]{1,0:T(8,128)(2,1)S(1)}) custom-call(s32[32,512]{1,0:T(8,128)S(1)} %plan.1.plan_ref, bf16[128,512]{1,0:T(8,128)(2,1)S(1)} %collective-permute-done.10.refs_0_, bf16[128,512]{1,0:T(8,128)(2,1)S(1)} %collective-permute-done.11.refs_1_, bf16[256,256]{1,0:T(8,128)(2,1)S(1)} %collective-permute-done.18.refs_2_, ...), custom_call_target="tpu_custom_call" | custom-call | flops 67108864 | bytes 655360 | tf_op jit(solution)/shard_map/attend/pallas_call | solution.py:433
  62.1 0.8 %deliver.3 = bf16[1,128,2048]{2,1,0:T(8,128)(2,1)} custom-call(bf16[128,512]{1,0:T(8,128)(2,1)S(1)} %get-tuple-element.73.refs_0_, bf16[128,512]{1,0:T(8,128)(2,1)S(1)} %get-tuple-element.74.refs_1_, bf16[1,128,2048]{2,1,0:T(8,128)(2,1)} %deliver.2.refs_2_), custom_call_target="tpu_custom_call", output_to_operand_aliasing={{}: (2, {})} | custom-call | tf_op jit(solution)/shard_map/deliver/pallas_call | solution.py:471
  (34 shorter events, 5.9 us)
Async XLA Ops:
  0.1 4.7 %collective-permute-start = (bf16[128,4096]{1,0:T(8,128)(2,1)}, bf16[128,4096]{1,0:T(8,128)(2,1)S(1)}, u32[]{:S(2)}, u32[]{:S(2)}) collective-permute-start(bf16[128,4096]{1,0:T(8,128)(2,1)} %bitcast.7), channel_id=1, source_target_pairs={{0,1},{1,0},{2,3},{3,2},{4,5},{5,4},{6,7},{7,6},{8,9},{9,8},{10,11... | collective-permute-start | bytes 3145736 | tf_op jit(solution)/shard_map/ppermute | solution.py:28
  0.5 26.5 %collective-permute-start.1 = (bf16[128,4096]{1,0:T(8,128)(2,1)}, bf16[128,4096]{1,0:T(8,128)(2,1)S(1)}, u32[]{:S(2)}, u32[]{:S(2)}) collective-permute-start(bf16[128,4096]{1,0:T(8,128)(2,1)} %bitcast.8), channel_id=1, source_target_pairs={{0,2},{1,3},{2,0},{3,1},{4,6},{5,7},{6,4},{7,5},{8,10},{9,11},{10,... | collective-permute-start | bytes 3145736 | tf_op jit(solution)/shard_map/ppermute | solution.py:28
  4.8 6.7 %copy-start = (s32[4,4,4]{2,1,0:T(4,128)S(1)}, s32[4,4,4]{2,1,0:T(4,128)}, u32[]{:S(2)}) copy-start(s32[4,4,4]{2,1,0:T(4,128)} %vertical_ref.1) | copy-start | bytes 772
  4.8 6.7 %copy-start.1 = (s32[4,4,4]{2,1,0:T(4,128)S(1)}, s32[4,4,4]{2,1,0:T(4,128)}, u32[]{:S(2)}) copy-start(s32[4,4,4]{2,1,0:T(4,128)} %slash_ref.1) | copy-start | bytes 772
  9.4 5.6 %collective-permute-start.5 = (bf16[256,256]{1,0:T(8,128)(2,1)S(1)}, bf16[256,256]{1,0:T(8,128)(2,1)S(1)}, u32[]{:S(2)}, u32[]{:S(2)}) collective-permute-start(bf16[256,256]{1,0:T(8,128)(2,1)S(1)} %get-tuple-element.43.refs_1_), channel_id=1, source_target_pairs={{0,4},{8,0},{16,8},{24,16},{28,24},{20,28},{12,20},{4,12},{1,5},{9... | collective-permute-start | bytes 393224 | tf_op jit(solution)/shard_map/ppermute | solution.py:259
  11.0 5.6 %collective-permute-start.2 = (bf16[256,256]{1,0:T(8,128)(2,1)S(1)}, bf16[256,256]{1,0:T(8,128)(2,1)S(1)}, u32[]{:S(2)}, u32[]{:S(2)}) collective-permute-start(bf16[256,256]{1,0:T(8,128)(2,1)S(1)} %get-tuple-element.43.refs_1_), channel_id=1, source_target_pairs={{0,8},{8,16},{16,24},{24,28},{28,20},{20,12},{12,4},{4,0},{1,9},{9... | collective-permute-start | bytes 393224 | tf_op jit(solution)/shard_map/ppermute | solution.py:259
  15.1 5.0 %collective-permute-start.6 = (bf16[256,256]{1,0:T(8,128)(2,1)S(1)}, bf16[256,256]{1,0:T(8,128)(2,1)S(1)}, u32[]{:S(2)}, u32[]{:S(2)}) collective-permute-start(bf16[256,256]{1,0:T(8,128)(2,1)S(1)} %collective-permute-done.5.refs_3_), channel_id=1, source_target_pairs={{0,4},{8,0},{16,8},{24,16},{28,24},{20,28},{12,20},{4,12},{1,5},{9... | collective-permute-start | bytes 393224 | tf_op jit(solution)/shard_map/ppermute | solution.py:259
  16.6 5.0 %collective-permute-start.3 = (bf16[256,256]{1,0:T(8,128)(2,1)S(1)}, bf16[256,256]{1,0:T(8,128)(2,1)S(1)}, u32[]{:S(2)}, u32[]{:S(2)}) collective-permute-start(bf16[256,256]{1,0:T(8,128)(2,1)S(1)} %collective-permute-done.2.refs_2_), channel_id=1, source_target_pairs={{0,8},{8,16},{16,24},{24,28},{28,20},{20,12},{12,4},{4,0},{1,9},{9... | collective-permute-start | bytes 393224 | tf_op jit(solution)/shard_map/ppermute | solution.py:259
  20.0 7.0 %collective-permute-start.7 = (bf16[256,256]{1,0:T(8,128)(2,1)S(1)}, bf16[256,256]{1,0:T(8,128)(2,1)S(1)}, u32[]{:S(2)}, u32[]{:S(2)}) collective-permute-start(bf16[256,256]{1,0:T(8,128)(2,1)S(1)} %collective-permute-done.6.refs_5_), channel_id=1, source_target_pairs={{0,4},{8,0},{16,8},{24,16},{28,24},{20,28},{12,20},{4,12},{1,5},{9... | collective-permute-start | bytes 393224 | tf_op jit(solution)/shard_map/ppermute | solution.py:259
  21.5 5.5 %collective-permute-start.4 = (bf16[256,256]{1,0:T(8,128)(2,1)S(1)}, bf16[256,256]{1,0:T(8,128)(2,1)S(1)}, u32[]{:S(2)}, u32[]{:S(2)}) collective-permute-start(bf16[256,256]{1,0:T(8,128)(2,1)S(1)} %collective-permute-done.3.refs_4_), channel_id=1, source_target_pairs={{0,8},{8,16},{16,24},{24,28},{28,20},{20,12},{12,4},{4,0},{1,9},{9... | collective-permute-start | bytes 393224 | tf_op jit(solution)/shard_map/ppermute | solution.py:259
  27.1 2.7 %collective-permute-start.8 = (bf16[128,4096]{1,0:T(8,128)(2,1)S(1)}, bf16[128,4096]{1,0:T(8,128)(2,1)S(1)}, u32[]{:S(2)}, u32[]{:S(2)}) collective-permute-start(bf16[128,4096]{1,0:T(8,128)(2,1)S(1)} %collective-permute-done.1.token_ref), channel_id=1, source_target_pairs={{0,1},{1,0},{2,3},{3,2},{4,5},{5,4},{6,7},{7,6},{8,9},{9,8},{10,11... | collective-permute-start | bytes 3145736 | tf_op jit(solution)/shard_map/ppermute | solution.py:28
  30.5 7.6 %collective-permute-start.13 = (bf16[256,256]{1,0:T(8,128)(2,1)S(1)}, bf16[256,256]{1,0:T(8,128)(2,1)S(1)}, u32[]{:S(2)}, u32[]{:S(2)}) collective-permute-start(bf16[256,256]{1,0:T(8,128)(2,1)S(1)} %collective-permute-done.4.refs_6_), channel_id=1, source_target_pairs={{0,8},{8,16},{16,24},{24,28},{28,20},{20,12},{12,4},{4,0},{1,9},{9... | collective-permute-start | bytes 393224 | tf_op jit(solution)/shard_map/ppermute | solution.py:259
  32.4 4.3 %collective-permute-start.12 = (bf16[128,256]{1,0:T(8,128)(2,1)S(1)}, bf16[128,256]{1,0:T(8,128)(2,1)S(1)}, u32[]{:S(2)}, u32[]{:S(2)}) collective-permute-start(bf16[128,256]{1,0:T(8,128)(2,1)S(1)} %get-tuple-element.51), channel_id=1, source_target_pairs={{0,2},{1,3},{2,0},{3,1},{4,6},{5,7},{6,4},{7,5},{8,10},{9,11},{10,... | collective-permute-start | bytes 196616 | tf_op jit(solution)/shard_map/ppermute | solution.py:28
  33.9 4.2 %collective-permute-start.9 = (bf16[128,256]{1,0:T(8,128)(2,1)S(1)}, bf16[128,256]{1,0:T(8,128)(2,1)S(1)}, u32[]{:S(2)}, u32[]{:S(2)}) collective-permute-start(bf16[128,256]{1,0:T(8,128)(2,1)S(1)} %get-tuple-element.54), channel_id=1, source_target_pairs={{0,3},{1,2},{2,1},{3,0},{4,7},{5,6},{6,5},{7,4},{8,11},{9,10},{10,... | collective-permute-start | bytes 196616 | tf_op jit(solution)/shard_map/ppermute | solution.py:28
  38.1 5.4 %collective-permute-start.16 = (bf16[256,256]{1,0:T(8,128)(2,1)S(1)}, bf16[256,256]{1,0:T(8,128)(2,1)S(1)}, u32[]{:S(2)}, u32[]{:S(2)}) collective-permute-start(bf16[256,256]{1,0:T(8,128)(2,1)S(1)} %constant_dynamic-update-slice_fusion.refs_2_), channel_id=1, source_target_pairs={{0,4},{8,0},{16,8},{24,16},{28,24},{20,28},{12,20},{4,12},{1,5},{9... | collective-permute-start | bytes 393224 | tf_op jit(solution)/shard_map/ppermute | solution.py:259
  38.6 5.3 %collective-permute-start.14 = (bf16[256,256]{1,0:T(8,128)(2,1)S(1)}, bf16[256,256]{1,0:T(8,128)(2,1)S(1)}, u32[]{:S(2)}, u32[]{:S(2)}) collective-permute-start(bf16[256,256]{1,0:T(8,128)(2,1)S(1)} %constant_dynamic-update-slice_fusion.refs_2_), channel_id=1, source_target_pairs={{0,8},{8,16},{16,24},{24,28},{28,20},{20,12},{12,4},{4,0},{1,9},{9... | collective-permute-start | bytes 393224 | tf_op jit(solution)/shard_map/ppermute | solution.py:259
  40.2 7.4 %collective-permute-start.11 = (bf16[128,512]{1,0:T(8,128)(2,1)S(1)}, bf16[128,512]{1,0:T(8,128)(2,1)S(1)}, u32[]{:S(2)}, u32[]{:S(2)}) collective-permute-start(bf16[128,512]{1,0:T(8,128)(2,1)S(1)} %get-tuple-element.58), channel_id=1, source_target_pairs={{0,3},{1,2},{2,1},{3,0},{4,7},{5,6},{6,5},{7,4},{8,11},{9,10},{10,... | collective-permute-start | bytes 393224 | tf_op jit(solution)/shard_map/ppermute | solution.py:28
  40.5 7.4 %collective-permute-start.10 = (bf16[128,512]{1,0:T(8,128)(2,1)S(1)}, bf16[128,512]{1,0:T(8,128)(2,1)S(1)}, u32[]{:S(2)}, u32[]{:S(2)}) collective-permute-start(bf16[128,512]{1,0:T(8,128)(2,1)S(1)} %get-tuple-element.57), channel_id=1, source_target_pairs={{0,2},{1,3},{2,0},{3,1},{4,6},{5,7},{6,4},{7,5},{8,10},{9,11},{10,... | collective-permute-start | bytes 393224 | tf_op jit(solution)/shard_map/ppermute | solution.py:28
  43.5 5.0 %collective-permute-start.19 = (bf16[256,256]{1,0:T(8,128)(2,1)S(1)}, bf16[256,256]{1,0:T(8,128)(2,1)S(1)}, u32[]{:S(2)}, u32[]{:S(2)}) collective-permute-start(bf16[256,256]{1,0:T(8,128)(2,1)S(1)} %collective-permute-done.16.refs_4_), channel_id=1, source_target_pairs={{0,4},{8,0},{16,8},{24,16},{28,24},{20,28},{12,20},{4,12},{1,5},{9... | collective-permute-start | bytes 393224 | tf_op jit(solution)/shard_map/ppermute | solution.py:259
  43.9 5.0 %collective-permute-start.15 = (bf16[256,256]{1,0:T(8,128)(2,1)S(1)}, bf16[256,256]{1,0:T(8,128)(2,1)S(1)}, u32[]{:S(2)}, u32[]{:S(2)}) collective-permute-start(bf16[256,256]{1,0:T(8,128)(2,1)S(1)} %collective-permute-done.14.refs_3_), channel_id=1, source_target_pairs={{0,8},{8,16},{16,24},{24,28},{28,20},{20,12},{12,4},{4,0},{1,9},{9... | collective-permute-start | bytes 393224 | tf_op jit(solution)/shard_map/ppermute | solution.py:259
  48.8 5.0 %collective-permute-start.17 = (bf16[256,256]{1,0:T(8,128)(2,1)S(1)}, bf16[256,256]{1,0:T(8,128)(2,1)S(1)}, u32[]{:S(2)}, u32[]{:S(2)}) collective-permute-start(bf16[256,256]{1,0:T(8,128)(2,1)S(1)} %collective-permute-done.15.refs_5_), channel_id=1, source_target_pairs={{0,8},{8,16},{16,24},{24,28},{28,20},{20,12},{12,4},{4,0},{1,9},{9... | collective-permute-start | bytes 393224 | tf_op jit(solution)/shard_map/ppermute | solution.py:259
  50.5 5.0 %collective-permute-start.20 = (bf16[256,256]{1,0:T(8,128)(2,1)S(1)}, bf16[256,256]{1,0:T(8,128)(2,1)S(1)}, u32[]{:S(2)}, u32[]{:S(2)}) collective-permute-start(bf16[256,256]{1,0:T(8,128)(2,1)S(1)} %collective-permute-done.19.refs_6_), channel_id=1, source_target_pairs={{0,4},{8,0},{16,8},{24,16},{28,24},{20,28},{12,20},{4,12},{1,5},{9... | collective-permute-start | bytes 393224 | tf_op jit(solution)/shard_map/ppermute | solution.py:259
  55.5 3.4 %collective-permute-start.21 = (bf16[128,512]{1,0:T(8,128)(2,1)S(1)}, bf16[128,512]{1,0:T(8,128)(2,1)S(1)}, u32[]{:S(2)}, u32[]{:S(2)}) collective-permute-start(bf16[128,512]{1,0:T(8,128)(2,1)S(1)} %get-tuple-element.76), channel_id=1, source_target_pairs={{0,1},{1,0},{2,3},{3,2},{4,5},{5,4},{6,7},{7,6},{8,9},{9,8},{10,11... | collective-permute-start | bytes 393224 | tf_op jit(solution)/shard_map/ppermute | solution.py:28
  55.5 5.9 %collective-permute-start.18 = (bf16[256,256]{1,0:T(8,128)(2,1)S(1)}, bf16[256,256]{1,0:T(8,128)(2,1)S(1)}, u32[]{:S(2)}, u32[]{:S(2)}) collective-permute-start(bf16[256,256]{1,0:T(8,128)(2,1)S(1)} %collective-permute-done.17.refs_7_), channel_id=1, source_target_pairs={{0,8},{8,16},{16,24},{24,28},{28,20},{20,12},{12,4},{4,0},{1,9},{9... | collective-permute-start | bytes 393224 | tf_op jit(solution)/shard_map/ppermute | solution.py:259
